TPU v7x, 128 devices: a whole 4x4x4 slice. The times are simulated.
128 devices in a mesh: grp: 8 (over z, core), dev: 16 (over x, y).
Axes of the slice: x: 4, y: 4, z: 4, core: 2. Of those that a mesh axis runs over, the one named last changes fastest.
Arguments:
- src_leaf: bfloat16 [8192, 64, 32], P(('grp', 'dev')), may hold values from -6 to 6
- adj_leaf: bfloat16 [8192, 64, 32], P(('grp', 'dev')), may hold values from -6 to 6
- up_leaf: bfloat16 [8192, 64, 64], P(('grp', 'dev')), may hold values from -0.5 to 0.5
- up_mid: bfloat16 [1024, 64, 64], P(('grp', 'dev')), may hold values from -0.5 to 0.5
- couple_leaf: bfloat16 [8192, 16, 64, 64], P(('grp', 'dev')), may hold values from -0.1875 to 0.1875
- couple_mid: bfloat16 [1024, 16, 64, 64], P(('grp', 'dev')), may hold values from -0.1875 to 0.1875
- couple_top: bfloat16 [128, 16, 64, 64], P(('grp', 'dev')), may hold values from -0.1875 to 0.1875
- send_slots: int32 [128, 128, 3], P(('grp', 'dev')), may hold values from 0 to 71, as said below
- leaf_list: int32 [8192, 16], P(('grp', 'dev')), may hold values from 0 to 382, as said below
- mid_list: int32 [1024, 16], P(('grp', 'dev')), may hold values from 2 to 383, as said below
- top_list: int32 [128, 16], P(('grp', 'dev')), may hold values from 0 to 127, as said below
Outputs:
- leaf_forward: bfloat16 [8192, 64, 32], P(('grp', 'dev'))
- leaf_adjoint: bfloat16 [8192, 64, 32], P(('grp', 'dev'))
Inputs may be any that keep to these rules, and one draw needn't show every extreme that they name: `send_slots`: slots s < 2 of each sender and receiver name distinct leaves of the sender's pool; the other slots name second-level clusters. `leaf_list`: every entry is p * 3 + s with s < 2; every such slot is named by some leaf of each device. `mid_list`: every entry is p * 3 + s with s >= 2; every such slot is named by some cluster of each device. `top_list`: column 0 names every top-level cluster once.
All inputs are finite; a program needn't handle non-finite values.
Results may differ from a plain program's by a relative error of at most 0.009.
Values may be sent and summed in bfloat16 or wider, within the bound.
No kernel may reach another device: no remote copies, remote signals or barrier semaphores. Data moves between devices by JAX's collectives and lax.ppermute only.
A program may use at most 192 MiB of HBM per device.

v0:
```python
import jax
import jax.numpy as jnp
from jax import lax
from jax.sharding import PartitionSpec as P


def lift_level(transfer, coeffs):
    parents = transfer.shape[0] // 8
    basis_size = transfer.shape[1]
    return jnp.einsum(
        "cirk,cirf->ckf",
        transfer.reshape(parents, 8, basis_size, basis_size),
        coeffs.reshape(parents, 8, basis_size, coeffs.shape[2]),
        preferred_element_type=jnp.float32,
    )


def lower_level(transfer, coeffs):
    parents = coeffs.shape[0]
    basis_size = transfer.shape[1]
    result = jnp.einsum(
        "cirk,ckf->cirf",
        transfer.reshape(parents, 8, basis_size, basis_size),
        coeffs,
        preferred_element_type=jnp.float32,
    )
    return result.reshape(parents * 8, basis_size, coeffs.shape[2])


def couple_forward(blocks, partner_coeffs):
    return jnp.einsum("ikrs,iksf->irf", blocks, partner_coeffs, preferred_element_type=jnp.float32)


def couple_adjoint(blocks, coeffs):
    return jnp.einsum("ikrs,irf->iksf", blocks, coeffs, preferred_element_type=jnp.float32)


def on_device(
    src_leaf,
    adj_leaf,
    up_leaf,
    up_mid,
    couple_leaf,
    couple_mid,
    couple_top,
    send_slots,
    leaf_list,
    mid_list,
    top_list,
):
    leaves, basis_size, forward_cols = src_leaf.shape
    adjoint_cols = adj_leaf.shape[2]
    peer_count = send_slots.shape[1]
    capacity = send_slots.shape[2]
    my_slots = send_slots[0]
    both_leaf = jnp.concatenate([src_leaf, adj_leaf], axis=2)
    both_mid = lift_level(up_leaf, both_leaf).astype(jnp.bfloat16)
    both_top = lift_level(up_mid, both_mid).astype(jnp.bfloat16)
    src_mid = both_mid[:, :, :forward_cols]
    adj_mid = both_mid[:, :, forward_cols:]
    src_top = both_top[:, :, :forward_cols]
    adj_top = both_top[:, :, forward_cols:]
    top_count = src_top.shape[0]
    coeff_pool = jnp.concatenate([src_leaf, src_mid], axis=0)
    pool_size = coeff_pool.shape[0]
    outgoing = coeff_pool[my_slots].reshape(peer_count, capacity * basis_size * forward_cols)
    arrived = lax.all_to_all(outgoing, ("grp", "dev"), split_axis=0, concat_axis=0, tiled=True)
    arrived = arrived.reshape(peer_count * capacity, basis_size, forward_cols)
    contrib_leaf = couple_adjoint(couple_leaf, adj_leaf)
    contrib_mid = couple_adjoint(couple_mid, adj_mid)
    contrib_rows = jnp.concatenate(
        [
            contrib_leaf.reshape(-1, basis_size * adjoint_cols),
            contrib_mid.reshape(-1, basis_size * adjoint_cols),
        ],
        axis=0,
    )
    targets = jnp.concatenate([leaf_list.reshape(-1), mid_list.reshape(-1)], axis=0)
    per_slot = jax.ops.segment_sum(contrib_rows, targets, num_segments=peer_count * capacity)
    per_slot = per_slot.reshape(peer_count, capacity * basis_size * adjoint_cols)
    returned = lax.all_to_all(per_slot, ("grp", "dev"), split_axis=0, concat_axis=0, tiled=True)
    returned = returned.reshape(peer_count * capacity, basis_size * adjoint_cols)
    pool_far = jax.ops.segment_sum(returned, my_slots.reshape(-1), num_segments=pool_size)
    pool_far = pool_far.reshape(pool_size, basis_size, adjoint_cols)
    contrib_top = couple_adjoint(couple_top, adj_top)
    top_term = jax.ops.segment_sum(
        contrib_top.reshape(-1, basis_size * adjoint_cols),
        top_list.reshape(-1),
        num_segments=top_count * peer_count,
    )
    top_term = top_term.reshape(top_count * peer_count, basis_size, adjoint_cols)
    top_far = lax.psum_scatter(top_term, ("grp", "dev"), scatter_dimension=0, tiled=True)
    all_top = lax.all_gather(src_top, ("grp", "dev"), axis=0, tiled=True)
    top_near = couple_forward(couple_top, all_top[top_list])
    leaf_near = couple_forward(couple_leaf, arrived[leaf_list])
    mid_near = couple_forward(couple_mid, arrived[mid_list])
    top_local = jnp.concatenate([top_near, top_far], axis=2).astype(jnp.bfloat16)
    mid_local = (
        jnp.concatenate([mid_near, pool_far[leaves:]], axis=2) + lower_level(up_mid, top_local)
    ).astype(jnp.bfloat16)
    leaf_total = jnp.concatenate([leaf_near, pool_far[:leaves]], axis=2) + lower_level(
        up_leaf, mid_local
    )
    return (
        leaf_total[:, :, :forward_cols].astype(jnp.bfloat16),
        leaf_total[:, :, forward_cols:].astype(jnp.bfloat16),
    )


def solution(mesh):
    placed = (
        P(("grp", "dev"), None, None),
        P(("grp", "dev"), None, None),
        P(("grp", "dev"), None, None),
        P(("grp", "dev"), None, None),
        P(("grp", "dev"), None, None, None),
        P(("grp", "dev"), None, None, None),
        P(("grp", "dev"), None, None, None),
        P(("grp", "dev"), None, None),
        P(("grp", "dev"), None),
        P(("grp", "dev"), None),
        P(("grp", "dev"), None),
    )
    return jax.shard_map(
        on_device,
        mesh=mesh,
        in_specs=placed,
        out_specs=(P(("grp", "dev"), None, None), P(("grp", "dev"), None, None)),
        check_vma=False,
    )
```

profile of v0, /device:TPU:0, one launch (start us, length us, event | category | flops | bytes accessed | tf_op | source)
XLA Modules:
  0.0 765.4 jit_solution(2266704051513987209)
XLA Ops:
  11.0 3.2 gather_fusion
  14.2 6.6 copy.41
  20.8 12.3 %all_to_all.16 = bf16[128,1,6144]{2,1,0:T(2,128)(2,1)} reshape(bf16[384,64,32]{2,1,0:T(8,128)(2,1)} %copy.41) | data formatting | bytes 3145728 | tf_op jit(solution)/shard_map/all_to_all | solution.py:67
  33.6 12.4 %reduce.2 = bf16[128,6144]{1,0:T(8,128)(2,1)} reduce(bf16[128,1,6144]{2,1,0:T(2,128)(2,1)} %all_to_all.16, bf16[]{:T(256)} %broadcast.42), dimensions={1}, to_apply=%all_to_all.16.reduce_sub_computation | reduce | bytes 3145730 | tf_op jit(solution)/shard_map/all_to_all | solution.py:67
  46.1 5.1 reshape.219
  51.2 11.6 %all-to-all-start = ((bf16[128,2,3072]{2,1,0:T(2,128)(2,1)}), bf16[128,2,3072]{2,1,0:T(2,128)(2,1)}, u32[]{:S(2)}, u32[]{:S(2)}) async-start(bf16[128,2,3072]{2,1,0:T(2,128)(2,1)} %reshape.219), calls=%async_computation | async-start | bytes 3145728 | tf_op jit(solution)/shard_map/all_to_all | solution.py:67
  63.7 1.9 scatter_custom_fusion.2
  67.2 2.9 copy.55
  70.1 17.6 %fusion.16 = f32[64,16,64,32]{3,2,1,0:T(8,128)} fusion(bf16[64,16,64,64]{3,2,1,0:T(8,128)(2,1)} %param.15, bf16[64,64,32]{1,2,0:T(8,128)(2,1)} %param.12), kind=kOutput, calls=%fused_computation.34 | convolution fusion | flops 268435456 | bytes 17039360 | tf_op jit(solution)/shard_map/ikrs,irf->iksf/dot_general | solution.py:35
  90.2 3.9 copy.48
  94.1 3.6 reshape.126
  97.8 25.4 %reshape.125 = f32[1024,2048]{1,0:T(8,128)} reshape(f32[64,16,64,32]{3,2,1,0:T(8,128)} %fusion.16) | data formatting | bytes 16777216 | tf_op jit(solution)/shard_map/reshape | solution.py:73
  123.4 35.2 %scatter_custom_fusion = f32[384,2048]{1,0:T(8,128)} fusion(s32[1152]{0:T(1024)S(1)} %pad_add_fusion, f32[128,2048]{1,0:T(8,128)S(1)} %reshape.126, f32[]{:T(128)} %constant.30, f32[1024,2048]{1,0:T(8,128)} %reshape.125, f32[]{:T(128)} %constant.8.clone.1), kind=kCustom, calls=%fused_computation.7 | custom fusion | flops 4718592 | bytes 12582920 | tf_op jit(solution)/shard_map/scatter-add | solution.py:79
  158.7 6.1 all_to_all.14
  165.9 64.1 %all_gather.3 = bf16[128,64,32]{1,2,0:T(8,128)(2,1)S(1)} all-gather(bf16[1,64,32]{1,2,0:T(8,128)(2,1)S(1)} %slice-done), channel_id=1, replica_groups=mesh['grp'=8,'dev'=16] {'grp','dev'}, dimensions={0}, use_global_device_ids=true | all-gather | bytes 528384 | tf_op jit(solution)/shard_map/all_gather | solution.py:93
  230.0 7.8 %all-to-all-start.1 = ((f32[128,1,6144]{2,1,0:T(1,128)}), f32[128,1,6144]{2,1,0:T(1,128)}, u32[]{:S(2)}, u32[]{:S(2)}) async-start(f32[128,1,6144]{2,1,0:T(1,128)} %all_to_all.14), calls=%async_computation.1 | async-start | bytes 6291456 | tf_op jit(solution)/shard_map/all_to_all | solution.py:81
  238.7 10.4 %reshape.220 = bf16[128,1,6144]{2,1,0:T(2,128)(2,1)} reshape(bf16[128,2,3072]{2,1,0:T(2,128)(2,1)} %all-to-all-done) | data formatting | bytes 3145728
  249.1 11.8 %reduce = bf16[128,6144]{1,0:T(8,128)(2,1)} reduce(bf16[128,1,6144]{2,1,0:T(2,128)(2,1)} %reshape.220, bf16[]{:T(256)} %constant.27), dimensions={1}, to_apply=%all_to_all.13.reduce_sub_computation | reduce | bytes 3145730 | tf_op jit(solution)/shard_map/all_to_all | solution.py:67
  260.8 7.4 reshape.122
  268.2 6.7 copy.44
  274.9 5.0 gather_fusion.2
  279.8 11.9 %gather_fusion.1 = bf16[1024,64,32]{1,2,0:T(8,128)(2,1)} fusion(bf16[384,64,32]{1,2,0:T(8,128)(2,1)} %copy.44, s32[1024]{0:T(1024)S(1)} %broadcast_clamp_fusion), kind=kCustom, calls=%fused_computation.1 | custom fusion | bytes 8392704 | tf_op jit(solution)/shard_map/gather | solution.py:95
  291.8 2.4 convolution_bitcast_fusion.5
  294.1 10.6 %convolution_bitcast_fusion.1 = f32[64,64,32]{1,2,0:T(8,128)S(1)} fusion(bf16[64,16,64,32]{2,3,1,0:T(8,128)(2,1)} %bitcast.116, bf16[64,16,64,64]{3,2,1,0:T(8,128)(2,1)} %param.15), kind=kOutput, calls=%fused_computation.15 | convolution fusion | flops 268435456 | bytes 13107200 | tf_op jit(solution)/shard_map/ikrs,iksf->irf/dot_general | solution.py:31
  304.7 411.7 %reduce-scatter.2.cloned.1.call-done = f32[1,64,32]{1,2,0:T(8,128)} async-done(((f32[128,64,32]{1,2,0:T(8,128)}), f32[1,64,32]{1,2,0:T(8,128)}) %reduce-scatter.2.cloned.1.call-update) | async-done | bytes 8208 | tf_op jit(solution)/shard_map/reduce_scatter | solution.py:92
  717.2 11.0 %reduce.1 = f32[128,6144]{1,0:T(8,128)} reduce(f32[128,1,6144]{2,1,0:T(1,128)} %all-to-all-done.1, f32[]{:T(128)} %constant.28), dimensions={1}, to_apply=%all_to_all.15.reduce_sub_computation | reduce | bytes 6291460 | tf_op jit(solution)/shard_map/all_to_all | solution.py:81
  728.2 4.4 reshape.178
  732.6 7.6 scatter_custom_fusion.1
  745.3 2.4 copy.49
  747.7 3.2 copy.50
  750.9 3.8 fusion.15
  754.7 2.4 fusion.4
  (70 shorter events, 18.1 us)
Async XLA Ops:
  7.2 81.3 %copy-start = (bf16[8,16,64,64]{3,2,1,0:T(8,128)(2,1)S(1)}, bf16[8,16,64,64]{3,2,1,0:T(8,128)(2,1)}, u32[]{:S(2)}) copy-start(bf16[8,16,64,64]{3,2,1,0:T(8,128)(2,1)} %param.16) | copy-start | bytes 3145732
  7.2 3.3 copy-start.1
  7.2 3.4 copy-start.10
  46.1 16.8 %copy-start.4 = (bf16[8,64,64]{2,1,0:T(8,128)(2,1)S(1)}, bf16[8,64,64]{2,1,0:T(8,128)(2,1)}, u32[]{:S(2)}) copy-start(bf16[8,64,64]{2,1,0:T(8,128)(2,1)} %param.14) | copy-start | bytes 196612
  46.1 17.0 %copy-start.2 = (bf16[1,16,64,64]{3,2,1,0:T(8,128)(2,1)S(1)}, bf16[1,16,64,64]{3,2,1,0:T(8,128)(2,1)}, u32[]{:S(2)}) copy-start(bf16[1,16,64,64]{3,2,1,0:T(8,128)(2,1)} %param.17) | copy-start | bytes 393220
  51.2 178.8 %all-to-all-start = ((bf16[128,2,3072]{2,1,0:T(2,128)(2,1)}), bf16[128,2,3072]{2,1,0:T(2,128)(2,1)}, u32[]{:S(2)}, u32[]{:S(2)}) async-start(bf16[128,2,3072]{2,1,0:T(2,128)(2,1)} %reshape.219), calls=%async_computation | async-start | bytes 3145728 | tf_op jit(solution)/shard_map/all_to_all | solution.py:67
  62.8 653.7 %reduce-scatter.2.cloned.1.call-start = ((), (), s32[]{:S(2)}) async-start(), calls=%async_computation.3 | async-start | bytes 2113536 | tf_op jit(solution)/shard_map/reduce_scatter | solution.py:92
  63.1 25.4 %copy-start.7 = (bf16[1,64,64]{1,2,0:T(8,128)(2,1)}, bf16[1,64,64]{1,2,0:T(8,128)(2,1)S(1)}, u32[]{:S(2)}) copy-start(bf16[1,64,64]{1,2,0:T(8,128)(2,1)S(1)} %fusion.12) | copy-start | bytes 24580
  70.1 17.6 %copy-start.11 = (s32[1,128,3]{1,0,2:T(1,128)S(1)}, s32[1,128,3]{1,0,2:T(1,128)}, u32[]{:S(2)}) copy-start(s32[1,128,3]{1,0,2:T(1,128)} %param.18) | copy-start | bytes 4612
  97.8 25.4 %copy-start.8 = (s32[64,16]{0,1:T(8,128)S(1)}, s32[64,16]{0,1:T(8,128)}, u32[]{:S(2)}) copy-start(s32[64,16]{0,1:T(8,128)} %param.19) | copy-start | bytes 12292
  97.8 25.6 %copy-start.9 = (s32[8,16]{1,0:T(8,128)S(1)}, s32[8,16]{1,0:T(8,128)}, u32[]{:S(2)}) copy-start(s32[8,16]{1,0:T(8,128)} %param.20) | copy-start | bytes 1540
  158.7 6.2 copy-start.6
  158.7 7.2 copy-start.12
  158.7 7.2 slice-start
  230.0 487.2 %all-to-all-start.1 = ((f32[128,1,6144]{2,1,0:T(1,128)}), f32[128,1,6144]{2,1,0:T(1,128)}, u32[]{:S(2)}, u32[]{:S(2)}) async-start(f32[128,1,6144]{2,1,0:T(1,128)} %all_to_all.14), calls=%async_computation.1 | async-start | bytes 6291456 | tf_op jit(solution)/shard_map/all_to_all | solution.py:81
  745.3 5.6 copy-start.3
  745.3 5.6 copy-start.5
Sparse Core Ops, SparseCore 0:
  70.2 646.1 reduce-scatter.1
where the time goes:
time: 776 us; the launch traced here: 765 us
  waiting for transfers between devices  412 us (53%)
  local copies, waits for them, and re-layouts  132 us (17%)
  other arithmetic  84.8 us (11%)
  blocking collectives  64.1 us (8%)
  matrix products  38.2 us (5%)
  starting transfers between devices  19.5 us (3%)
  between operations  14.8 us (2%)
    reduce_scatter x1, waiting for transfers between devices, on_device(): lax.psum_scatter(top_term, ('grp', 'dev'), scatter_dimension=0, tiled=True)  412 us
    all_gather x1, blocking collectives, on_device(): all_top = lax.all_gather(src_top, ('grp', 'dev'), axis=0, tiled=True)  64.1 us
    scatter-add x1, other arithmetic, on_device(): jax.ops.segment_sum(contrib_rows, targets, num_segments=peer_count * capa...  35.2 us
    reshape x1, local copies, waits for them, and re-layouts, on_device(): contrib_leaf.reshape(-1, basis_size * adjoint_cols)  25.4 us
    all_to_all x2, other arithmetic, on_device(): lax.all_to_all(outgoing, ('grp', 'dev'), split_axis=0, concat_axis=0, til...  24.2 us
    dot_general x3, matrix products, couple_adjoint(): jnp.einsum('ikrs,irf->iksf', blocks, coeffs, preferred_element_type=jnp.f...  19.5 us
    unnamed x30, local copies, waits for them, and re-layouts  16.4 us
  transfers between devices with their start and end apart: 3, of which 1 were waited for; matrix products, arithmetic and copies ran while one was open for 21% of the time, Pallas kernels for 0%

commit v1 on v0

v1 whole, which is shorter than its diff:
```python
import functools

import jax
import jax.numpy as jnp
from jax import lax
from jax.experimental import pallas as pl
from jax.experimental.pallas import tpu as pltpu
from jax.sharding import PartitionSpec as P

BF16 = jnp.bfloat16
F32 = jnp.float32


def mul(x, y):
    return lax.dot_general(x, y, (((1,), (0,)), ((), ())), preferred_element_type=F32)


def mul_t(x, y):
    return lax.dot_general(x, y, (((1,), (1,)), ((), ())), preferred_element_type=F32)


def side(*blocks):
    return jnp.concatenate(blocks, axis=1)


def fold(x):
    half = x.shape[0] // 2
    return side(x[:half], x[half:])


def unfold(x):
    half = x.shape[1] // 2
    return jnp.concatenate([x[:, :half], x[:, half:]], axis=0)


def lift(rows, up, c):
    size, rank = up.shape[1:]
    return mul(side(*[rows[8 * c + i] for i in range(8)]), up[8 * c : 8 * c + 8].reshape(8 * size, rank))


def turn(up, c, eye):
    rank, size = up.shape[1:]
    return mul_t(eye, up[8 * c : 8 * c + 8].reshape(8 * rank, size)).astype(BF16)


def lower(local, down):
    rank = down.shape[0]
    below = mul(local, down)
    return [below[:, i * rank : (i + 1) * rank] for i in range(8)]


def lift_kernel(
    slots_in, src_in, up_leaf_in, up_mid_in, out, slots, src, up_leaf, up_mid, message, mid_src, tile, sems
):
    leaves, nf, rank = src.shape
    mids = up_mid.shape[0]
    parts = 4
    part = out.shape[0] // parts
    fetch_src = pltpu.make_async_copy(src_in, src, sems.at[0])
    fetch_leaf = pltpu.make_async_copy(up_leaf_in, up_leaf, sems.at[1])
    fetch_mid = pltpu.make_async_copy(up_mid_in, up_mid, sems.at[2])
    fetch_slots = pltpu.make_async_copy(slots_in, slots, sems.at[7])
    fetch_slots.start()
    fetch_src.start()
    fetch_leaf.start()
    fetch_mid.start()

    def pack_leaf(p, carry):
        message[p, :nf] = side(src[slots[0, 0, p]], src[slots[1, 0, p]])
        return carry

    fetch_slots.wait()
    fetch_src.wait()
    lax.fori_loop(0, out.shape[0], pack_leaf, 0, unroll=16)
    fetch_leaf.wait()
    for c in range(mids):
        mid_src[c] = lift(src, up_leaf, c).astype(BF16)
    fetch_mid.wait()
    top_src = lift(mid_src, up_mid, 0).astype(BF16)
    for core in range(2):
        top_half = fold(top_src[core * nf // 2 : (core + 1) * nf // 2])
        for c in range(mids):
            tile[core, c] = jnp.concatenate([fold(mid_src[c]), top_half], axis=0)

    sends = []
    for n in range(parts):
        for core in range(2):

            def pack_rest(i, carry):
                p = n * part + core * (part // 2) + i
                message[p, nf:] = tile[core, slots[2, 0, p] - leaves]
                return carry

            lax.fori_loop(0, part // 2, pack_rest, 0, unroll=16)
        place = pl.ds(n * part, part)
        sends.append(pltpu.make_async_copy(message.at[place], out.at[place], sems.at[3 + n]))
        sends[n].start()
    wait_all(sends)


def top_kernel(top_list, adj, up_leaf, up_mid, couple_top, outgoing, mid_adj, own, other, total):
    nf, rank = adj.shape[1:]
    half = nf // 2
    total[...] = jnp.zeros(total.shape, F32)
    for c in range(mid_adj.shape[0]):
        mid_adj[c] = lift(adj, up_leaf, c).astype(BF16)
    top_adj = lift(mid_adj, up_mid, 0).astype(BF16)
    for k in range(0, couple_top.shape[1], 4):
        terms = mul(top_adj, side(*[couple_top[0, k + j] for j in range(4)]))
        for j in range(4):
            term = terms[:, j * rank : (j + 1) * rank]
            e = top_list[0, k + j]
            sums = [total[core, e] + fold(term[core * half : (core + 1) * half]) for core in range(2)]
            for core in range(2):
                total[core, e] = sums[core]
    core = lax.axis_index("grp") % 2
    own[...] = total[core]
    other[...] = total[1 - core].astype(BF16)


def start_all(copies):
    for copy in copies:
        copy.start()


def wait_all(copies):
    for copy in copies:
        copy.wait()


def adjoint_kernel(
    leaf_list_in,
    mid_list_in,
    adj_in,
    mid_adj_in,
    couple_leaf_in,
    couple_mid_in,
    out,
    leaf_pairs_out,
    mid_pairs_out,
    leaf_list,
    mid_list,
    adj,
    mid_adj,
    couple_leaf,
    couple_mid,
    leaf_pairs,
    mid_pairs,
    message,
    even,
    odd,
    sems,
    leaf_sems,
    pair_sems,
    out_sems,
):
    width, rank = couple_leaf.shape[1:3]
    nf = adj.shape[1]
    half = nf // 2
    steps = leaf_sems.shape[0]
    chunk = adj.shape[0] // steps
    is_low = lax.broadcasted_iota(jnp.int32, (half, 2 * rank), 1) < rank

    def leaves(step):
        return pl.ds(pl.multiple_of(step * chunk, chunk), chunk)

    def fetch(step):
        return pltpu.make_async_copy(
            couple_leaf_in.at[leaves(step)], couple_leaf.at[leaves(step)], leaf_sems.at[step]
        )

    def keep_pairs(step):
        return pltpu.make_async_copy(
            leaf_pairs.at[leaves(step)], leaf_pairs_out.at[leaves(step)], pair_sems.at[step]
        )

    fetches = [
        pltpu.make_async_copy(leaf_list_in, leaf_list, sems.at[0]),
        pltpu.make_async_copy(mid_list_in, mid_list, sems.at[1]),
        pltpu.make_async_copy(adj_in, adj, sems.at[2]),
        pltpu.make_async_copy(mid_adj_in, mid_adj, sems.at[3]),
    ]
    fetch_mid = pltpu.make_async_copy(couple_mid_in, couple_mid, sems.at[4])
    keep_mid = pltpu.make_async_copy(mid_pairs, mid_pairs_out, sems.at[5])
    start_all(fetches)
    for step in range(steps):
        fetch(step).start()
    fetch_mid.start()

    def clear(e, carry):
        even[e] = jnp.zeros((half, 2 * rank), F32)
        odd[e] = jnp.zeros((half, 2 * rank), F32)
        return carry

    lax.fori_loop(0, even.shape[0], clear, 0, unroll=8)
    wait_all(fetches)

    def scatter(row, blocks, slot, keep):
        for k in range(0, width, 4):
            pairs = [side(blocks(k), blocks(k + 1)), side(blocks(k + 2), blocks(k + 3))]
            terms = mul(row, side(*pairs))
            for j in range(2):
                keep(k // 2 + j, pairs[j])
                pair = terms[:, 2 * j * rank : 2 * (j + 1) * rank]
                crossed = pltpu.roll(pair[half:], rank, 1)
                e, o = slot(k + 2 * j), slot(k + 2 * j + 1)
                even_sum = even[e] + jnp.where(is_low, pair[:half], crossed)
                odd_sum = odd[o] + jnp.where(is_low, crossed, pair[:half])
                even[e] = even_sum
                odd[o] = odd_sum

    def leaf_step(step, carry):
        fetch(step).wait()
        for a in range(chunk):
            g = step * chunk + a

            def keep(k, pair):
                leaf_pairs[g, k] = pair

            scatter(adj[g], lambda k: couple_leaf[g, k], lambda k: leaf_list[k, g], keep)
        keep_pairs(step).start()
        return carry

    lax.fori_loop(0, steps, leaf_step, 0)
    fetch_mid.wait()
    for c in range(mid_adj.shape[0]):

        def keep(k, pair):
            mid_pairs[c, k] = pair

        scatter(mid_adj[c], lambda k: couple_mid[c, k], lambda k: mid_list[c, k], keep)
    keep_mid.start()

    def pack(p, carry):
        for s in range(3):
            e = 3 * p + s
            message[p, s * half : (s + 1) * half] = (even[e] + pltpu.roll(odd[e], rank, 1)).astype(BF16)
        return carry

    parts = out_sems.shape[0]
    part = out.shape[0] // parts
    sends = []
    for n in range(parts):
        lax.fori_loop(n * part, (n + 1) * part, pack, 0, unroll=8)
        place = pl.ds(n * part, part)
        sends.append(pltpu.make_async_copy(message.at[place], out.at[place], out_sems.at[n]))
        sends[n].start()
    for step in range(steps):
        keep_pairs(step).wait()
    keep_mid.wait()
    wait_all(sends)


def gather(pairs, partner):
    near = 0
    for k in range(0, 16, 4):
        near += mul_t(side(*[partner(k + j) for j in range(4)]), side(pairs(k // 2), pairs(k // 2 + 1)))
    return near


def forward_kernel(
    leaf_list_in,
    mid_list_in,
    arrived_in,
    leaf_pairs_in,
    mid_pairs_in,
    leaf_near_out,
    mid_near_out,
    leaf_list,
    mid_list,
    arrived,
    leaf_pairs,
    mid_pairs,
    leaf_near,
    mid_near,
    coeff,
    sems,
    arrived_sems,
    leaf_sems,
    near_sems,
):
    leaves, nf, rank = leaf_near.shape
    steps = leaf_sems.shape[0]
    chunk = leaves // steps
    parts = arrived_sems.shape[0]
    part = arrived.shape[0] // parts

    def place(step):
        return pl.ds(pl.multiple_of(step * chunk, chunk), chunk)

    def fetch(step):
        return pltpu.make_async_copy(leaf_pairs_in.at[place(step)], leaf_pairs.at[place(step)], leaf_sems.at[step])

    def keep(step):
        return pltpu.make_async_copy(leaf_near.at[place(step)], leaf_near_out.at[place(step)], near_sems.at[step])

    lists = [
        pltpu.make_async_copy(leaf_list_in, leaf_list, sems.at[0]),
        pltpu.make_async_copy(mid_list_in, mid_list, sems.at[1]),
    ]
    messages = []
    for n in range(parts):
        rows_n = pl.ds(n * part, part)
        messages.append(pltpu.make_async_copy(arrived_in.at[rows_n], arrived.at[rows_n], arrived_sems.at[n]))
    fetch_mid = pltpu.make_async_copy(mid_pairs_in, mid_pairs, sems.at[2])
    keep_mid = pltpu.make_async_copy(mid_near, mid_near_out, sems.at[3])
    start_all(messages)
    start_all(lists)
    for step in range(steps):
        fetch(step).start()
    fetch_mid.start()

    def unpack(p, carry):
        pair = arrived[p, :nf]
        coeff[3 * p] = pair[:, :rank]
        coeff[3 * p + 1] = pair[:, rank:]
        coeff[3 * p + 2] = unfold(arrived[p, nf : nf + nf // 2])
        return carry

    for n in range(parts):
        messages[n].wait()
        lax.fori_loop(n * part, (n + 1) * part, unpack, 0, unroll=8)
    wait_all(lists)

    def leaf_step(step, carry):
        fetch(step).wait()
        for a in range(chunk):
            g = step * chunk + a
            leaf_near[g] = gather(lambda k: leaf_pairs[g, k], lambda k: coeff[leaf_list[k, g]])
        keep(step).start()
        return carry

    lax.fori_loop(0, steps, leaf_step, 0)
    fetch_mid.wait()
    for c in range(mid_near.shape[0]):
        mid_near[c] = gather(lambda k: mid_pairs[c, k], lambda k: coeff[mid_list[c, k]])
    keep_mid.start()
    for step in range(steps):
        keep(step).wait()
    keep_mid.wait()


def finish_kernel(
    top_list, own_half, other_half, leaf_near, mid_near, up_leaf, up_mid, couple_top, forward, down_leaf, down_mid
):
    nf, rank = forward.shape[1:]
    shape = (rank, rank)
    eye = (lax.broadcasted_iota(jnp.int32, shape, 0) == lax.broadcasted_iota(jnp.int32, shape, 1)).astype(BF16)

    def partner(k):
        j = top_list[0, k]
        return jnp.concatenate([unfold(own_half[j]), unfold(other_half[j])], axis=0)

    near = gather(lambda k: side(couple_top[0, 2 * k], couple_top[0, 2 * k + 1]), partner)
    swapped = jnp.concatenate([near[nf // 2 :], near[: nf // 2]], axis=0)
    core = lax.axis_index("grp") % 2
    down_mid[...] = turn(up_mid, 0, eye)
    below_top = lower(jnp.where(core == 0, near, swapped).astype(BF16), down_mid[...])
    for c in range(mid_near.shape[0]):
        down = turn(up_leaf, c, eye)
        down_leaf[c] = down
        below = lower((mid_near[c] + below_top[c]).astype(BF16), down)
        for i in range(8):
            forward[8 * c + i] = (leaf_near[8 * c + i] + below[i]).astype(BF16)


def lower_kernel(
    slots_in,
    returned_in,
    down_leaf_in,
    down_mid_in,
    out,
    slots,
    returned,
    down_leaf,
    down_mid,
    adjoint,
    even,
    odd,
    even_mid,
    odd_mid,
    sems,
):
    leaves, nf, rank = adjoint.shape
    mids = down_leaf.shape[0]
    part = returned.shape[0] // 4
    fetches = []
    for n in range(4):
        place = pl.ds(n * part, part)
        fetches.append(pltpu.make_async_copy(returned_in.at[place], returned.at[place], sems.at[n]))
    fetch_leaf = pltpu.make_async_copy(down_leaf_in, down_leaf, sems.at[4])
    fetch_mid = pltpu.make_async_copy(down_mid_in, down_mid, sems.at[5])
    fetch_slots = pltpu.make_async_copy(slots_in, slots, sems.at[14])
    fetch_slots.start()
    start_all(fetches)
    fetch_mid.start()
    fetch_leaf.start()
    for far in (even, odd, even_mid, odd_mid):
        far[...] = jnp.zeros(far.shape, F32)
    half = nf // 2

    def collect(first, i, top):
        sums = []
        for p, far, far_mid in ((first + 2 * i, even, even_mid), (first + 2 * i + 1, odd, odd_mid)):
            for s, held in ((0, far), (1, far), (2, far_mid)):
                u = slots[s, 0, p] - (leaves if s == 2 else 0)
                sums.append((held, u, held[u] + returned[p, s * half : (s + 1) * half].astype(F32)))
            top += returned[p, 3 * half :].astype(F32)
        for held, u, value in sums:
            held[u] = value
        return top

    fetch_slots.wait()
    tops = [jnp.zeros((half // 2, 2 * rank), F32)] * 2
    for n in range(4):
        fetches[n].wait()
        for core in range(2):
            first = n * part + core * (part // 2)
            tops[core] = lax.fori_loop(0, part // 4, functools.partial(collect, first), tops[core], unroll=True)
    fars = [unfold(even_mid[c] + odd_mid[c]) for c in range(mids)]
    top_far = jnp.concatenate([unfold(tops[0]), unfold(tops[1])], axis=0)
    fetch_mid.wait()
    below_top = lower(top_far.astype(BF16), down_mid[...])
    fetch_leaf.wait()
    sends = []
    for c in range(mids):
        below = lower((fars[c] + below_top[c]).astype(BF16), down_leaf[c])
        for i in range(8):
            a = c * 8 + i
            adjoint[a] = (unfold(even[a] + odd[a]) + below[i]).astype(BF16)
        place = pl.ds(8 * c, 8)
        sends.append(pltpu.make_async_copy(adjoint.at[place], out.at[place], sems.at[6 + c]))
        sends[c].start()
    wait_all(sends)


SMEM = pl.BlockSpec(memory_space=pltpu.SMEM)
VMEM = pl.BlockSpec(memory_space=pltpu.VMEM)
HBM = pl.BlockSpec(memory_space=pl.ANY)


def exchange(x):
    return lax.all_to_all(x, ("grp", "dev"), split_axis=0, concat_axis=0, tiled=True)


def swap(x):
    return lax.ppermute(x, "grp", [(g, g ^ 1) for g in range(lax.axis_size("grp"))])


def on_device(
    src_leaf,
    adj_leaf,
    up_leaf,
    up_mid,
    couple_leaf,
    couple_mid,
    couple_top,
    send_slots,
    leaf_list,
    mid_list,
    top_list,
):
    leaves, rank, nf = src_leaf.shape
    mids = up_mid.shape[0]
    peers = send_slots.shape[1]
    width = couple_leaf.shape[1]
    steps = mids
    src = jnp.swapaxes(src_leaf, 1, 2)
    adj = jnp.swapaxes(adj_leaf, 1, 2)
    slots = jnp.transpose(send_slots, (2, 0, 1))
    leaf_slots = leaf_list.T
    message = (peers, 7 * nf // 4, 2 * rank)
    half_top = (peers, nf // 4, 2 * rank)
    shape = jax.ShapeDtypeStruct
    params = pltpu.CompilerParams(vmem_limit_bytes=66000000)
    small = pl.CostEstimate(flops=10**6, bytes_accessed=10**5, transcendentals=0)

    outgoing = pl.pallas_call(
        lift_kernel,
        out_shape=shape(message, BF16),
        in_specs=[HBM] * 4,
        out_specs=HBM,
        scratch_shapes=[
            pltpu.SMEM(slots.shape, jnp.int32),
            pltpu.VMEM((leaves, nf, rank), BF16),
            pltpu.VMEM((leaves, rank, rank), BF16),
            pltpu.VMEM((mids, rank, rank), BF16),
            pltpu.VMEM(message, BF16),
            pltpu.VMEM((mids, nf, rank), BF16),
            pltpu.VMEM((2, mids, 3 * nf // 4, 2 * rank), BF16),
            pltpu.SemaphoreType.DMA((8,)),
        ],
        compiler_params=params,
        name="lift",
    )(slots, src, up_leaf, up_mid)
    arrived = exchange(outgoing)

    leaf_pairs_shape = (leaves, width // 2, rank, 2 * rank)
    mid_pairs_shape = (mids, width // 2, rank, 2 * rank)
    mid_adj, own_terms, other_terms = pl.pallas_call(
        top_kernel,
        out_shape=(shape((mids, nf, rank), BF16), shape(half_top, F32), shape(half_top, BF16)),
        in_specs=[SMEM] + [VMEM] * 4 + [HBM],
        out_specs=(VMEM, VMEM, VMEM),
        scratch_shapes=[pltpu.VMEM((2,) + half_top, F32)],
        compiler_params=params,
        cost_estimate=small,
        name="top",
    )(top_list, adj, up_leaf, up_mid, couple_top, outgoing)
    swapped_terms = swap(other_terms)
    per_slot, leaf_pairs, mid_pairs = pl.pallas_call(
        adjoint_kernel,
        out_shape=(shape(message, BF16), shape(leaf_pairs_shape, BF16), shape(mid_pairs_shape, BF16)),
        in_specs=[HBM] * 6,
        out_specs=(HBM, HBM, HBM),
        scratch_shapes=[
            pltpu.SMEM(leaf_slots.shape, jnp.int32),
            pltpu.SMEM(mid_list.shape, jnp.int32),
            pltpu.VMEM(adj.shape, BF16),
            pltpu.VMEM(mid_adj.shape, BF16),
            pltpu.VMEM(couple_leaf.shape, BF16),
            pltpu.VMEM(couple_mid.shape, BF16),
            pltpu.VMEM(leaf_pairs_shape, BF16),
            pltpu.VMEM(mid_pairs_shape, BF16),
            pltpu.VMEM(message, BF16),
            pltpu.VMEM((3 * peers, nf // 2, 2 * rank), F32),
            pltpu.VMEM((3 * peers, nf // 2, 2 * rank), F32),
            pltpu.SemaphoreType.DMA((6,)),
            pltpu.SemaphoreType.DMA((steps,)),
            pltpu.SemaphoreType.DMA((steps,)),
            pltpu.SemaphoreType.DMA((4,)),
        ],
        compiler_params=params,
        cost_estimate=small,
        name="adjoint",
    )(leaf_slots, mid_list, adj, mid_adj, couple_leaf, couple_mid)
    top_terms = (own_terms + swapped_terms.astype(F32)).astype(BF16)
    returned = exchange(lax.dynamic_update_slice(per_slot, top_terms, (0, 3 * nf // 2, 0)))

    own_half = arrived[:, 3 * nf // 2 :]
    other_half = swap(own_half)
    leaf_near, mid_near = pl.pallas_call(
        forward_kernel,
        out_shape=(shape((leaves, nf, rank), F32), shape((mids, nf, rank), F32)),
        in_specs=[HBM] * 5,
        out_specs=(HBM, HBM),
        scratch_shapes=[
            pltpu.SMEM(leaf_slots.shape, jnp.int32),
            pltpu.SMEM(mid_list.shape, jnp.int32),
            pltpu.VMEM(message, BF16),
            pltpu.VMEM(leaf_pairs_shape, BF16),
            pltpu.VMEM(mid_pairs_shape, BF16),
            pltpu.VMEM((leaves, nf, rank), F32),
            pltpu.VMEM((mids, nf, rank), F32),
            pltpu.VMEM((3 * peers, nf, rank), BF16),
            pltpu.SemaphoreType.DMA((4,)),
            pltpu.SemaphoreType.DMA((4,)),
            pltpu.SemaphoreType.DMA((steps,)),
            pltpu.SemaphoreType.DMA((steps,)),
        ],
        compiler_params=params,
        cost_estimate=small,
        name="forward",
    )(leaf_slots, mid_list, arrived, leaf_pairs, mid_pairs)
    forward, down_leaf, down_mid = pl.pallas_call(
        finish_kernel,
        out_shape=(
            shape((leaves, nf, rank), BF16),
            shape((mids, rank, 8 * rank), BF16),
            shape((rank, 8 * rank), BF16),
        ),
        in_specs=[SMEM] + [VMEM] * 7,
        out_specs=(VMEM, VMEM, VMEM),
        compiler_params=params,
        cost_estimate=small,
        name="finish",
    )(top_list, own_half, other_half, leaf_near, mid_near, up_leaf, up_mid, couple_top)

    adjoint = pl.pallas_call(
        lower_kernel,
        out_shape=shape((leaves, nf, rank), BF16),
        in_specs=[HBM] * 4,
        out_specs=HBM,
        scratch_shapes=[
            pltpu.SMEM(slots.shape, jnp.int32),
            pltpu.VMEM(message, BF16),
            pltpu.VMEM((mids, rank, 8 * rank), BF16),
            pltpu.VMEM((rank, 8 * rank), BF16),
            pltpu.VMEM((leaves, nf, rank), BF16),
            pltpu.VMEM((leaves, nf // 2, 2 * rank), F32),
            pltpu.VMEM((leaves, nf // 2, 2 * rank), F32),
            pltpu.VMEM((mids, nf // 2, 2 * rank), F32),
            pltpu.VMEM((mids, nf // 2, 2 * rank), F32),
            pltpu.SemaphoreType.DMA((15,)),
        ],
        compiler_params=params,
        name="lower",
    )(slots, returned, down_leaf, down_mid)
    return jnp.swapaxes(forward, 1, 2), jnp.swapaxes(adjoint, 1, 2)


def solution(mesh):
    placed = (
        P(("grp", "dev"), None, None),
        P(("grp", "dev"), None, None),
        P(("grp", "dev"), None, None),
        P(("grp", "dev"), None, None),
        P(("grp", "dev"), None, None, None),
        P(("grp", "dev"), None, None, None),
        P(("grp", "dev"), None, None, None),
        P(("grp", "dev"), None, None),
        P(("grp", "dev"), None),
        P(("grp", "dev"), None),
        P(("grp", "dev"), None),
    )
    return jax.shard_map(
        on_device,
        mesh=mesh,
        in_specs=placed,
        out_specs=(P(("grp", "dev"), None, None), P(("grp", "dev"), None, None)),
        check_vma=False,
    )
```

time: 776 us -> 78.9 us (0.10); the launches traced: 765 us -> 78.3 us
  waiting for transfers between devices: 412 us -> 20.4 us
  local copies, waits for them, and re-layouts: 132 us -> 1.68 us
  other arithmetic: 84.8 us -> 0.8 us
  blocking collectives: 64.1 us -> 0 us
  matrix products: 38.2 us -> 0 us
  Pallas kernels: 0 us -> 37.3 us
  between operations: 14.8 us -> 0.73 us
    reduce_scatter x1 -> x0, waiting for transfers between devices: 412 us -> none  [on_device(): lax.psum_scatter(top_term, ('grp', 'dev'), scatter_dimension=0, tiled=True)]
    all_gather x1 -> x0, blocking collectives: 64.1 us -> none  [on_device(): all_top = lax.all_gather(src_top, ('grp', 'dev'), axis=0, tiled=True)]
    reshape x9 -> x0, local copies, waits for them, and re-layouts: 50.8 us -> none  [the longest x1 25.4 us: on_device(): contrib_leaf.reshape(-1, basis_size * adjoint_cols)]
    scatter-add x3 -> x0, other arithmetic: 44.7 us -> none  [the longest x1 35.2 us: on_device(): jax.ops.segment_sum(contrib_rows, targets, num_segments=peer_count * capa...]
    dot_general x9 -> x0, matrix products: 38.2 us -> none  [the longest x3 19.5 us: couple_adjoint(): jnp.einsum('ikrs,irf->iksf', blocks, coeffs, preferred_element_type=jnp.f...]
    pallas_call x0 -> x6, Pallas kernels: none -> 37.3 us  [the longest x1 13.5 us: on_device(): pl.pallas_call(adjoint_kernel, out_shape=(shape(message, BF16), shape(lea...]
    all_to_all x3 -> x0, other arithmetic: 35.2 us -> none  [the longest x2 24.2 us: on_device(): lax.all_to_all(outgoing, ('grp', 'dev'), split_axis=0, concat_axis=0, til...]
    gather x5 -> x0, local copies, waits for them, and re-layouts: 27.3 us -> none  [the longest x1 11.9 us: on_device(): leaf_near = couple_forward(couple_leaf, arrived[leaf_list])]
  transfers between devices with their start and end apart: 3 -> 4, of which waited for: 1 -> 2; matrix products, arithmetic and copies ran while one was open for 21% -> 2% of each run, Pallas kernels for 0% -> 39%
where the time goes in v1:
time: 78.9 us; the launch traced here: 78.3 us
  Pallas kernels  37.3 us (47%)
  waiting for transfers between devices  20.4 us (26%)
  starting transfers between devices  17.4 us (22%)
  local copies, waits for them, and re-layouts  1.68 us (2%)
  other arithmetic  0.8 us (1%)
    all_to_all x2, waiting for transfers between devices, exchange(): lax.all_to_all(x, ('grp', 'dev'), split_axis=0, concat_axis=0, tiled=True)  20.4 us
    all_to_all x2, starting transfers between devices, exchange(): lax.all_to_all(x, ('grp', 'dev'), split_axis=0, concat_axis=0, tiled=True)  17.3 us
    pallas_call x1, Pallas kernels, on_device(): pl.pallas_call(adjoint_kernel, out_shape=(shape(message, BF16), shape(lea...  13.5 us
    pallas_call x1, Pallas kernels, on_device(): pl.pallas_call(forward_kernel, out_shape=(shape((leaves, nf, rank), F32),...  9.07 us
    pallas_call x1, Pallas kernels, on_device(): pl.pallas_call(finish_kernel, out_shape=(shape((leaves, nf, rank), BF16),...  4.62 us
    pallas_call x1, Pallas kernels, on_device(): pl.pallas_call(lift_kernel, out_shape=shape(message, BF16), in_specs=[HBM...  3.87 us
    pallas_call x1, Pallas kernels, on_device(): pl.pallas_call(top_kernel, out_shape=(shape((mids, nf, rank), BF16), shap...  3.15 us
    pallas_call x1, Pallas kernels, on_device(): pl.pallas_call(lower_kernel, out_shape=shape((leaves, nf, rank), BF16), i...  2.99 us
  transfers between devices with their start and end apart: 4, of which 2 were waited for; matrix products, arithmetic and copies ran while one was open for 2% of the time, Pallas kernels for 39%

profile of v1, /device:TPU:0, one launch (start us, length us, event | category | flops | bytes accessed | tf_op | source)
XLA Modules:
  0.0 78.3 jit_solution(13934989915976681014)
XLA Ops:
  0.6 3.9 %lift.1.outgoing = bf16[128,56,128]{2,1,0:T(8,128)(2,1)} custom-call(s32[3,1,128]{2,1,0:T(1,128)} %bitcast.12, bf16[64,32,64]{2,1,0:T(8,128)(2,1)} %bitcast.8, bf16[64,64,64]{2,1,0:T(8,128)(2,1)} %up_leaf.3, bf16[8,64,64]{2,1,0:T(8,128)(2,1)} %up_mid.3), custom_call_target="tpu_custom_call" | custom-call | tf_op jit(solution)/shard_map/lift/pallas_call | solution.py:478
  4.5 11.6 %all-to-all-start = ((bf16[128,56,128]{2,1,0:T(8,128)(2,1)}), bf16[128,56,128]{2,1,0:T(8,128)(2,1)}, u32[]{:S(2)}, u32[]{:S(2)}) async-start(bf16[128,56,128]{2,1,0:T(8,128)(2,1)} %lift.1.outgoing), calls=%async_computation | async-start | bytes 3670016 | tf_op jit(solution)/shard_map/all_to_all | solution.py:443
  16.1 3.2 %top.1 = (bf16[8,32,64]{2,1,0:T(8,128)(2,1)}, f32[128,8,128]{2,1,0:T(8,128)}, bf16[128,8,128]{2,1,0:T(8,128)(2,1)}) custom-call(s32[1,16]{1,0:T(1,128)} %top_list.3, bf16[64,32,64]{2,1,0:T(8,128)(2,1)} %bitcast.6, bf16[64,64,64]{2,1,0:T(8,128)(2,1)} %up_leaf.3, bf16[8,64,64]{2,1,0:T(8,128)(2,1)} %up_mid.3, bf16[1,16,64,64]{3,2,1,0:T(8,128)(2,1)} %couple_top.3, ...), custom_call_target="tpu_custom_call" | custom-call | flops 1000000 | bytes 100000 | tf_op jit(solution)/shard_map/top/pallas_call | solution.py:500
  19.3 0.0 collective-permute-start.1
  19.3 0.0 copy-start.1
  19.3 13.5 %adjoint.1 = (bf16[128,56,128]{2,1,0:T(8,128)(2,1)}, bf16[64,8,64,128]{3,2,1,0:T(8,128)(2,1)}, bf16[8,8,64,128]{3,2,1,0:T(8,128)(2,1)}) custom-call(s32[16,64]{1,0:T(8,128)} %bitcast.10, s32[8,16]{1,0:T(8,128)} %mid_list_in.3, bf16[64,32,64]{2,1,0:T(8,128)(2,1)} %bitcast.7, bf16[8,32,64]{2,1,0:T(8,128)(2,1)} %get-tuple-element.13.mid_adj_in, ...), custom_call_target="tpu_custom_call" | custom-call | flops 1000000 | bytes 100000 | tf_op jit(solution)/shard_map/adjoint/pallas_call | solution.py:511
  32.8 0.0 collective-permute-done.1
  32.9 0.0 copy-done.1
  32.9 0.8 %fusion = bf16[128,56,128]{2,1,0:T(8,128)(2,1)} fusion(bf16[128,56,128]{2,1,0:T(8,128)(2,1)} %get-tuple-element.19, f32[128,8,128]{2,1,0:T(8,128)S(1)} %copy-done.1, bf16[128,8,128]{2,1,0:T(8,128)(2,1)S(1)} %collective-permute-done.1), kind=kLoop, calls=%fused_computation.1 | loop fusion | flops 393216 | bytes 1048576 | tf_op jit(solution)/shard_map/dynamic_update_slice | solution.py:538
  33.7 9.2 %all-to-all-done.arrived_in = bf16[128,56,128]{2,1,0:T(8,128)(2,1)} async-done(((bf16[128,56,128]{2,1,0:T(8,128)(2,1)}), bf16[128,56,128]{2,1,0:T(8,128)(2,1)}, u32[]{:S(2)}, u32[]{:S(2)}) %all-to-all-start) | async-done | bytes 1835040 | tf_op jit(solution)/shard_map/all_to_all | solution.py:443
  42.8 5.7 %all-to-all-start.1 = ((bf16[128,56,128]{2,1,0:T(8,128)(2,1)}), bf16[128,56,128]{2,1,0:T(8,128)(2,1)}, u32[]{:S(2)}, u32[]{:S(2)}) async-start(bf16[128,56,128]{2,1,0:T(8,128)(2,1)} %fusion), calls=%async_computation.1 | async-start | bytes 3670016 | tf_op jit(solution)/shard_map/all_to_all | solution.py:443
  48.6 1.0 %slice.4.own_half = bf16[128,8,128]{2,1,0:T(8,128)(2,1)S(1)} slice(bf16[128,56,128]{2,1,0:T(8,128)(2,1)} %all-to-all-done.arrived_in), slice={[0:128], [48:56], [0:128]} | slice | bytes 524288 | tf_op jit(solution)/shard_map/slice | solution.py:540
  49.5 0.0 copy-start
  49.5 0.1 collective-permute-start
  49.6 9.1 %forward.1 = (f32[64,32,64]{2,1,0:T(8,128)}, f32[8,32,64]{2,1,0:T(8,128)}) custom-call(s32[16,64]{1,0:T(8,128)} %bitcast.11, s32[8,16]{1,0:T(8,128)} %mid_list_in.3, bf16[128,56,128]{2,1,0:T(8,128)(2,1)} %all-to-all-done.arrived_in, bf16[64,8,64,128]{3,2,1,0:T(8,128)(2,1)} %get-tuple-element.14.leaf_pairs_in, ...), custom_call_target="tpu_custom_call" | custom-call | flops 1000000 | bytes 100000 | tf_op jit(solution)/shard_map/forward/pallas_call | solution.py:542
  58.7 0.0 copy-done
  58.7 0.0 collective-permute-done.other_half
  58.7 0.0 copy-start.2
  58.7 0.7 copy-done.2
  59.4 4.6 %finish.1 = (bf16[64,32,64]{2,1,0:T(8,128)(2,1)}, bf16[8,64,512]{2,1,0:T(8,128)(2,1)}, bf16[64,512]{1,0:T(8,128)(2,1)}) custom-call(s32[1,16]{1,0:T(1,128)} %top_list.3, bf16[128,8,128]{2,1,0:T(8,128)(2,1)} %copy-done, bf16[128,8,128]{2,1,0:T(8,128)(2,1)} %copy-done.2, f32[64,32,64]{2,1,0:T(8,128)} %get-tuple-element.16.leaf_near, ...), custom_call_target="tpu_custom_call" | custom-call | flops 1000000 | bytes 100000 | tf_op jit(solution)/shard_map/finish/pallas_call | solution.py:565
  64.1 11.2 %all-to-all-done.1.returned_in = bf16[128,56,128]{2,1,0:T(8,128)(2,1)} async-done(((bf16[128,56,128]{2,1,0:T(8,128)(2,1)}), bf16[128,56,128]{2,1,0:T(8,128)(2,1)}, u32[]{:S(2)}, u32[]{:S(2)}) %all-to-all-start.1) | async-done | bytes 1835040 | tf_op jit(solution)/shard_map/all_to_all | solution.py:443
  75.3 3.0 %lower.1 = bf16[64,32,64]{2,1,0:T(8,128)(2,1)} custom-call(s32[3,1,128]{2,1,0:T(1,128)} %bitcast.13, bf16[128,56,128]{2,1,0:T(8,128)(2,1)} %all-to-all-done.1.returned_in, bf16[8,64,512]{2,1,0:T(8,128)(2,1)} %get-tuple-element.22.down_leaf_in, bf16[64,512]{1,0:T(8,128)(2,1)} %get-tuple-element.23.down_mid_in), custom_call_target="tpu_custom_call" | custom-call | tf_op jit(solution)/shard_map/lower/pallas_call | solution.py:579
Async XLA Ops:
  4.5 38.3 %all-to-all-start = ((bf16[128,56,128]{2,1,0:T(8,128)(2,1)}), bf16[128,56,128]{2,1,0:T(8,128)(2,1)}, u32[]{:S(2)}, u32[]{:S(2)}) async-start(bf16[128,56,128]{2,1,0:T(8,128)(2,1)} %lift.1.outgoing), calls=%async_computation | async-start | bytes 3670016 | tf_op jit(solution)/shard_map/all_to_all | solution.py:443
  19.3 13.6 %collective-permute-start.1 = (bf16[128,8,128]{2,1,0:T(8,128)(2,1)}, bf16[128,8,128]{2,1,0:T(8,128)(2,1)S(1)}, u32[]{:S(2)}, u32[]{:S(2)}) collective-permute-start(bf16[128,8,128]{2,1,0:T(8,128)(2,1)} %get-tuple-element.21), channel_id=1, source_target_pairs={{0,16},{16,0},{32,48},{48,32},{64,80},{80,64},{96,112},{112,96},{1... | collective-permute-start | bytes 786440 | tf_op jit(solution)/shard_map/ppermute | solution.py:447
  19.3 13.6 %copy-start.1 = (f32[128,8,128]{2,1,0:T(8,128)S(1)}, f32[128,8,128]{2,1,0:T(8,128)}, u32[]{:S(2)}) copy-start(f32[128,8,128]{2,1,0:T(8,128)} %get-tuple-element.20) | copy-start | bytes 1572868
  42.8 32.4 %all-to-all-start.1 = ((bf16[128,56,128]{2,1,0:T(8,128)(2,1)}), bf16[128,56,128]{2,1,0:T(8,128)(2,1)}, u32[]{:S(2)}, u32[]{:S(2)}) async-start(bf16[128,56,128]{2,1,0:T(8,128)(2,1)} %fusion), calls=%async_computation.1 | async-start | bytes 3670016 | tf_op jit(solution)/shard_map/all_to_all | solution.py:443
  49.5 9.2 %copy-start = (bf16[128,8,128]{2,1,0:T(8,128)(2,1)}, bf16[128,8,128]{2,1,0:T(8,128)(2,1)S(1)}, u32[]{:S(2)}) copy-start(bf16[128,8,128]{2,1,0:T(8,128)(2,1)S(1)} %slice.4.own_half) | copy-start | bytes 786436
  49.5 9.2 %collective-permute-start = (bf16[128,8,128]{2,1,0:T(8,128)(2,1)S(1)}, bf16[128,8,128]{2,1,0:T(8,128)(2,1)S(1)}, u32[]{:S(2)}, u32[]{:S(2)}) collective-permute-start(bf16[128,8,128]{2,1,0:T(8,128)(2,1)S(1)} %slice.4.own_half), channel_id=1, source_target_pairs={{0,16},{16,0},{32,48},{48,32},{64,80},{80,64},{96,112},{112,96},{1... | collective-permute-start | bytes 786440 | tf_op jit(solution)/shard_map/ppermute | solution.py:447
  58.7 0.7 copy-start.2

commit v2 on v1

--- a/solution.py
+++ b/solution.py
@@ -1,5 +1,3 @@
-import functools
-
 import jax
 import jax.numpy as jnp
 from jax import lax
@@ -98,24 +96,25 @@
     wait_all(sends)
 
 
+def device_of(i, core):
+    return (i >> 4) * 32 + core * 16 + (i & 15)
+
+
 def top_kernel(top_list, adj, up_leaf, up_mid, couple_top, outgoing, mid_adj, own, other, total):
-    nf, rank = adj.shape[1:]
-    half = nf // 2
+    rank = adj.shape[2]
     total[...] = jnp.zeros(total.shape, F32)
     for c in range(mid_adj.shape[0]):
         mid_adj[c] = lift(adj, up_leaf, c).astype(BF16)
     top_adj = lift(mid_adj, up_mid, 0).astype(BF16)
+    core = lax.axis_index("grp") & 1
     for k in range(0, couple_top.shape[1], 4):
         terms = mul(top_adj, side(*[couple_top[0, k + j] for j in range(4)]))
         for j in range(4):
-            term = terms[:, j * rank : (j + 1) * rank]
-            e = top_list[0, k + j]
-            sums = [total[core, e] + fold(term[core * half : (core + 1) * half]) for core in range(2)]
-            for core in range(2):
-                total[core, e] = sums[core]
-    core = lax.axis_index("grp") % 2
-    own[...] = total[core]
-    other[...] = total[1 - core].astype(BF16)
+            p = top_list[0, k + j]
+            place = ((p >> 4) & 1) ^ core
+            total[place, (p >> 5) * 16 + (p & 15)] += fold(terms[:, j * rank : (j + 1) * rank])
+    own[...] = total[0]
+    other[...] = total[1].astype(BF16)
 
 
 def start_all(copies):
@@ -136,22 +135,18 @@
     couple_leaf_in,
     couple_mid_in,
     out,
-    leaf_pairs_out,
-    mid_pairs_out,
+    other,
     leaf_list,
     mid_list,
     adj,
     mid_adj,
     couple_leaf,
     couple_mid,
-    leaf_pairs,
-    mid_pairs,
     message,
     even,
     odd,
     sems,
     leaf_sems,
-    pair_sems,
     out_sems,
 ):
     width, rank = couple_leaf.shape[1:3]
@@ -161,18 +156,9 @@
     chunk = adj.shape[0] // steps
     is_low = lax.broadcasted_iota(jnp.int32, (half, 2 * rank), 1) < rank
 
-    def leaves(step):
-        return pl.ds(pl.multiple_of(step * chunk, chunk), chunk)
-
     def fetch(step):
-        return pltpu.make_async_copy(
-            couple_leaf_in.at[leaves(step)], couple_leaf.at[leaves(step)], leaf_sems.at[step]
-        )
-
-    def keep_pairs(step):
-        return pltpu.make_async_copy(
-            leaf_pairs.at[leaves(step)], leaf_pairs_out.at[leaves(step)], pair_sems.at[step]
-        )
+        place = pl.ds(pl.multiple_of(step * chunk, chunk), chunk)
+        return pltpu.make_async_copy(couple_leaf_in.at[place], couple_leaf.at[place], leaf_sems.at[step])
 
     fetches = [
         pltpu.make_async_copy(leaf_list_in, leaf_list, sems.at[0]),
@@ -181,7 +167,6 @@
         pltpu.make_async_copy(mid_adj_in, mid_adj, sems.at[3]),
     ]
     fetch_mid = pltpu.make_async_copy(couple_mid_in, couple_mid, sems.at[4])
-    keep_mid = pltpu.make_async_copy(mid_pairs, mid_pairs_out, sems.at[5])
     start_all(fetches)
     for step in range(steps):
         fetch(step).start()
@@ -195,12 +180,10 @@
     lax.fori_loop(0, even.shape[0], clear, 0, unroll=8)
     wait_all(fetches)
 
-    def scatter(row, blocks, slot, keep):
+    def scatter(row, blocks, slot):
         for k in range(0, width, 4):
-            pairs = [side(blocks(k), blocks(k + 1)), side(blocks(k + 2), blocks(k + 3))]
-            terms = mul(row, side(*pairs))
+            terms = mul(row, side(*[blocks(k + j) for j in range(4)]))
             for j in range(2):
-                keep(k // 2 + j, pairs[j])
                 pair = terms[:, 2 * j * rank : 2 * (j + 1) * rank]
                 crossed = pltpu.roll(pair[half:], rank, 1)
                 e, o = slot(k + 2 * j), slot(k + 2 * j + 1)
@@ -213,48 +196,42 @@
         fetch(step).wait()
         for a in range(chunk):
             g = step * chunk + a
-
-            def keep(k, pair):
-                leaf_pairs[g, k] = pair
-
-            scatter(adj[g], lambda k: couple_leaf[g, k], lambda k: leaf_list[k, g], keep)
-        keep_pairs(step).start()
+            scatter(adj[g], lambda k: couple_leaf[g, k], lambda k: leaf_list[k, g])
         return carry
 
     lax.fori_loop(0, steps, leaf_step, 0)
     fetch_mid.wait()
     for c in range(mid_adj.shape[0]):
-
-        def keep(k, pair):
-            mid_pairs[c, k] = pair
-
-        scatter(mid_adj[c], lambda k: couple_mid[c, k], lambda k: mid_list[c, k], keep)
-    keep_mid.start()
-
-    def pack(p, carry):
-        for s in range(3):
-            e = 3 * p + s
-            message[p, s * half : (s + 1) * half] = (even[e] + pltpu.roll(odd[e], rank, 1)).astype(BF16)
-        return carry
-
-    parts = out_sems.shape[0]
-    part = out.shape[0] // parts
+        scatter(mid_adj[c], lambda k: couple_mid[c, k], lambda k: mid_list[c, k])
+
+    core = lax.axis_index("grp") & 1
     sends = []
-    for n in range(parts):
-        lax.fori_loop(n * part, (n + 1) * part, pack, 0, unroll=8)
-        place = pl.ds(n * part, part)
-        sends.append(pltpu.make_async_copy(message.at[place], out.at[place], out_sems.at[n]))
-        sends[n].start()
-    for step in range(steps):
-        keep_pairs(step).wait()
-    keep_mid.wait()
+    for place, target in ((1, other), (0, out)):
+
+        def pack(i, carry):
+            p = device_of(i, core ^ place)
+            for s in range(3):
+                e = 3 * p + s
+                block = even[e] + pltpu.roll(odd[e], rank, 1)
+                message[place, i, s * half : (s + 1) * half] = block.astype(BF16)
+            return carry
+
+        part = other.shape[0] // 2
+        for n in range(2):
+            lax.fori_loop(n * part, (n + 1) * part, pack, 0, unroll=8)
+            rows = pl.ds(n * part, part)
+            copy = pltpu.make_async_copy(
+                message.at[place, rows], target.at[rows, pl.ds(0, 3 * half)], out_sems.at[2 * place + n]
+            )
+            copy.start()
+            sends.append(copy)
     wait_all(sends)
 
 
-def gather(pairs, partner):
+def gather(blocks, partner):
     near = 0
     for k in range(0, 16, 4):
-        near += mul_t(side(*[partner(k + j) for j in range(4)]), side(pairs(k // 2), pairs(k // 2 + 1)))
+        near += mul_t(side(*[partner(k + j) for j in range(4)]), side(*[blocks(k + j) for j in range(4)]))
     return near
 
 
@@ -262,15 +239,15 @@
     leaf_list_in,
     mid_list_in,
     arrived_in,
-    leaf_pairs_in,
-    mid_pairs_in,
+    couple_leaf_in,
+    couple_mid_in,
     leaf_near_out,
     mid_near_out,
     leaf_list,
     mid_list,
     arrived,
-    leaf_pairs,
-    mid_pairs,
+    couple_leaf,
+    couple_mid,
     leaf_near,
     mid_near,
     coeff,
@@ -289,7 +266,7 @@
         return pl.ds(pl.multiple_of(step * chunk, chunk), chunk)
 
     def fetch(step):
-        return pltpu.make_async_copy(leaf_pairs_in.at[place(step)], leaf_pairs.at[place(step)], leaf_sems.at[step])
+        return pltpu.make_async_copy(couple_leaf_in.at[place(step)], couple_leaf.at[place(step)], leaf_sems.at[step])
 
     def keep(step):
         return pltpu.make_async_copy(leaf_near.at[place(step)], leaf_near_out.at[place(step)], near_sems.at[step])
@@ -302,7 +279,7 @@
     for n in range(parts):
         rows_n = pl.ds(n * part, part)
         messages.append(pltpu.make_async_copy(arrived_in.at[rows_n], arrived.at[rows_n], arrived_sems.at[n]))
-    fetch_mid = pltpu.make_async_copy(mid_pairs_in, mid_pairs, sems.at[2])
+    fetch_mid = pltpu.make_async_copy(couple_mid_in, couple_mid, sems.at[2])
     keep_mid = pltpu.make_async_copy(mid_near, mid_near_out, sems.at[3])
     start_all(messages)
     start_all(lists)
@@ -326,14 +303,14 @@
         fetch(step).wait()
         for a in range(chunk):
             g = step * chunk + a
-            leaf_near[g] = gather(lambda k: leaf_pairs[g, k], lambda k: coeff[leaf_list[k, g]])
+            leaf_near[g] = gather(lambda k: couple_leaf[g, k], lambda k: coeff[leaf_list[k, g]])
         keep(step).start()
         return carry
 
     lax.fori_loop(0, steps, leaf_step, 0)
     fetch_mid.wait()
     for c in range(mid_near.shape[0]):
-        mid_near[c] = gather(lambda k: mid_pairs[c, k], lambda k: coeff[mid_list[c, k]])
+        mid_near[c] = gather(lambda k: couple_mid[c, k], lambda k: coeff[mid_list[c, k]])
     keep_mid.start()
     for step in range(steps):
         keep(step).wait()
@@ -351,7 +328,7 @@
         j = top_list[0, k]
         return jnp.concatenate([unfold(own_half[j]), unfold(other_half[j])], axis=0)
 
-    near = gather(lambda k: side(couple_top[0, 2 * k], couple_top[0, 2 * k + 1]), partner)
+    near = gather(lambda k: couple_top[0, k], partner)
     swapped = jnp.concatenate([near[nf // 2 :], near[: nf // 2]], axis=0)
     core = lax.axis_index("grp") % 2
     down_mid[...] = turn(up_mid, 0, eye)
@@ -398,29 +375,28 @@
     for far in (even, odd, even_mid, odd_mid):
         far[...] = jnp.zeros(far.shape, F32)
     half = nf // 2
-
-    def collect(first, i, top):
+    core = lax.axis_index("grp") & 1
+
+    def collect(i, top):
         sums = []
-        for p, far, far_mid in ((first + 2 * i, even, even_mid), (first + 2 * i + 1, odd, odd_mid)):
+        for place, far, far_mid in ((0, even, even_mid), (1, odd, odd_mid)):
+            p = device_of(i, core ^ place)
             for s, held in ((0, far), (1, far), (2, far_mid)):
                 u = slots[s, 0, p] - (leaves if s == 2 else 0)
-                sums.append((held, u, held[u] + returned[p, s * half : (s + 1) * half].astype(F32)))
-            top += returned[p, 3 * half :].astype(F32)
+                first = (3 * place + s) * half
+                sums.append((held, u, held[u] + returned[i, first : first + half].astype(F32)))
         for held, u, value in sums:
             held[u] = value
-        return top
+        return top + returned[i, 6 * half :].astype(F32)
 
     fetch_slots.wait()
-    tops = [jnp.zeros((half // 2, 2 * rank), F32)] * 2
+    top = jnp.zeros((half, 2 * rank), F32)
     for n in range(4):
         fetches[n].wait()
-        for core in range(2):
-            first = n * part + core * (part // 2)
-            tops[core] = lax.fori_loop(0, part // 4, functools.partial(collect, first), tops[core], unroll=True)
+        top = lax.fori_loop(n * part, (n + 1) * part, collect, top, unroll=8)
     fars = [unfold(even_mid[c] + odd_mid[c]) for c in range(mids)]
-    top_far = jnp.concatenate([unfold(tops[0]), unfold(tops[1])], axis=0)
     fetch_mid.wait()
-    below_top = lower(top_far.astype(BF16), down_mid[...])
+    below_top = lower(unfold(top).astype(BF16), down_mid[...])
     fetch_leaf.wait()
     sends = []
     for c in range(mids):
@@ -470,7 +446,10 @@
     slots = jnp.transpose(send_slots, (2, 0, 1))
     leaf_slots = leaf_list.T
     message = (peers, 7 * nf // 4, 2 * rank)
-    half_top = (peers, nf // 4, 2 * rank)
+    chips = peers // 2
+    second_message = (chips, 7 * nf // 2, 2 * rank)
+    swapped_message = (chips, 3 * nf // 2, 2 * rank)
+    top_shape = (chips, nf // 2, 2 * rank)
     shape = jax.ShapeDtypeStruct
     params = pltpu.CompilerParams(vmem_limit_bytes=66000000)
     small = pl.CostEstimate(flops=10**6, bytes_accessed=10**5, transcendentals=0)
@@ -495,24 +474,22 @@
     )(slots, src, up_leaf, up_mid)
     arrived = exchange(outgoing)
 
-    leaf_pairs_shape = (leaves, width // 2, rank, 2 * rank)
-    mid_pairs_shape = (mids, width // 2, rank, 2 * rank)
     mid_adj, own_terms, other_terms = pl.pallas_call(
         top_kernel,
-        out_shape=(shape((mids, nf, rank), BF16), shape(half_top, F32), shape(half_top, BF16)),
+        out_shape=(shape((mids, nf, rank), BF16), shape(top_shape, F32), shape(top_shape, BF16)),
         in_specs=[SMEM] + [VMEM] * 4 + [HBM],
         out_specs=(VMEM, VMEM, VMEM),
-        scratch_shapes=[pltpu.VMEM((2,) + half_top, F32)],
+        scratch_shapes=[pltpu.VMEM((2,) + top_shape, F32)],
         compiler_params=params,
         cost_estimate=small,
         name="top",
     )(top_list, adj, up_leaf, up_mid, couple_top, outgoing)
     swapped_terms = swap(other_terms)
-    per_slot, leaf_pairs, mid_pairs = pl.pallas_call(
+    per_slot, for_other = pl.pallas_call(
         adjoint_kernel,
-        out_shape=(shape(message, BF16), shape(leaf_pairs_shape, BF16), shape(mid_pairs_shape, BF16)),
+        out_shape=(shape(second_message, BF16), shape(swapped_message, BF16)),
         in_specs=[HBM] * 6,
-        out_specs=(HBM, HBM, HBM),
+        out_specs=(HBM, HBM),
         scratch_shapes=[
             pltpu.SMEM(leaf_slots.shape, jnp.int32),
             pltpu.SMEM(mid_list.shape, jnp.int32),
@@ -520,13 +497,10 @@
             pltpu.VMEM(mid_adj.shape, BF16),
             pltpu.VMEM(couple_leaf.shape, BF16),
             pltpu.VMEM(couple_mid.shape, BF16),
-            pltpu.VMEM(leaf_pairs_shape, BF16),
-            pltpu.VMEM(mid_pairs_shape, BF16),
-            pltpu.VMEM(message, BF16),
+            pltpu.VMEM((2,) + swapped_message, BF16),
             pltpu.VMEM((3 * peers, nf // 2, 2 * rank), F32),
             pltpu.VMEM((3 * peers, nf // 2, 2 * rank), F32),
-            pltpu.SemaphoreType.DMA((6,)),
-            pltpu.SemaphoreType.DMA((steps,)),
+            pltpu.SemaphoreType.DMA((5,)),
             pltpu.SemaphoreType.DMA((steps,)),
             pltpu.SemaphoreType.DMA((4,)),
         ],
@@ -535,7 +509,12 @@
         name="adjoint",
     )(leaf_slots, mid_list, adj, mid_adj, couple_leaf, couple_mid)
     top_terms = (own_terms + swapped_terms.astype(F32)).astype(BF16)
-    returned = exchange(lax.dynamic_update_slice(per_slot, top_terms, (0, 3 * nf // 2, 0)))
+    per_slot = lax.dynamic_update_slice(per_slot, swap(for_other), (0, 3 * nf // 2, 0))
+    per_slot = lax.dynamic_update_slice(per_slot, top_terms, (0, 3 * nf, 0))
+    same_core = [[device_of(i, core) for i in range(chips)] for core in range(2)]
+    returned = lax.all_to_all(
+        per_slot, ("grp", "dev"), split_axis=0, concat_axis=0, axis_index_groups=same_core, tiled=True
+    )
 
     own_half = arrived[:, 3 * nf // 2 :]
     other_half = swap(own_half)
@@ -548,8 +527,8 @@
             pltpu.SMEM(leaf_slots.shape, jnp.int32),
             pltpu.SMEM(mid_list.shape, jnp.int32),
             pltpu.VMEM(message, BF16),
-            pltpu.VMEM(leaf_pairs_shape, BF16),
-            pltpu.VMEM(mid_pairs_shape, BF16),
+            pltpu.VMEM(couple_leaf.shape, BF16),
+            pltpu.VMEM(couple_mid.shape, BF16),
             pltpu.VMEM((leaves, nf, rank), F32),
             pltpu.VMEM((mids, nf, rank), F32),
             pltpu.VMEM((3 * peers, nf, rank), BF16),
@@ -561,7 +540,7 @@
         compiler_params=params,
         cost_estimate=small,
         name="forward",
-    )(leaf_slots, mid_list, arrived, leaf_pairs, mid_pairs)
+    )(leaf_slots, mid_list, arrived, couple_leaf, couple_mid)
     forward, down_leaf, down_mid = pl.pallas_call(
         finish_kernel,
         out_shape=(
@@ -583,7 +562,7 @@
         out_specs=HBM,
         scratch_shapes=[
             pltpu.SMEM(slots.shape, jnp.int32),
-            pltpu.VMEM(message, BF16),
+            pltpu.VMEM(second_message, BF16),
             pltpu.VMEM((mids, rank, 8 * rank), BF16),
             pltpu.VMEM((rank, 8 * rank), BF16),
             pltpu.VMEM((leaves, nf, rank), BF16),

time: 78.9 us -> 78.5 us (level)
  waiting for transfers between devices: 20.4 us -> 15.3 us
  Pallas kernels: 37.3 us -> 40.8 us
  local copies, waits for them, and re-layouts: 1.68 us -> 2.74 us
    all_to_all x2 -> x1, waiting for transfers between devices: 20.4 us -> 5.51 us  [exchange(): lax.all_to_all(x, ('grp', 'dev'), split_axis=0, concat_axis=0, tiled=True)]
    all_to_all x0 -> x1, waiting for transfers between devices: none -> 7.7 us  [on_device(): lax.all_to_all(per_slot, ('grp', 'dev'), split_axis=0, concat_axis=0, axi...]
    all_to_all x2 -> x1, starting transfers between devices: 17.3 us -> 11.6 us  [exchange(): lax.all_to_all(x, ('grp', 'dev'), split_axis=0, concat_axis=0, tiled=True)]
    all_to_all x0 -> x1, starting transfers between devices: none -> 5.52 us  [on_device(): lax.all_to_all(per_slot, ('grp', 'dev'), split_axis=0, concat_axis=0, axi...]
    pallas_call x1, Pallas kernels: 9.07 us -> 12.4 us  [on_device(): pl.pallas_call(forward_kernel, out_shape=(shape((leaves, nf, rank), F32),...]
    ppermute x2 -> x3, waiting for transfers between devices: 0.01 us -> 2.09 us  [swap(): lax.ppermute(x, 'grp', [(g, g ^ 1) for g in range(lax.axis_size('grp'))])]
    dynamic_update_slice x0 -> x1, local copies, waits for them, and re-layouts: none -> 1.04 us  [on_device(): lax.dynamic_update_slice(per_slot, swap(for_other), (0, 3 * nf // 2, 0))]
  transfers between devices with their start and end apart: 4 -> 5, of which waited for: 2 -> 3; matrix products, arithmetic and copies ran while one was open for 2% -> 4% of each run, Pallas kernels for 39% -> 43%
where the time goes in v2:
time: 78.5 us; the launch traced here: 78.1 us
  Pallas kernels  40.8 us (52%)
  starting transfers between devices  17.8 us (23%)
  waiting for transfers between devices  15.3 us (19%)
  local copies, waits for them, and re-layouts  2.74 us (3%)
  other arithmetic  0.8 us (1%)
    pallas_call x1, Pallas kernels, on_device(): pl.pallas_call(adjoint_kernel, out_shape=(shape(second_message, BF16), sh...  13.5 us
    pallas_call x1, Pallas kernels, on_device(): pl.pallas_call(forward_kernel, out_shape=(shape((leaves, nf, rank), F32),...  12.4 us
    all_to_all x1, starting transfers between devices, exchange(): lax.all_to_all(x, ('grp', 'dev'), split_axis=0, concat_axis=0, tiled=True)  11.6 us
    all_to_all x1, waiting for transfers between devices, on_device(): lax.all_to_all(per_slot, ('grp', 'dev'), split_axis=0, concat_axis=0, axi...  7.7 us
    all_to_all x1, starting transfers between devices, on_device(): lax.all_to_all(per_slot, ('grp', 'dev'), split_axis=0, concat_axis=0, axi...  5.52 us
    all_to_all x1, waiting for transfers between devices, exchange(): lax.all_to_all(x, ('grp', 'dev'), split_axis=0, concat_axis=0, tiled=True)  5.51 us
    pallas_call x1, Pallas kernels, on_device(): pl.pallas_call(finish_kernel, out_shape=(shape((leaves, nf, rank), BF16),...  4.62 us
    pallas_call x1, Pallas kernels, on_device(): pl.pallas_call(lift_kernel, out_shape=shape(message, BF16), in_specs=[HBM...  3.83 us
  transfers between devices with their start and end apart: 5, of which 3 were waited for; matrix products, arithmetic and copies ran while one was open for 4% of the time, Pallas kernels for 43%

profile of v2, /device:TPU:0, one launch (start us, length us, event | category | flops | bytes accessed | tf_op | source)
XLA Modules:
  0.0 78.1 jit_solution(17705656270660923081)
XLA Ops:
  0.6 3.8 %lift.1.outgoing = bf16[128,56,128]{2,1,0:T(8,128)(2,1)} custom-call(s32[3,1,128]{2,1,0:T(1,128)} %bitcast.12, bf16[64,32,64]{2,1,0:T(8,128)(2,1)} %bitcast.8, bf16[64,64,64]{2,1,0:T(8,128)(2,1)} %up_leaf.3, bf16[8,64,64]{2,1,0:T(8,128)(2,1)} %up_mid.3), custom_call_target="tpu_custom_call" | custom-call | tf_op jit(solution)/shard_map/lift/pallas_call | solution.py:457
  4.5 11.6 %all-to-all-start = ((bf16[128,56,128]{2,1,0:T(8,128)(2,1)}), bf16[128,56,128]{2,1,0:T(8,128)(2,1)}, u32[]{:S(2)}, u32[]{:S(2)}) async-start(bf16[128,56,128]{2,1,0:T(8,128)(2,1)} %lift.1.outgoing), calls=%async_computation | async-start | bytes 3670016 | tf_op jit(solution)/shard_map/all_to_all | solution.py:419
  16.1 3.2 %top.1 = (bf16[8,32,64]{2,1,0:T(8,128)(2,1)}, f32[64,16,128]{2,1,0:T(8,128)}, bf16[64,16,128]{2,1,0:T(8,128)(2,1)}) custom-call(s32[1,16]{1,0:T(1,128)} %top_list.3, bf16[64,32,64]{2,1,0:T(8,128)(2,1)} %bitcast.6, bf16[64,64,64]{2,1,0:T(8,128)(2,1)} %up_leaf.3, bf16[8,64,64]{2,1,0:T(8,128)(2,1)} %up_mid.3, bf16[1,16,64,64]{3,2,1,0:T(8,128)(2,1)} %couple_top.3, ...), custom_call_target="tpu_custom_call" | custom-call | flops 1000000 | bytes 100000 | tf_op jit(solution)/shard_map/top/pallas_call | solution.py:477
  19.2 0.0 copy-start.3
  19.2 13.5 %adjoint.1 = (bf16[64,112,128]{2,1,0:T(8,128)(2,1)}, bf16[64,48,128]{2,1,0:T(8,128)(2,1)}) custom-call(s32[16,64]{1,0:T(8,128)} %bitcast.10, s32[8,16]{1,0:T(8,128)} %mid_list_in.3, bf16[64,32,64]{2,1,0:T(8,128)(2,1)} %bitcast.7, bf16[8,32,64]{2,1,0:T(8,128)(2,1)} %get-tuple-element.15.mid_adj_in, bf16[64,16,64,64]{3,2,1,0:T(8,128)(2,1)} %couple_leaf_in.3, ...), custom_call_target="tpu_custom_call" | custom-call | flops 1000000 | bytes 100000 | tf_op jit(solution)/shard_map/adjoint/pallas_call | solution.py:488
  32.8 0.0 copy-start.1
  32.8 0.1 collective-permute-start.1
  32.9 0.0 copy-done.3
  32.9 0.5 collective-permute-start.2
  33.4 2.1 %collective-permute-done.1 = bf16[64,48,128]{2,1,0:T(8,128)(2,1)S(1)} collective-permute-done((bf16[64,48,128]{2,1,0:T(8,128)(2,1)}, bf16[64,48,128]{2,1,0:T(8,128)(2,1)S(1)}, u32[]{:S(2)}, u32[]{:S(2)}) %collective-permute-start.1) | collective-permute-done | bytes 786464 | tf_op jit(solution)/shard_map/ppermute | solution.py:423
  35.4 1.0 %constant_dynamic-update-slice_fusion = bf16[64,112,128]{2,1,0:T(8,128)(2,1)} fusion(bf16[64,112,128]{2,1,0:T(8,128)(2,1)} %get-tuple-element.16, bf16[64,48,128]{2,1,0:T(8,128)(2,1)S(1)} %collective-permute-done.1), kind=kLoop, calls=%fused_computation.2 | loop fusion | bytes 1572864 | tf_op jit(solution)/shard_map/dynamic_update_slice | solution.py:512
  36.5 0.0 collective-permute-done.2
  36.5 0.0 copy-done.1
  36.5 0.8 %fusion = bf16[64,112,128]{2,1,0:T(8,128)(2,1)} fusion(bf16[64,112,128]{2,1,0:T(8,128)(2,1)} %constant_dynamic-update-slice_fusion, f32[64,16,128]{2,1,0:T(8,128)S(1)} %copy-done.1, bf16[64,16,128]{2,1,0:T(8,128)(2,1)S(1)} %collective-permute-done.2), kind=kLoop, calls=%fused_computation.1 | loop fusion | flops 393216 | bytes 1048576 | tf_op jit(solution)/shard_map/dynamic_update_slice | solution.py:513
  37.3 5.5 %all-to-all-done.arrived_in = bf16[128,56,128]{2,1,0:T(8,128)(2,1)} async-done(((bf16[128,56,128]{2,1,0:T(8,128)(2,1)}), bf16[128,56,128]{2,1,0:T(8,128)(2,1)}, u32[]{:S(2)}, u32[]{:S(2)}) %all-to-all-start) | async-done | bytes 1835040 | tf_op jit(solution)/shard_map/all_to_all | solution.py:419
  42.8 5.5 %all-to-all-start.1 = ((bf16[64,112,128]{2,1,0:T(8,128)(2,1)}), bf16[64,112,128]{2,1,0:T(8,128)(2,1)}, u32[]{:S(2)}, u32[]{:S(2)}) async-start(bf16[64,112,128]{2,1,0:T(8,128)(2,1)} %fusion), calls=%async_computation.1 | async-start | bytes 3670016 | tf_op jit(solution)/shard_map/all_to_all | solution.py:515
  48.3 1.0 %slice.4.own_half = bf16[128,8,128]{2,1,0:T(8,128)(2,1)S(1)} slice(bf16[128,56,128]{2,1,0:T(8,128)(2,1)} %all-to-all-done.arrived_in), slice={[0:128], [48:56], [0:128]} | slice | bytes 524288 | tf_op jit(solution)/shard_map/slice | solution.py:519
  49.3 0.0 copy-start
  49.3 0.1 collective-permute-start
  49.4 12.4 %forward.1 = (f32[64,32,64]{2,1,0:T(8,128)}, f32[8,32,64]{2,1,0:T(8,128)}) custom-call(s32[16,64]{1,0:T(8,128)} %bitcast.11, s32[8,16]{1,0:T(8,128)} %mid_list_in.3, bf16[128,56,128]{2,1,0:T(8,128)(2,1)} %all-to-all-done.arrived_in, bf16[64,16,64,64]{3,2,1,0:T(8,128)(2,1)} %couple_leaf_in.3, bf16[8,16,64,64]{3,2,1,0:T(8,128)(2,1)} %couple_mid_in.3), custom_call_target="tpu_custom_call" | custom-call | flops 1000000 | bytes 100000 | tf_op jit(solution)/shard_map/forward/pallas_call | solution.py:521
  61.8 0.0 copy-done
  61.8 0.0 collective-permute-done.other_half
  61.8 0.0 copy-start.2
  61.8 0.7 copy-done.2
  62.5 4.6 %finish.1 = (bf16[64,32,64]{2,1,0:T(8,128)(2,1)}, bf16[8,64,512]{2,1,0:T(8,128)(2,1)}, bf16[64,512]{1,0:T(8,128)(2,1)}) custom-call(s32[1,16]{1,0:T(1,128)} %top_list.3, bf16[128,8,128]{2,1,0:T(8,128)(2,1)} %copy-done, bf16[128,8,128]{2,1,0:T(8,128)(2,1)} %copy-done.2, f32[64,32,64]{2,1,0:T(8,128)} %get-tuple-element.12.leaf_near, ...), custom_call_target="tpu_custom_call" | custom-call | flops 1000000 | bytes 100000 | tf_op jit(solution)/shard_map/finish/pallas_call | solution.py:544
  67.2 7.7 %all-to-all-done.1.returned_in = bf16[64,112,128]{2,1,0:T(8,128)(2,1)} async-done(((bf16[64,112,128]{2,1,0:T(8,128)(2,1)}), bf16[64,112,128]{2,1,0:T(8,128)(2,1)}, u32[]{:S(2)}, u32[]{:S(2)}) %all-to-all-start.1) | async-done | bytes 1835040 | tf_op jit(solution)/shard_map/all_to_all | solution.py:515
  74.9 3.3 %lower.1 = bf16[64,32,64]{2,1,0:T(8,128)(2,1)} custom-call(s32[3,1,128]{2,1,0:T(1,128)} %bitcast.13, bf16[64,112,128]{2,1,0:T(8,128)(2,1)} %all-to-all-done.1.returned_in, bf16[8,64,512]{2,1,0:T(8,128)(2,1)} %get-tuple-element.20.down_leaf_in, bf16[64,512]{1,0:T(8,128)(2,1)} %get-tuple-element.21.down_mid_in), custom_call_target="tpu_custom_call" | custom-call | tf_op jit(solution)/shard_map/lower/pallas_call | solution.py:558
Async XLA Ops:
  4.5 38.3 %all-to-all-start = ((bf16[128,56,128]{2,1,0:T(8,128)(2,1)}), bf16[128,56,128]{2,1,0:T(8,128)(2,1)}, u32[]{:S(2)}, u32[]{:S(2)}) async-start(bf16[128,56,128]{2,1,0:T(8,128)(2,1)} %lift.1.outgoing), calls=%async_computation | async-start | bytes 3670016 | tf_op jit(solution)/shard_map/all_to_all | solution.py:419
  19.2 13.6 %copy-start.3 = (bf16[64,16,128]{2,1,0:T(8,128)(2,1)S(1)}, bf16[64,16,128]{2,1,0:T(8,128)(2,1)}, u32[]{:S(2)}) copy-start(bf16[64,16,128]{2,1,0:T(8,128)(2,1)} %get-tuple-element.19) | copy-start | bytes 786436
  32.8 3.7 %copy-start.1 = (f32[64,16,128]{2,1,0:T(8,128)S(1)}, f32[64,16,128]{2,1,0:T(8,128)}, u32[]{:S(2)}) copy-start(f32[64,16,128]{2,1,0:T(8,128)} %get-tuple-element.18) | copy-start | bytes 1572868
  32.8 2.7 %collective-permute-start.1 = (bf16[64,48,128]{2,1,0:T(8,128)(2,1)}, bf16[64,48,128]{2,1,0:T(8,128)(2,1)S(1)}, u32[]{:S(2)}, u32[]{:S(2)}) collective-permute-start(bf16[64,48,128]{2,1,0:T(8,128)(2,1)} %get-tuple-element.17), channel_id=1, source_target_pairs={{0,16},{16,0},{32,48},{48,32},{64,80},{80,64},{96,112},{112,96},{1... | collective-permute-start | bytes 2359304 | tf_op jit(solution)/shard_map/ppermute | solution.py:423
  32.9 3.6 %collective-permute-start.2 = (bf16[64,16,128]{2,1,0:T(8,128)(2,1)S(1)}, bf16[64,16,128]{2,1,0:T(8,128)(2,1)S(1)}, u32[]{:S(2)}, u32[]{:S(2)}) collective-permute-start(bf16[64,16,128]{2,1,0:T(8,128)(2,1)S(1)} %copy-done.3), channel_id=1, source_target_pairs={{0,16},{16,0},{32,48},{48,32},{64,80},{80,64},{96,112},{112,96},{1... | collective-permute-start | bytes 786440 | tf_op jit(solution)/shard_map/ppermute | solution.py:423
  42.8 32.1 %all-to-all-start.1 = ((bf16[64,112,128]{2,1,0:T(8,128)(2,1)}), bf16[64,112,128]{2,1,0:T(8,128)(2,1)}, u32[]{:S(2)}, u32[]{:S(2)}) async-start(bf16[64,112,128]{2,1,0:T(8,128)(2,1)} %fusion), calls=%async_computation.1 | async-start | bytes 3670016 | tf_op jit(solution)/shard_map/all_to_all | solution.py:515
  49.3 12.5 %copy-start = (bf16[128,8,128]{2,1,0:T(8,128)(2,1)}, bf16[128,8,128]{2,1,0:T(8,128)(2,1)S(1)}, u32[]{:S(2)}) copy-start(bf16[128,8,128]{2,1,0:T(8,128)(2,1)S(1)} %slice.4.own_half) | copy-start | bytes 786436
  49.3 12.5 %collective-permute-start = (bf16[128,8,128]{2,1,0:T(8,128)(2,1)S(1)}, bf16[128,8,128]{2,1,0:T(8,128)(2,1)S(1)}, u32[]{:S(2)}, u32[]{:S(2)}) collective-permute-start(bf16[128,8,128]{2,1,0:T(8,128)(2,1)S(1)} %slice.4.own_half), channel_id=1, source_target_pairs={{0,16},{16,0},{32,48},{48,32},{64,80},{80,64},{96,112},{112,96},{1... | collective-permute-start | bytes 786440 | tf_op jit(solution)/shard_map/ppermute | solution.py:423
  61.8 0.7 copy-start.2

commit v3 on v2

--- a/solution.py
+++ b/solution.py
@@ -47,57 +47,62 @@
     return [below[:, i * rank : (i + 1) * rank] for i in range(8)]
 
 
+def device_of(i, core):
+    return (i >> 4) * 32 + core * 16 + (i & 15)
+
+
+def place_of(p):
+    return (p >> 5) * 16 + (p & 15)
+
+
 def lift_kernel(
     slots_in, src_in, up_leaf_in, up_mid_in, out, slots, src, up_leaf, up_mid, message, mid_src, tile, sems
 ):
     leaves, nf, rank = src.shape
     mids = up_mid.shape[0]
+    half = nf // 2
+    core = lax.axis_index("grp") & 1
     parts = 4
     part = out.shape[0] // parts
-    fetch_src = pltpu.make_async_copy(src_in, src, sems.at[0])
-    fetch_leaf = pltpu.make_async_copy(up_leaf_in, up_leaf, sems.at[1])
-    fetch_mid = pltpu.make_async_copy(up_mid_in, up_mid, sems.at[2])
+    fetch_src = pltpu.make_async_copy(src_in, src, sems.at[4])
+    fetch_leaf = pltpu.make_async_copy(up_leaf_in, up_leaf, sems.at[5])
+    fetch_mid = pltpu.make_async_copy(up_mid_in, up_mid, sems.at[6])
     fetch_slots = pltpu.make_async_copy(slots_in, slots, sems.at[7])
     fetch_slots.start()
     fetch_src.start()
     fetch_leaf.start()
     fetch_mid.start()
 
-    def pack_leaf(p, carry):
-        message[p, :nf] = side(src[slots[0, 0, p]], src[slots[1, 0, p]])
+    def pack_leaf(i, carry):
+        for place in range(2):
+            p = device_of(i, core ^ place)
+            first = 3 * half * place
+            message[i, first : first + nf] = side(src[slots[0, 0, p]], src[slots[1, 0, p]])
         return carry
 
     fetch_slots.wait()
     fetch_src.wait()
-    lax.fori_loop(0, out.shape[0], pack_leaf, 0, unroll=16)
+    lax.fori_loop(0, out.shape[0], pack_leaf, 0, unroll=8)
     fetch_leaf.wait()
     for c in range(mids):
         mid_src[c] = lift(src, up_leaf, c).astype(BF16)
     fetch_mid.wait()
-    top_src = lift(mid_src, up_mid, 0).astype(BF16)
-    for core in range(2):
-        top_half = fold(top_src[core * nf // 2 : (core + 1) * nf // 2])
-        for c in range(mids):
-            tile[core, c] = jnp.concatenate([fold(mid_src[c]), top_half], axis=0)
+    top_src = fold(lift(mid_src, up_mid, 0).astype(BF16))
+    for c in range(mids):
+        tile[c] = jnp.concatenate([fold(mid_src[c]), top_src], axis=0)
+
+    def pack_rest(i, carry):
+        message[i, nf : 3 * half] = tile[slots[2, 0, device_of(i, core)] - leaves, :half]
+        message[i, 3 * half + nf :] = tile[slots[2, 0, device_of(i, core ^ 1)] - leaves]
+        return carry
 
     sends = []
     for n in range(parts):
-        for core in range(2):
-
-            def pack_rest(i, carry):
-                p = n * part + core * (part // 2) + i
-                message[p, nf:] = tile[core, slots[2, 0, p] - leaves]
-                return carry
-
-            lax.fori_loop(0, part // 2, pack_rest, 0, unroll=16)
+        lax.fori_loop(n * part, (n + 1) * part, pack_rest, 0, unroll=8)
         place = pl.ds(n * part, part)
-        sends.append(pltpu.make_async_copy(message.at[place], out.at[place], sems.at[3 + n]))
+        sends.append(pltpu.make_async_copy(message.at[place], out.at[place], sems.at[n]))
         sends[n].start()
     wait_all(sends)
-
-
-def device_of(i, core):
-    return (i >> 4) * 32 + core * 16 + (i & 15)
 
 
 def top_kernel(top_list, adj, up_leaf, up_mid, couple_top, outgoing, mid_adj, own, other, total):
@@ -112,7 +117,7 @@
         for j in range(4):
             p = top_list[0, k + j]
             place = ((p >> 4) & 1) ^ core
-            total[place, (p >> 5) * 16 + (p & 15)] += fold(terms[:, j * rank : (j + 1) * rank])
+            total[place, place_of(p)] += fold(terms[:, j * rank : (j + 1) * rank])
     own[...] = total[0]
     other[...] = total[1].astype(BF16)
 
@@ -136,17 +141,22 @@
     couple_mid_in,
     out,
     other,
+    leaf_pairs_out,
+    mid_pairs_out,
     leaf_list,
     mid_list,
     adj,
     mid_adj,
     couple_leaf,
     couple_mid,
+    leaf_pairs,
+    mid_pairs,
     message,
     even,
     odd,
     sems,
     leaf_sems,
+    pair_sems,
     out_sems,
 ):
     width, rank = couple_leaf.shape[1:3]
@@ -160,6 +170,10 @@
         place = pl.ds(pl.multiple_of(step * chunk, chunk), chunk)
         return pltpu.make_async_copy(couple_leaf_in.at[place], couple_leaf.at[place], leaf_sems.at[step])
 
+    def keep_pairs(step):
+        place = pl.ds(pl.multiple_of(step * chunk, chunk), chunk)
+        return pltpu.make_async_copy(leaf_pairs.at[place], leaf_pairs_out.at[place], pair_sems.at[step])
+
     fetches = [
         pltpu.make_async_copy(leaf_list_in, leaf_list, sems.at[0]),
         pltpu.make_async_copy(mid_list_in, mid_list, sems.at[1]),
@@ -167,6 +181,7 @@
         pltpu.make_async_copy(mid_adj_in, mid_adj, sems.at[3]),
     ]
     fetch_mid = pltpu.make_async_copy(couple_mid_in, couple_mid, sems.at[4])
+    keep_mid = pltpu.make_async_copy(mid_pairs, mid_pairs_out, sems.at[5])
     start_all(fetches)
     for step in range(steps):
         fetch(step).start()
@@ -180,10 +195,12 @@
     lax.fori_loop(0, even.shape[0], clear, 0, unroll=8)
     wait_all(fetches)
 
-    def scatter(row, blocks, slot):
+    def scatter(row, blocks, slot, keep):
         for k in range(0, width, 4):
-            terms = mul(row, side(*[blocks(k + j) for j in range(4)]))
+            pairs = [side(blocks(k), blocks(k + 1)), side(blocks(k + 2), blocks(k + 3))]
+            terms = mul(row, side(*pairs))
             for j in range(2):
+                keep(k // 2 + j, pairs[j])
                 pair = terms[:, 2 * j * rank : 2 * (j + 1) * rank]
                 crossed = pltpu.roll(pair[half:], rank, 1)
                 e, o = slot(k + 2 * j), slot(k + 2 * j + 1)
@@ -196,13 +213,23 @@
         fetch(step).wait()
         for a in range(chunk):
             g = step * chunk + a
-            scatter(adj[g], lambda k: couple_leaf[g, k], lambda k: leaf_list[k, g])
+
+            def keep(k, pair):
+                leaf_pairs[g, k] = pair
+
+            scatter(adj[g], lambda k: couple_leaf[g, k], lambda k: leaf_list[k, g], keep)
+        keep_pairs(step).start()
         return carry
 
     lax.fori_loop(0, steps, leaf_step, 0)
     fetch_mid.wait()
     for c in range(mid_adj.shape[0]):
-        scatter(mid_adj[c], lambda k: couple_mid[c, k], lambda k: mid_list[c, k])
+
+        def keep(k, pair):
+            mid_pairs[c, k] = pair
+
+        scatter(mid_adj[c], lambda k: couple_mid[c, k], lambda k: mid_list[c, k], keep)
+    keep_mid.start()
 
     core = lax.axis_index("grp") & 1
     sends = []
@@ -225,13 +252,16 @@
             )
             copy.start()
             sends.append(copy)
+    for step in range(steps):
+        keep_pairs(step).wait()
+    keep_mid.wait()
     wait_all(sends)
 
 
-def gather(blocks, partner):
+def gather(pairs, partner):
     near = 0
     for k in range(0, 16, 4):
-        near += mul_t(side(*[partner(k + j) for j in range(4)]), side(*[blocks(k + j) for j in range(4)]))
+        near += mul_t(side(*[partner(k + j) for j in range(4)]), side(pairs(k // 2), pairs(k // 2 + 1)))
     return near
 
 
@@ -239,15 +269,16 @@
     leaf_list_in,
     mid_list_in,
     arrived_in,
-    couple_leaf_in,
-    couple_mid_in,
+    swapped_in,
+    leaf_pairs_in,
+    mid_pairs_in,
     leaf_near_out,
     mid_near_out,
     leaf_list,
     mid_list,
     arrived,
-    couple_leaf,
-    couple_mid,
+    leaf_pairs,
+    mid_pairs,
     leaf_near,
     mid_near,
     coeff,
@@ -259,27 +290,27 @@
     leaves, nf, rank = leaf_near.shape
     steps = leaf_sems.shape[0]
     chunk = leaves // steps
-    parts = arrived_sems.shape[0]
-    part = arrived.shape[0] // parts
-
-    def place(step):
+    def leaves_of(step):
         return pl.ds(pl.multiple_of(step * chunk, chunk), chunk)
 
     def fetch(step):
-        return pltpu.make_async_copy(couple_leaf_in.at[place(step)], couple_leaf.at[place(step)], leaf_sems.at[step])
+        return pltpu.make_async_copy(leaf_pairs_in.at[leaves_of(step)], leaf_pairs.at[leaves_of(step)], leaf_sems.at[step])
 
     def keep(step):
-        return pltpu.make_async_copy(leaf_near.at[place(step)], leaf_near_out.at[place(step)], near_sems.at[step])
+        return pltpu.make_async_copy(leaf_near.at[leaves_of(step)], leaf_near_out.at[leaves_of(step)], near_sems.at[step])
 
     lists = [
         pltpu.make_async_copy(leaf_list_in, leaf_list, sems.at[0]),
         pltpu.make_async_copy(mid_list_in, mid_list, sems.at[1]),
     ]
+    part = arrived.shape[1] // 2
     messages = []
-    for n in range(parts):
-        rows_n = pl.ds(n * part, part)
-        messages.append(pltpu.make_async_copy(arrived_in.at[rows_n], arrived.at[rows_n], arrived_sems.at[n]))
-    fetch_mid = pltpu.make_async_copy(couple_mid_in, couple_mid, sems.at[2])
+    for n in range(2):
+        rows = pl.ds(n * part, part)
+        for place, source in ((0, arrived_in), (1, swapped_in)):
+            piece = source.at[rows, pl.ds(0, arrived.shape[2])]
+            messages.append(pltpu.make_async_copy(piece, arrived.at[place, rows], arrived_sems.at[2 * n + place]))
+    fetch_mid = pltpu.make_async_copy(mid_pairs_in, mid_pairs, sems.at[2])
     keep_mid = pltpu.make_async_copy(mid_near, mid_near_out, sems.at[3])
     start_all(messages)
     start_all(lists)
@@ -287,30 +318,35 @@
         fetch(step).start()
     fetch_mid.start()
 
-    def unpack(p, carry):
-        pair = arrived[p, :nf]
-        coeff[3 * p] = pair[:, :rank]
-        coeff[3 * p + 1] = pair[:, rank:]
-        coeff[3 * p + 2] = unfold(arrived[p, nf : nf + nf // 2])
+    core = lax.axis_index("grp") & 1
+
+    def unpack(i, carry):
+        for place in range(2):
+            p = device_of(i, core ^ place)
+            pair = arrived[place, i, :nf]
+            coeff[3 * p] = pair[:, :rank]
+            coeff[3 * p + 1] = pair[:, rank:]
+            coeff[3 * p + 2] = unfold(arrived[place, i, nf:])
         return carry
 
-    for n in range(parts):
-        messages[n].wait()
-        lax.fori_loop(n * part, (n + 1) * part, unpack, 0, unroll=8)
+    for n in range(2):
+        messages[2 * n].wait()
+        messages[2 * n + 1].wait()
+        lax.fori_loop(n * part, (n + 1) * part, unpack, 0, unroll=4)
     wait_all(lists)
 
     def leaf_step(step, carry):
         fetch(step).wait()
         for a in range(chunk):
             g = step * chunk + a
-            leaf_near[g] = gather(lambda k: couple_leaf[g, k], lambda k: coeff[leaf_list[k, g]])
+            leaf_near[g] = gather(lambda k: leaf_pairs[g, k], lambda k: coeff[leaf_list[k, g]])
         keep(step).start()
         return carry
 
     lax.fori_loop(0, steps, leaf_step, 0)
     fetch_mid.wait()
     for c in range(mid_near.shape[0]):
-        mid_near[c] = gather(lambda k: couple_mid[c, k], lambda k: coeff[mid_list[c, k]])
+        mid_near[c] = gather(lambda k: mid_pairs[c, k], lambda k: coeff[mid_list[c, k]])
     keep_mid.start()
     for step in range(steps):
         keep(step).wait()
@@ -318,21 +354,22 @@
 
 
 def finish_kernel(
-    top_list, own_half, other_half, leaf_near, mid_near, up_leaf, up_mid, couple_top, forward, down_leaf, down_mid
+    top_list, own_tops, other_tops, leaf_near, mid_near, up_leaf, up_mid, couple_top, forward, down_leaf, down_mid, tops
 ):
-    nf, rank = forward.shape[1:]
+    rank = forward.shape[2]
     shape = (rank, rank)
     eye = (lax.broadcasted_iota(jnp.int32, shape, 0) == lax.broadcasted_iota(jnp.int32, shape, 1)).astype(BF16)
+    core = lax.axis_index("grp") & 1
+    tops[0] = own_tops[...]
+    tops[1] = other_tops[...]
 
     def partner(k):
-        j = top_list[0, k]
-        return jnp.concatenate([unfold(own_half[j]), unfold(other_half[j])], axis=0)
-
-    near = gather(lambda k: couple_top[0, k], partner)
-    swapped = jnp.concatenate([near[nf // 2 :], near[: nf // 2]], axis=0)
-    core = lax.axis_index("grp") % 2
+        p = top_list[0, k]
+        return unfold(tops[((p >> 4) & 1) ^ core, place_of(p)])
+
+    near = gather(lambda k: side(couple_top[0, 2 * k], couple_top[0, 2 * k + 1]), partner)
     down_mid[...] = turn(up_mid, 0, eye)
-    below_top = lower(jnp.where(core == 0, near, swapped).astype(BF16), down_mid[...])
+    below_top = lower(near.astype(BF16), down_mid[...])
     for c in range(mid_near.shape[0]):
         down = turn(up_leaf, c, eye)
         down_leaf[c] = down
@@ -416,7 +453,8 @@
 
 
 def exchange(x):
-    return lax.all_to_all(x, ("grp", "dev"), split_axis=0, concat_axis=0, tiled=True)
+    order = [[device_of(i, core) for i in range(x.shape[0])] for core in range(2)]
+    return lax.all_to_all(x, ("grp", "dev"), split_axis=0, concat_axis=0, axis_index_groups=order, tiled=True)
 
 
 def swap(x):
@@ -445,9 +483,8 @@
     adj = jnp.swapaxes(adj_leaf, 1, 2)
     slots = jnp.transpose(send_slots, (2, 0, 1))
     leaf_slots = leaf_list.T
-    message = (peers, 7 * nf // 4, 2 * rank)
     chips = peers // 2
-    second_message = (chips, 7 * nf // 2, 2 * rank)
+    message = (chips, 7 * nf // 2, 2 * rank)
     swapped_message = (chips, 3 * nf // 2, 2 * rank)
     top_shape = (chips, nf // 2, 2 * rank)
     shape = jax.ShapeDtypeStruct
@@ -466,7 +503,7 @@
             pltpu.VMEM((mids, rank, rank), BF16),
             pltpu.VMEM(message, BF16),
             pltpu.VMEM((mids, nf, rank), BF16),
-            pltpu.VMEM((2, mids, 3 * nf // 4, 2 * rank), BF16),
+            pltpu.VMEM((mids, nf, 2 * rank), BF16),
             pltpu.SemaphoreType.DMA((8,)),
         ],
         compiler_params=params,
@@ -485,11 +522,18 @@
         name="top",
     )(top_list, adj, up_leaf, up_mid, couple_top, outgoing)
     swapped_terms = swap(other_terms)
-    per_slot, for_other = pl.pallas_call(
+    leaf_pairs_shape = (leaves, width // 2, rank, 2 * rank)
+    mid_pairs_shape = (mids, width // 2, rank, 2 * rank)
+    per_slot, for_other, leaf_pairs, mid_pairs = pl.pallas_call(
         adjoint_kernel,
-        out_shape=(shape(second_message, BF16), shape(swapped_message, BF16)),
+        out_shape=(
+            shape(message, BF16),
+            shape(swapped_message, BF16),
+            shape(leaf_pairs_shape, BF16),
+            shape(mid_pairs_shape, BF16),
+        ),
         in_specs=[HBM] * 6,
-        out_specs=(HBM, HBM),
+        out_specs=(HBM, HBM, HBM, HBM),
         scratch_shapes=[
             pltpu.SMEM(leaf_slots.shape, jnp.int32),
             pltpu.SMEM(mid_list.shape, jnp.int32),
@@ -497,10 +541,13 @@
             pltpu.VMEM(mid_adj.shape, BF16),
             pltpu.VMEM(couple_leaf.shape, BF16),
             pltpu.VMEM(couple_mid.shape, BF16),
+            pltpu.VMEM(leaf_pairs_shape, BF16),
+            pltpu.VMEM(mid_pairs_shape, BF16),
             pltpu.VMEM((2,) + swapped_message, BF16),
             pltpu.VMEM((3 * peers, nf // 2, 2 * rank), F32),
             pltpu.VMEM((3 * peers, nf // 2, 2 * rank), F32),
-            pltpu.SemaphoreType.DMA((5,)),
+            pltpu.SemaphoreType.DMA((6,)),
+            pltpu.SemaphoreType.DMA((steps,)),
             pltpu.SemaphoreType.DMA((steps,)),
             pltpu.SemaphoreType.DMA((4,)),
         ],
@@ -511,24 +558,20 @@
     top_terms = (own_terms + swapped_terms.astype(F32)).astype(BF16)
     per_slot = lax.dynamic_update_slice(per_slot, swap(for_other), (0, 3 * nf // 2, 0))
     per_slot = lax.dynamic_update_slice(per_slot, top_terms, (0, 3 * nf, 0))
-    same_core = [[device_of(i, core) for i in range(chips)] for core in range(2)]
-    returned = lax.all_to_all(
-        per_slot, ("grp", "dev"), split_axis=0, concat_axis=0, axis_index_groups=same_core, tiled=True
-    )
-
-    own_half = arrived[:, 3 * nf // 2 :]
-    other_half = swap(own_half)
+    returned = exchange(per_slot)
+
+    swapped = swap(arrived[:, 3 * nf // 2 :])
     leaf_near, mid_near = pl.pallas_call(
         forward_kernel,
         out_shape=(shape((leaves, nf, rank), F32), shape((mids, nf, rank), F32)),
-        in_specs=[HBM] * 5,
+        in_specs=[HBM] * 6,
         out_specs=(HBM, HBM),
         scratch_shapes=[
             pltpu.SMEM(leaf_slots.shape, jnp.int32),
             pltpu.SMEM(mid_list.shape, jnp.int32),
-            pltpu.VMEM(message, BF16),
-            pltpu.VMEM(couple_leaf.shape, BF16),
-            pltpu.VMEM(couple_mid.shape, BF16),
+            pltpu.VMEM((2,) + swapped_message, BF16),
+            pltpu.VMEM(leaf_pairs_shape, BF16),
+            pltpu.VMEM(mid_pairs_shape, BF16),
             pltpu.VMEM((leaves, nf, rank), F32),
             pltpu.VMEM((mids, nf, rank), F32),
             pltpu.VMEM((3 * peers, nf, rank), BF16),
@@ -540,20 +583,27 @@
         compiler_params=params,
         cost_estimate=small,
         name="forward",
-    )(leaf_slots, mid_list, arrived, couple_leaf, couple_mid)
+    )(leaf_slots, mid_list, arrived, swapped, leaf_pairs, mid_pairs)
     forward, down_leaf, down_mid = pl.pallas_call(
         finish_kernel,
+        grid=(1,),
         out_shape=(
             shape((leaves, nf, rank), BF16),
             shape((mids, rank, 8 * rank), BF16),
             shape((rank, 8 * rank), BF16),
         ),
-        in_specs=[SMEM] + [VMEM] * 7,
+        in_specs=[
+            SMEM,
+            pl.BlockSpec(top_shape, lambda _: (0, 6, 0)),
+            pl.BlockSpec(top_shape, lambda _: (0, 3, 0)),
+        ]
+        + [VMEM] * 5,
         out_specs=(VMEM, VMEM, VMEM),
+        scratch_shapes=[pltpu.VMEM((2,) + top_shape, BF16)],
         compiler_params=params,
         cost_estimate=small,
         name="finish",
-    )(top_list, own_half, other_half, leaf_near, mid_near, up_leaf, up_mid, couple_top)
+    )(top_list, arrived, swapped, leaf_near, mid_near, up_leaf, up_mid, couple_top)
 
     adjoint = pl.pallas_call(
         lower_kernel,
@@ -562,7 +612,7 @@
         out_specs=HBM,
         scratch_shapes=[
             pltpu.SMEM(slots.shape, jnp.int32),
-            pltpu.VMEM(second_message, BF16),
+            pltpu.VMEM(message, BF16),
             pltpu.VMEM((mids, rank, 8 * rank), BF16),
             pltpu.VMEM((rank, 8 * rank), BF16),
             pltpu.VMEM((leaves, nf, rank), BF16),

time: 78.5 us -> 78.9 us (level)
  waiting for transfers between devices: 15.3 us -> 18.1 us
  Pallas kernels: 40.8 us -> 38 us
    pallas_call x1, Pallas kernels: 12.4 us -> 9.46 us  [on_device(): pl.pallas_call(forward_kernel, out_shape=(shape((leaves, nf, rank), F32),...]
    ppermute x3, waiting for transfers between devices: 2.09 us -> 4.86 us  [swap(): lax.ppermute(x, 'grp', [(g, g ^ 1) for g in range(lax.axis_size('grp'))])]
  transfers between devices with their start and end apart: 5 -> 5, of which waited for: 3 -> 4; matrix products, arithmetic and copies ran while one was open for 4% -> 4% of each run, Pallas kernels for 43% -> 39%
where the time goes in v3:
time: 78.9 us; the launch traced here: 78.4 us
  Pallas kernels  38 us (48%)
  starting transfers between devices  18.5 us (23%)
  waiting for transfers between devices  18.1 us (23%)
  local copies, waits for them, and re-layouts  2.38 us (3%)
  other arithmetic  0.79 us (1%)
    all_to_all x2, starting transfers between devices, exchange(): lax.all_to_all(x, ('grp', 'dev'), split_axis=0, concat_axis=0, axis_index...  17.8 us
    pallas_call x1, Pallas kernels, on_device(): pl.pallas_call(adjoint_kernel, out_shape=(shape(message, BF16), shape(swa...  13.5 us
    all_to_all x2, waiting for transfers between devices, exchange(): lax.all_to_all(x, ('grp', 'dev'), split_axis=0, concat_axis=0, axis_index...  13.2 us
    pallas_call x1, Pallas kernels, on_device(): pl.pallas_call(forward_kernel, out_shape=(shape((leaves, nf, rank), F32),...  9.46 us
    ppermute x3, waiting for transfers between devices, swap(): lax.ppermute(x, 'grp', [(g, g ^ 1) for g in range(lax.axis_size('grp'))])  4.86 us
    pallas_call x1, Pallas kernels, on_device(): pl.pallas_call(finish_kernel, grid=(1,), out_shape=(shape((leaves, nf, ra...  4.61 us
    pallas_call x1, Pallas kernels, on_device(): pl.pallas_call(lift_kernel, out_shape=shape(message, BF16), in_specs=[HBM...  4 us
    pallas_call x1, Pallas kernels, on_device(): pl.pallas_call(lower_kernel, out_shape=shape((leaves, nf, rank), BF16), i...  3.26 us
  transfers between devices with their start and end apart: 5, of which 4 were waited for; matrix products, arithmetic and copies ran while one was open for 4% of the time, Pallas kernels for 39%

profile of v3, /device:TPU:0, one launch (start us, length us, event | category | flops | bytes accessed | tf_op | source)
XLA Modules:
  0.0 78.4 jit_solution(5834692275737000381)
XLA Ops:
  0.6 4.0 %lift.1.outgoing = bf16[64,112,128]{2,1,0:T(8,128)(2,1)} custom-call(s32[3,1,128]{2,1,0:T(1,128)} %bitcast.12, bf16[64,32,64]{2,1,0:T(8,128)(2,1)} %bitcast.8, bf16[64,64,64]{2,1,0:T(8,128)(2,1)} %up_leaf.3, bf16[8,64,64]{2,1,0:T(8,128)(2,1)} %up_mid.3), custom_call_target="tpu_custom_call" | custom-call | tf_op jit(solution)/shard_map/lift/pallas_call | solution.py:494
  4.6 11.7 %all-to-all-start = ((bf16[64,112,128]{2,1,0:T(8,128)(2,1)}), bf16[64,112,128]{2,1,0:T(8,128)(2,1)}, u32[]{:S(2)}, u32[]{:S(2)}) async-start(bf16[64,112,128]{2,1,0:T(8,128)(2,1)} %lift.1.outgoing), calls=%async_computation | async-start | bytes 3670016 | tf_op jit(solution)/shard_map/all_to_all | solution.py:457
  16.4 3.2 %top.1 = (bf16[8,32,64]{2,1,0:T(8,128)(2,1)}, f32[64,16,128]{2,1,0:T(8,128)}, bf16[64,16,128]{2,1,0:T(8,128)(2,1)}) custom-call(s32[1,16]{1,0:T(1,128)} %top_list.3, bf16[64,32,64]{2,1,0:T(8,128)(2,1)} %bitcast.6, bf16[64,64,64]{2,1,0:T(8,128)(2,1)} %up_leaf.3, bf16[8,64,64]{2,1,0:T(8,128)(2,1)} %up_mid.3, bf16[1,16,64,64]{3,2,1,0:T(8,128)(2,1)} %couple_top.3, ...), custom_call_target="tpu_custom_call" | custom-call | flops 1000000 | bytes 100000 | tf_op jit(solution)/shard_map/top/pallas_call | solution.py:514
  19.5 0.0 copy-start.1
  19.5 13.5 %adjoint.1 = (bf16[64,112,128]{2,1,0:T(8,128)(2,1)}, bf16[64,48,128]{2,1,0:T(8,128)(2,1)}, bf16[64,8,64,128]{3,2,1,0:T(8,128)(2,1)}, bf16[8,8,64,128]{3,2,1,0:T(8,128)(2,1)}) custom-call(s32[16,64]{1,0:T(8,128)} %bitcast.10, s32[8,16]{1,0:T(8,128)} %mid_list_in.3, bf16[64,32,64]{2,1,0:T(8,128)(2,1)} %bitcast.7, ...), custom_call_target="tpu_custom_call" | custom-call | flops 1000000 | bytes 100000 | tf_op jit(solution)/shard_map/adjoint/pallas_call | solution.py:527
  33.1 0.0 copy-start
  33.1 0.1 collective-permute-start.1
  33.2 0.0 copy-done.1
  33.2 0.5 collective-permute-start.2
  33.7 2.1 %collective-permute-done.1 = bf16[64,48,128]{2,1,0:T(8,128)(2,1)S(1)} collective-permute-done((bf16[64,48,128]{2,1,0:T(8,128)(2,1)}, bf16[64,48,128]{2,1,0:T(8,128)(2,1)S(1)}, u32[]{:S(2)}, u32[]{:S(2)}) %collective-permute-start.1) | collective-permute-done | bytes 786464 | tf_op jit(solution)/shard_map/ppermute | solution.py:461
  35.7 1.1 %constant_dynamic-update-slice_fusion = bf16[64,112,128]{2,1,0:T(8,128)(2,1)} fusion(bf16[64,112,128]{2,1,0:T(8,128)(2,1)} %get-tuple-element.20, bf16[64,48,128]{2,1,0:T(8,128)(2,1)S(1)} %collective-permute-done.1), kind=kLoop, calls=%fused_computation.2 | loop fusion | bytes 1572864 | tf_op jit(solution)/shard_map/dynamic_update_slice | solution.py:559
  36.8 0.0 collective-permute-done.2
  36.8 0.0 copy-done
  36.8 0.8 %fusion = bf16[64,112,128]{2,1,0:T(8,128)(2,1)} fusion(bf16[64,112,128]{2,1,0:T(8,128)(2,1)} %constant_dynamic-update-slice_fusion, f32[64,16,128]{2,1,0:T(8,128)S(1)} %copy-done, bf16[64,16,128]{2,1,0:T(8,128)(2,1)S(1)} %collective-permute-done.2), kind=kLoop, calls=%fused_computation.1 | loop fusion | flops 393216 | bytes 1048576 | tf_op jit(solution)/shard_map/dynamic_update_slice | solution.py:560
  37.6 5.5 %all-to-all-done.arrived_in.own_tops = bf16[64,112,128]{2,1,0:T(8,128)(2,1)} async-done(((bf16[64,112,128]{2,1,0:T(8,128)(2,1)}), bf16[64,112,128]{2,1,0:T(8,128)(2,1)}, u32[]{:S(2)}, u32[]{:S(2)}) %all-to-all-start) | async-done | bytes 1835040 | tf_op jit(solution)/shard_map/all_to_all | solution.py:457
  43.1 6.1 %all-to-all-start.1 = ((bf16[64,112,128]{2,1,0:T(8,128)(2,1)}), bf16[64,112,128]{2,1,0:T(8,128)(2,1)}, u32[]{:S(2)}, u32[]{:S(2)}) async-start(bf16[64,112,128]{2,1,0:T(8,128)(2,1)} %fusion), calls=%async_computation.1 | async-start | bytes 3670016 | tf_op jit(solution)/shard_map/all_to_all | solution.py:457
  49.2 1.3 %slice.4 = bf16[64,64,128]{2,1,0:T(8,128)(2,1)S(1)} slice(bf16[64,112,128]{2,1,0:T(8,128)(2,1)} %all-to-all-done.arrived_in.own_tops), slice={[0:64], [48:112], [0:128]} | slice | bytes 2097152 | tf_op jit(solution)/shard_map/slice | solution.py:563
  50.5 0.1 collective-permute-start
  50.6 2.8 %collective-permute-done.swapped_in.other_tops = bf16[64,64,128]{2,1,0:T(8,128)(2,1)} collective-permute-done((bf16[64,64,128]{2,1,0:T(8,128)(2,1)S(1)}, bf16[64,64,128]{2,1,0:T(8,128)(2,1)}, u32[]{:S(2)}, u32[]{:S(2)}) %collective-permute-start) | collective-permute-done | bytes 1048608 | tf_op jit(solution)/shard_map/ppermute | solution.py:461
  53.4 9.5 %forward.1 = (f32[64,32,64]{2,1,0:T(8,128)}, f32[8,32,64]{2,1,0:T(8,128)}) custom-call(s32[16,64]{1,0:T(8,128)} %bitcast.11, s32[8,16]{1,0:T(8,128)} %mid_list_in.3, bf16[64,112,128]{2,1,0:T(8,128)(2,1)} %all-to-all-done.arrived_in.own_tops, bf16[64,64,128]{2,1,0:T(8,128)(2,1)} %collective-permute-done.swapped_in.other_tops, ...), custom_call_target="tpu_custom_call" | custom-call | flops 1000000 | bytes 100000 | tf_op jit(solution)/shard_map/forward/pallas_call | solution.py:564
  62.9 4.6 %finish.1 = (bf16[64,32,64]{2,1,0:T(8,128)(2,1)}, bf16[8,64,512]{2,1,0:T(8,128)(2,1)}, bf16[64,512]{1,0:T(8,128)(2,1)}) custom-call(s32[1,16]{1,0:T(1,128)} %top_list.3, bf16[64,112,128]{2,1,0:T(8,128)(2,1)} %all-to-all-done.arrived_in.own_tops, bf16[64,64,128]{2,1,0:T(8,128)(2,1)} %collective-permute-done.swapped_in.other_tops, ...), custom_call_target="tpu_custom_call" | custom-call | flops 1000000 | bytes 100000 | tf_op jit(solution)/shard_map/finish/pallas_call | solution.py:587
  67.5 7.7 %all-to-all-done.1.returned_in = bf16[64,112,128]{2,1,0:T(8,128)(2,1)} async-done(((bf16[64,112,128]{2,1,0:T(8,128)(2,1)}), bf16[64,112,128]{2,1,0:T(8,128)(2,1)}, u32[]{:S(2)}, u32[]{:S(2)}) %all-to-all-start.1) | async-done | bytes 1835040 | tf_op jit(solution)/shard_map/all_to_all | solution.py:457
  75.2 3.3 %lower.1 = bf16[64,32,64]{2,1,0:T(8,128)(2,1)} custom-call(s32[3,1,128]{2,1,0:T(1,128)} %bitcast.13, bf16[64,112,128]{2,1,0:T(8,128)(2,1)} %all-to-all-done.1.returned_in, bf16[8,64,512]{2,1,0:T(8,128)(2,1)} %get-tuple-element.24.down_leaf_in, bf16[64,512]{1,0:T(8,128)(2,1)} %get-tuple-element.25.down_mid_in), custom_call_target="tpu_custom_call" | custom-call | tf_op jit(solution)/shard_map/lower/pallas_call | solution.py:608
Async XLA Ops:
  4.6 38.5 %all-to-all-start = ((bf16[64,112,128]{2,1,0:T(8,128)(2,1)}), bf16[64,112,128]{2,1,0:T(8,128)(2,1)}, u32[]{:S(2)}, u32[]{:S(2)}) async-start(bf16[64,112,128]{2,1,0:T(8,128)(2,1)} %lift.1.outgoing), calls=%async_computation | async-start | bytes 3670016 | tf_op jit(solution)/shard_map/all_to_all | solution.py:457
  19.5 13.6 %copy-start.1 = (bf16[64,16,128]{2,1,0:T(8,128)(2,1)S(1)}, bf16[64,16,128]{2,1,0:T(8,128)(2,1)}, u32[]{:S(2)}) copy-start(bf16[64,16,128]{2,1,0:T(8,128)(2,1)} %get-tuple-element.23) | copy-start | bytes 786436
  33.1 3.8 %copy-start = (f32[64,16,128]{2,1,0:T(8,128)S(1)}, f32[64,16,128]{2,1,0:T(8,128)}, u32[]{:S(2)}) copy-start(f32[64,16,128]{2,1,0:T(8,128)} %get-tuple-element.22) | copy-start | bytes 1572868
  33.1 2.7 %collective-permute-start.1 = (bf16[64,48,128]{2,1,0:T(8,128)(2,1)}, bf16[64,48,128]{2,1,0:T(8,128)(2,1)S(1)}, u32[]{:S(2)}, u32[]{:S(2)}) collective-permute-start(bf16[64,48,128]{2,1,0:T(8,128)(2,1)} %get-tuple-element.21), channel_id=1, source_target_pairs={{0,16},{16,0},{32,48},{48,32},{64,80},{80,64},{96,112},{112,96},{1... | collective-permute-start | bytes 2359304 | tf_op jit(solution)/shard_map/ppermute | solution.py:461
  33.2 3.6 %collective-permute-start.2 = (bf16[64,16,128]{2,1,0:T(8,128)(2,1)S(1)}, bf16[64,16,128]{2,1,0:T(8,128)(2,1)S(1)}, u32[]{:S(2)}, u32[]{:S(2)}) collective-permute-start(bf16[64,16,128]{2,1,0:T(8,128)(2,1)S(1)} %copy-done.1), channel_id=1, source_target_pairs={{0,16},{16,0},{32,48},{48,32},{64,80},{80,64},{96,112},{112,96},{1... | collective-permute-start | bytes 786440 | tf_op jit(solution)/shard_map/ppermute | solution.py:461
  43.1 32.0 %all-to-all-start.1 = ((bf16[64,112,128]{2,1,0:T(8,128)(2,1)}), bf16[64,112,128]{2,1,0:T(8,128)(2,1)}, u32[]{:S(2)}, u32[]{:S(2)}) async-start(bf16[64,112,128]{2,1,0:T(8,128)(2,1)} %fusion), calls=%async_computation.1 | async-start | bytes 3670016 | tf_op jit(solution)/shard_map/all_to_all | solution.py:457
  50.5 2.9 %collective-permute-start = (bf16[64,64,128]{2,1,0:T(8,128)(2,1)S(1)}, bf16[64,64,128]{2,1,0:T(8,128)(2,1)}, u32[]{:S(2)}, u32[]{:S(2)}) collective-permute-start(bf16[64,64,128]{2,1,0:T(8,128)(2,1)S(1)} %slice.4), channel_id=1, source_target_pairs={{0,16},{16,0},{32,48},{48,32},{64,80},{80,64},{96,112},{112,96},{1... | collective-permute-start | bytes 3145736 | tf_op jit(solution)/shard_map/ppermute | solution.py:461

commit v4 on v2

--- a/solution.py
+++ b/solution.py
@@ -54,9 +54,9 @@
     mids = up_mid.shape[0]
     parts = 4
     part = out.shape[0] // parts
-    fetch_src = pltpu.make_async_copy(src_in, src, sems.at[0])
-    fetch_leaf = pltpu.make_async_copy(up_leaf_in, up_leaf, sems.at[1])
-    fetch_mid = pltpu.make_async_copy(up_mid_in, up_mid, sems.at[2])
+    fetch_src = pltpu.make_async_copy(src_in, src, sems.at[4])
+    fetch_leaf = pltpu.make_async_copy(up_leaf_in, up_leaf, sems.at[5])
+    fetch_mid = pltpu.make_async_copy(up_mid_in, up_mid, sems.at[6])
     fetch_slots = pltpu.make_async_copy(slots_in, slots, sems.at[7])
     fetch_slots.start()
     fetch_src.start()
@@ -91,13 +91,17 @@
 
             lax.fori_loop(0, part // 2, pack_rest, 0, unroll=16)
         place = pl.ds(n * part, part)
-        sends.append(pltpu.make_async_copy(message.at[place], out.at[place], sems.at[3 + n]))
+        sends.append(pltpu.make_async_copy(message.at[place], out.at[place], sems.at[n]))
         sends[n].start()
     wait_all(sends)
 
 
 def device_of(i, core):
     return (i >> 4) * 32 + core * 16 + (i & 15)
+
+
+def place_of(p):
+    return (p >> 5) * 16 + (p & 15)
 
 
 def top_kernel(top_list, adj, up_leaf, up_mid, couple_top, outgoing, mid_adj, own, other, total):
@@ -112,7 +116,7 @@
         for j in range(4):
             p = top_list[0, k + j]
             place = ((p >> 4) & 1) ^ core
-            total[place, (p >> 5) * 16 + (p & 15)] += fold(terms[:, j * rank : (j + 1) * rank])
+            total[place, place_of(p)] += fold(terms[:, j * rank : (j + 1) * rank])
     own[...] = total[0]
     other[...] = total[1].astype(BF16)
 
@@ -136,17 +140,22 @@
     couple_mid_in,
     out,
     other,
+    leaf_pairs_out,
+    mid_pairs_out,
     leaf_list,
     mid_list,
     adj,
     mid_adj,
     couple_leaf,
     couple_mid,
+    leaf_pairs,
+    mid_pairs,
     message,
     even,
     odd,
     sems,
     leaf_sems,
+    pair_sems,
     out_sems,
 ):
     width, rank = couple_leaf.shape[1:3]
@@ -160,6 +169,10 @@
         place = pl.ds(pl.multiple_of(step * chunk, chunk), chunk)
         return pltpu.make_async_copy(couple_leaf_in.at[place], couple_leaf.at[place], leaf_sems.at[step])
 
+    def keep_pairs(step):
+        place = pl.ds(pl.multiple_of(step * chunk, chunk), chunk)
+        return pltpu.make_async_copy(leaf_pairs.at[place], leaf_pairs_out.at[place], pair_sems.at[step])
+
     fetches = [
         pltpu.make_async_copy(leaf_list_in, leaf_list, sems.at[0]),
         pltpu.make_async_copy(mid_list_in, mid_list, sems.at[1]),
@@ -167,6 +180,7 @@
         pltpu.make_async_copy(mid_adj_in, mid_adj, sems.at[3]),
     ]
     fetch_mid = pltpu.make_async_copy(couple_mid_in, couple_mid, sems.at[4])
+    keep_mid = pltpu.make_async_copy(mid_pairs, mid_pairs_out, sems.at[5])
     start_all(fetches)
     for step in range(steps):
         fetch(step).start()
@@ -180,10 +194,12 @@
     lax.fori_loop(0, even.shape[0], clear, 0, unroll=8)
     wait_all(fetches)
 
-    def scatter(row, blocks, slot):
+    def scatter(row, blocks, slot, keep):
         for k in range(0, width, 4):
-            terms = mul(row, side(*[blocks(k + j) for j in range(4)]))
+            pairs = [side(blocks(k), blocks(k + 1)), side(blocks(k + 2), blocks(k + 3))]
+            terms = mul(row, side(*pairs))
             for j in range(2):
+                keep(k // 2 + j, pairs[j])
                 pair = terms[:, 2 * j * rank : 2 * (j + 1) * rank]
                 crossed = pltpu.roll(pair[half:], rank, 1)
                 e, o = slot(k + 2 * j), slot(k + 2 * j + 1)
@@ -196,13 +212,23 @@
         fetch(step).wait()
         for a in range(chunk):
             g = step * chunk + a
-            scatter(adj[g], lambda k: couple_leaf[g, k], lambda k: leaf_list[k, g])
+
+            def keep(k, pair):
+                leaf_pairs[g, k] = pair
+
+            scatter(adj[g], lambda k: couple_leaf[g, k], lambda k: leaf_list[k, g], keep)
+        keep_pairs(step).start()
         return carry
 
     lax.fori_loop(0, steps, leaf_step, 0)
     fetch_mid.wait()
     for c in range(mid_adj.shape[0]):
-        scatter(mid_adj[c], lambda k: couple_mid[c, k], lambda k: mid_list[c, k])
+
+        def keep(k, pair):
+            mid_pairs[c, k] = pair
+
+        scatter(mid_adj[c], lambda k: couple_mid[c, k], lambda k: mid_list[c, k], keep)
+    keep_mid.start()
 
     core = lax.axis_index("grp") & 1
     sends = []
@@ -225,13 +251,16 @@
             )
             copy.start()
             sends.append(copy)
+    for step in range(steps):
+        keep_pairs(step).wait()
+    keep_mid.wait()
     wait_all(sends)
 
 
-def gather(blocks, partner):
+def gather(pairs, partner):
     near = 0
     for k in range(0, 16, 4):
-        near += mul_t(side(*[partner(k + j) for j in range(4)]), side(*[blocks(k + j) for j in range(4)]))
+        near += mul_t(side(*[partner(k + j) for j in range(4)]), side(pairs(k // 2), pairs(k // 2 + 1)))
     return near
 
 
@@ -239,15 +268,15 @@
     leaf_list_in,
     mid_list_in,
     arrived_in,
-    couple_leaf_in,
-    couple_mid_in,
+    leaf_pairs_in,
+    mid_pairs_in,
     leaf_near_out,
     mid_near_out,
     leaf_list,
     mid_list,
     arrived,
-    couple_leaf,
-    couple_mid,
+    leaf_pairs,
+    mid_pairs,
     leaf_near,
     mid_near,
     coeff,
@@ -266,7 +295,7 @@
         return pl.ds(pl.multiple_of(step * chunk, chunk), chunk)
 
     def fetch(step):
-        return pltpu.make_async_copy(couple_leaf_in.at[place(step)], couple_leaf.at[place(step)], leaf_sems.at[step])
+        return pltpu.make_async_copy(leaf_pairs_in.at[place(step)], leaf_pairs.at[place(step)], leaf_sems.at[step])
 
     def keep(step):
         return pltpu.make_async_copy(leaf_near.at[place(step)], leaf_near_out.at[place(step)], near_sems.at[step])
@@ -279,7 +308,7 @@
     for n in range(parts):
         rows_n = pl.ds(n * part, part)
         messages.append(pltpu.make_async_copy(arrived_in.at[rows_n], arrived.at[rows_n], arrived_sems.at[n]))
-    fetch_mid = pltpu.make_async_copy(couple_mid_in, couple_mid, sems.at[2])
+    fetch_mid = pltpu.make_async_copy(mid_pairs_in, mid_pairs, sems.at[2])
     keep_mid = pltpu.make_async_copy(mid_near, mid_near_out, sems.at[3])
     start_all(messages)
     start_all(lists)
@@ -303,14 +332,14 @@
         fetch(step).wait()
         for a in range(chunk):
             g = step * chunk + a
-            leaf_near[g] = gather(lambda k: couple_leaf[g, k], lambda k: coeff[leaf_list[k, g]])
+            leaf_near[g] = gather(lambda k: leaf_pairs[g, k], lambda k: coeff[leaf_list[k, g]])
         keep(step).start()
         return carry
 
     lax.fori_loop(0, steps, leaf_step, 0)
     fetch_mid.wait()
     for c in range(mid_near.shape[0]):
-        mid_near[c] = gather(lambda k: couple_mid[c, k], lambda k: coeff[mid_list[c, k]])
+        mid_near[c] = gather(lambda k: mid_pairs[c, k], lambda k: coeff[mid_list[c, k]])
     keep_mid.start()
     for step in range(steps):
         keep(step).wait()
@@ -328,7 +357,7 @@
         j = top_list[0, k]
         return jnp.concatenate([unfold(own_half[j]), unfold(other_half[j])], axis=0)
 
-    near = gather(lambda k: couple_top[0, k], partner)
+    near = gather(lambda k: side(couple_top[0, 2 * k], couple_top[0, 2 * k + 1]), partner)
     swapped = jnp.concatenate([near[nf // 2 :], near[: nf // 2]], axis=0)
     core = lax.axis_index("grp") % 2
     down_mid[...] = turn(up_mid, 0, eye)
@@ -341,37 +370,9 @@
             forward[8 * c + i] = (leaf_near[8 * c + i] + below[i]).astype(BF16)
 
 
-def lower_kernel(
-    slots_in,
-    returned_in,
-    down_leaf_in,
-    down_mid_in,
-    out,
-    slots,
-    returned,
-    down_leaf,
-    down_mid,
-    adjoint,
-    even,
-    odd,
-    even_mid,
-    odd_mid,
-    sems,
-):
+def lower_kernel(slots, returned, down_leaf, down_mid, out, adjoint, even, odd, even_mid, odd_mid, sems):
     leaves, nf, rank = adjoint.shape
     mids = down_leaf.shape[0]
-    part = returned.shape[0] // 4
-    fetches = []
-    for n in range(4):
-        place = pl.ds(n * part, part)
-        fetches.append(pltpu.make_async_copy(returned_in.at[place], returned.at[place], sems.at[n]))
-    fetch_leaf = pltpu.make_async_copy(down_leaf_in, down_leaf, sems.at[4])
-    fetch_mid = pltpu.make_async_copy(down_mid_in, down_mid, sems.at[5])
-    fetch_slots = pltpu.make_async_copy(slots_in, slots, sems.at[14])
-    fetch_slots.start()
-    start_all(fetches)
-    fetch_mid.start()
-    fetch_leaf.start()
     for far in (even, odd, even_mid, odd_mid):
         far[...] = jnp.zeros(far.shape, F32)
     half = nf // 2
@@ -389,15 +390,9 @@
             held[u] = value
         return top + returned[i, 6 * half :].astype(F32)
 
-    fetch_slots.wait()
-    top = jnp.zeros((half, 2 * rank), F32)
-    for n in range(4):
-        fetches[n].wait()
-        top = lax.fori_loop(n * part, (n + 1) * part, collect, top, unroll=8)
+    top = lax.fori_loop(0, returned.shape[0], collect, jnp.zeros((half, 2 * rank), F32), unroll=8)
     fars = [unfold(even_mid[c] + odd_mid[c]) for c in range(mids)]
-    fetch_mid.wait()
     below_top = lower(unfold(top).astype(BF16), down_mid[...])
-    fetch_leaf.wait()
     sends = []
     for c in range(mids):
         below = lower((fars[c] + below_top[c]).astype(BF16), down_leaf[c])
@@ -405,7 +400,7 @@
             a = c * 8 + i
             adjoint[a] = (unfold(even[a] + odd[a]) + below[i]).astype(BF16)
         place = pl.ds(8 * c, 8)
-        sends.append(pltpu.make_async_copy(adjoint.at[place], out.at[place], sems.at[6 + c]))
+        sends.append(pltpu.make_async_copy(adjoint.at[place], out.at[place], sems.at[c]))
         sends[c].start()
     wait_all(sends)
 
@@ -452,6 +447,7 @@
     top_shape = (chips, nf // 2, 2 * rank)
     shape = jax.ShapeDtypeStruct
     params = pltpu.CompilerParams(vmem_limit_bytes=66000000)
+    roomy = pltpu.CompilerParams(vmem_limit_bytes=64000000)
     small = pl.CostEstimate(flops=10**6, bytes_accessed=10**5, transcendentals=0)
 
     outgoing = pl.pallas_call(
@@ -485,11 +481,18 @@
         name="top",
     )(top_list, adj, up_leaf, up_mid, couple_top, outgoing)
     swapped_terms = swap(other_terms)
-    per_slot, for_other = pl.pallas_call(
+    leaf_pairs_shape = (leaves, width // 2, rank, 2 * rank)
+    mid_pairs_shape = (mids, width // 2, rank, 2 * rank)
+    per_slot, for_other, leaf_pairs, mid_pairs = pl.pallas_call(
         adjoint_kernel,
-        out_shape=(shape(second_message, BF16), shape(swapped_message, BF16)),
+        out_shape=(
+            shape(second_message, BF16),
+            shape(swapped_message, BF16),
+            shape(leaf_pairs_shape, BF16),
+            shape(mid_pairs_shape, BF16),
+        ),
         in_specs=[HBM] * 6,
-        out_specs=(HBM, HBM),
+        out_specs=(HBM, HBM, HBM, HBM),
         scratch_shapes=[
             pltpu.SMEM(leaf_slots.shape, jnp.int32),
             pltpu.SMEM(mid_list.shape, jnp.int32),
@@ -497,10 +500,13 @@
             pltpu.VMEM(mid_adj.shape, BF16),
             pltpu.VMEM(couple_leaf.shape, BF16),
             pltpu.VMEM(couple_mid.shape, BF16),
+            pltpu.VMEM(leaf_pairs_shape, BF16),
+            pltpu.VMEM(mid_pairs_shape, BF16),
             pltpu.VMEM((2,) + swapped_message, BF16),
             pltpu.VMEM((3 * peers, nf // 2, 2 * rank), F32),
             pltpu.VMEM((3 * peers, nf // 2, 2 * rank), F32),
-            pltpu.SemaphoreType.DMA((5,)),
+            pltpu.SemaphoreType.DMA((6,)),
+            pltpu.SemaphoreType.DMA((steps,)),
             pltpu.SemaphoreType.DMA((steps,)),
             pltpu.SemaphoreType.DMA((4,)),
         ],
@@ -527,8 +533,8 @@
             pltpu.SMEM(leaf_slots.shape, jnp.int32),
             pltpu.SMEM(mid_list.shape, jnp.int32),
             pltpu.VMEM(message, BF16),
-            pltpu.VMEM(couple_leaf.shape, BF16),
-            pltpu.VMEM(couple_mid.shape, BF16),
+            pltpu.VMEM(leaf_pairs_shape, BF16),
+            pltpu.VMEM(mid_pairs_shape, BF16),
             pltpu.VMEM((leaves, nf, rank), F32),
             pltpu.VMEM((mids, nf, rank), F32),
             pltpu.VMEM((3 * peers, nf, rank), BF16),
@@ -537,10 +543,10 @@
             pltpu.SemaphoreType.DMA((steps,)),
             pltpu.SemaphoreType.DMA((steps,)),
         ],
-        compiler_params=params,
+        compiler_params=roomy,
         cost_estimate=small,
         name="forward",
-    )(leaf_slots, mid_list, arrived, couple_leaf, couple_mid)
+    )(leaf_slots, mid_list, arrived, leaf_pairs, mid_pairs)
     forward, down_leaf, down_mid = pl.pallas_call(
         finish_kernel,
         out_shape=(
@@ -550,7 +556,7 @@
         ),
         in_specs=[SMEM] + [VMEM] * 7,
         out_specs=(VMEM, VMEM, VMEM),
-        compiler_params=params,
+        compiler_params=roomy,
         cost_estimate=small,
         name="finish",
     )(top_list, own_half, other_half, leaf_near, mid_near, up_leaf, up_mid, couple_top)
@@ -558,21 +564,17 @@
     adjoint = pl.pallas_call(
         lower_kernel,
         out_shape=shape((leaves, nf, rank), BF16),
-        in_specs=[HBM] * 4,
+        in_specs=[SMEM, VMEM, VMEM, VMEM],
         out_specs=HBM,
         scratch_shapes=[
-            pltpu.SMEM(slots.shape, jnp.int32),
-            pltpu.VMEM(second_message, BF16),
-            pltpu.VMEM((mids, rank, 8 * rank), BF16),
-            pltpu.VMEM((rank, 8 * rank), BF16),
             pltpu.VMEM((leaves, nf, rank), BF16),
             pltpu.VMEM((leaves, nf // 2, 2 * rank), F32),
             pltpu.VMEM((leaves, nf // 2, 2 * rank), F32),
             pltpu.VMEM((mids, nf // 2, 2 * rank), F32),
             pltpu.VMEM((mids, nf // 2, 2 * rank), F32),
-            pltpu.SemaphoreType.DMA((15,)),
+            pltpu.SemaphoreType.DMA((mids,)),
         ],
-        compiler_params=params,
+        compiler_params=pltpu.CompilerParams(vmem_limit_bytes=40000000),
         name="lower",
     )(slots, returned, down_leaf, down_mid)
     return jnp.swapaxes(forward, 1, 2), jnp.swapaxes(adjoint, 1, 2)

time: 78.5 us -> 79.7 us (1.015)
  Pallas kernels: 40.8 us -> 36.9 us
  waiting for transfers between devices: 15.3 us -> 19.1 us
  local copies, waits for them, and re-layouts: 2.74 us -> 4.71 us
  starting transfers between devices: 17.8 us -> 17 us
    all_to_all x1, waiting for transfers between devices: 7.7 us -> 11.6 us  [on_device(): lax.all_to_all(per_slot, ('grp', 'dev'), split_axis=0, concat_axis=0, axi...]
    pallas_call x1, Pallas kernels: 12.4 us -> 9.08 us  [on_device(): pl.pallas_call(forward_kernel, out_shape=(shape((leaves, nf, rank), F32),...]
    unnamed x8 -> x14, local copies, waits for them, and re-layouts: 0.73 us -> 2.59 us
  transfers between devices with their start and end apart: 5 -> 5, of which waited for: 3 -> 3; matrix products, arithmetic and copies ran while one was open for 4% -> 4% of each run, Pallas kernels for 43% -> 38%
where the time goes in v4:
time: 79.7 us; the launch traced here: 79.2 us
  Pallas kernels  36.9 us (46%)
  waiting for transfers between devices  19.1 us (24%)
  starting transfers between devices  17 us (21%)
  local copies, waits for them, and re-layouts  4.71 us (6%)
  other arithmetic  0.8 us (1%)
    pallas_call x1, Pallas kernels, on_device(): pl.pallas_call(adjoint_kernel, out_shape=(shape(second_message, BF16), sh...  13.5 us
    all_to_all x1, starting transfers between devices, exchange(): lax.all_to_all(x, ('grp', 'dev'), split_axis=0, concat_axis=0, tiled=True)  11.6 us
    all_to_all x1, waiting for transfers between devices, on_device(): lax.all_to_all(per_slot, ('grp', 'dev'), split_axis=0, concat_axis=0, axi...  11.6 us
    pallas_call x1, Pallas kernels, on_device(): pl.pallas_call(forward_kernel, out_shape=(shape((leaves, nf, rank), F32),...  9.08 us
    all_to_all x1, waiting for transfers between devices, exchange(): lax.all_to_all(x, ('grp', 'dev'), split_axis=0, concat_axis=0, tiled=True)  5.4 us
    all_to_all x1, starting transfers between devices, on_device(): lax.all_to_all(per_slot, ('grp', 'dev'), split_axis=0, concat_axis=0, axi...  4.73 us
    pallas_call x1, Pallas kernels, on_device(): pl.pallas_call(finish_kernel, out_shape=(shape((leaves, nf, rank), BF16),...  4.62 us
    pallas_call x1, Pallas kernels, on_device(): pl.pallas_call(lift_kernel, out_shape=shape(message, BF16), in_specs=[HBM...  3.81 us
  transfers between devices with their start and end apart: 5, of which 3 were waited for; matrix products, arithmetic and copies ran while one was open for 4% of the time, Pallas kernels for 38%

profile of v4, /device:TPU:0, one launch (start us, length us, event | category | flops | bytes accessed | tf_op | source)
XLA Modules:
  0.0 79.2 jit_solution(441166112963446143)
XLA Ops:
  0.6 3.8 %lift.1.outgoing = bf16[128,56,128]{2,1,0:T(8,128)(2,1)} custom-call(s32[3,1,128]{2,1,0:T(1,128)} %bitcast.6, bf16[64,32,64]{2,1,0:T(8,128)(2,1)} %bitcast.10, bf16[64,64,64]{2,1,0:T(8,128)(2,1)} %up_leaf.3, bf16[8,64,64]{2,1,0:T(8,128)(2,1)} %up_mid.3), custom_call_target="tpu_custom_call" | custom-call | tf_op jit(solution)/shard_map/lift/pallas_call | solution.py:453
  4.4 11.6 %all-to-all-start = ((bf16[128,56,128]{2,1,0:T(8,128)(2,1)}), bf16[128,56,128]{2,1,0:T(8,128)(2,1)}, u32[]{:S(2)}, u32[]{:S(2)}) async-start(bf16[128,56,128]{2,1,0:T(8,128)(2,1)} %lift.1.outgoing), calls=%async_computation | async-start | bytes 3670016 | tf_op jit(solution)/shard_map/all_to_all | solution.py:414
  16.1 3.2 %top.1 = (bf16[8,32,64]{2,1,0:T(8,128)(2,1)}, f32[64,16,128]{2,1,0:T(8,128)}, bf16[64,16,128]{2,1,0:T(8,128)(2,1)}) custom-call(s32[1,16]{1,0:T(1,128)} %top_list.3, bf16[64,32,64]{2,1,0:T(8,128)(2,1)} %bitcast.8, bf16[64,64,64]{2,1,0:T(8,128)(2,1)} %up_leaf.3, bf16[8,64,64]{2,1,0:T(8,128)(2,1)} %up_mid.3, bf16[1,16,64,64]{3,2,1,0:T(8,128)(2,1)} %couple_top.3, ...), custom_call_target="tpu_custom_call" | custom-call | flops 1000000 | bytes 100000 | tf_op jit(solution)/shard_map/top/pallas_call | solution.py:473
  19.2 0.0 copy-start.6
  19.2 13.5 %adjoint.1 = (bf16[64,112,128]{2,1,0:T(8,128)(2,1)}, bf16[64,48,128]{2,1,0:T(8,128)(2,1)}, bf16[64,8,64,128]{3,2,1,0:T(8,128)(2,1)}, bf16[8,8,64,128]{3,2,1,0:T(8,128)(2,1)}) custom-call(s32[16,64]{1,0:T(8,128)} %bitcast.12, s32[8,16]{1,0:T(8,128)} %mid_list_in.3, bf16[64,32,64]{2,1,0:T(8,128)(2,1)} %bitcast.9, ...), custom_call_target="tpu_custom_call" | custom-call | flops 1000000 | bytes 100000 | tf_op jit(solution)/shard_map/adjoint/pallas_call | solution.py:486
  32.7 0.0 copy-start.4
  32.8 0.1 collective-permute-start.1
  32.9 0.0 copy-done.6
  32.9 0.5 collective-permute-start.2
  33.4 2.1 %collective-permute-done.1 = bf16[64,48,128]{2,1,0:T(8,128)(2,1)S(1)} collective-permute-done((bf16[64,48,128]{2,1,0:T(8,128)(2,1)}, bf16[64,48,128]{2,1,0:T(8,128)(2,1)S(1)}, u32[]{:S(2)}, u32[]{:S(2)}) %collective-permute-start.1) | collective-permute-done | bytes 786464 | tf_op jit(solution)/shard_map/ppermute | solution.py:418
  35.4 1.1 %constant_dynamic-update-slice_fusion = bf16[64,112,128]{2,1,0:T(8,128)(2,1)} fusion(bf16[64,112,128]{2,1,0:T(8,128)(2,1)} %get-tuple-element.20, bf16[64,48,128]{2,1,0:T(8,128)(2,1)S(1)} %collective-permute-done.1), kind=kLoop, calls=%fused_computation.2 | loop fusion | bytes 1572864 | tf_op jit(solution)/shard_map/dynamic_update_slice | solution.py:518
  36.6 0.0 collective-permute-done.2
  36.6 0.0 copy-done.4
  36.6 0.8 %fusion = bf16[64,112,128]{2,1,0:T(8,128)(2,1)} fusion(bf16[64,112,128]{2,1,0:T(8,128)(2,1)} %constant_dynamic-update-slice_fusion, f32[64,16,128]{2,1,0:T(8,128)S(1)} %copy-done.4, bf16[64,16,128]{2,1,0:T(8,128)(2,1)S(1)} %collective-permute-done.2), kind=kLoop, calls=%fused_computation.1 | loop fusion | flops 393216 | bytes 1048576 | tf_op jit(solution)/shard_map/dynamic_update_slice | solution.py:519
  37.4 5.4 %all-to-all-done.arrived_in = bf16[128,56,128]{2,1,0:T(8,128)(2,1)} async-done(((bf16[128,56,128]{2,1,0:T(8,128)(2,1)}), bf16[128,56,128]{2,1,0:T(8,128)(2,1)}, u32[]{:S(2)}, u32[]{:S(2)}) %all-to-all-start) | async-done | bytes 1835040 | tf_op jit(solution)/shard_map/all_to_all | solution.py:414
  42.8 4.7 %all-to-all-start.1 = ((bf16[64,112,128]{2,1,0:T(8,128)(2,1)}), bf16[64,112,128]{2,1,0:T(8,128)(2,1)S(1)}, u32[]{:S(2)}, u32[]{:S(2)}) async-start(bf16[64,112,128]{2,1,0:T(8,128)(2,1)} %fusion), calls=%async_computation.1 | async-start | bytes 3670016 | tf_op jit(solution)/shard_map/all_to_all | solution.py:521
  47.5 1.0 %slice.4.own_half = bf16[128,8,128]{2,1,0:T(8,128)(2,1)S(1)} slice(bf16[128,56,128]{2,1,0:T(8,128)(2,1)} %all-to-all-done.arrived_in), slice={[0:128], [48:56], [0:128]} | slice | bytes 524288 | tf_op jit(solution)/shard_map/slice | solution.py:525
  48.5 0.0 copy-start.3
  48.5 0.1 collective-permute-start
  48.6 9.1 %forward.1 = (f32[64,32,64]{2,1,0:T(8,128)}, f32[8,32,64]{2,1,0:T(8,128)}) custom-call(s32[16,64]{1,0:T(8,128)} %bitcast.13, s32[8,16]{1,0:T(8,128)} %mid_list_in.3, bf16[128,56,128]{2,1,0:T(8,128)(2,1)} %all-to-all-done.arrived_in, bf16[64,8,64,128]{3,2,1,0:T(8,128)(2,1)} %get-tuple-element.15.leaf_pairs_in, ...), custom_call_target="tpu_custom_call" | custom-call | flops 1000000 | bytes 100000 | tf_op jit(solution)/shard_map/forward/pallas_call | solution.py:527
  57.7 0.0 copy-done.3
  57.7 0.0 copy-start.2
  57.7 0.0 collective-permute-done.other_half
  57.7 0.0 copy-start.5
  57.7 0.7 copy-done.5
  58.4 4.6 %finish.1 = (bf16[64,32,64]{2,1,0:T(8,128)(2,1)}, bf16[8,64,512]{2,1,0:T(8,128)(2,1)}, bf16[64,512]{1,0:T(8,128)(2,1)}) custom-call(s32[1,16]{1,0:T(1,128)} %top_list.3, bf16[128,8,128]{2,1,0:T(8,128)(2,1)} %copy-done.3, bf16[128,8,128]{2,1,0:T(8,128)(2,1)} %copy-done.5, f32[64,32,64]{2,1,0:T(8,128)} %get-tuple-element.17.leaf_near, ...), custom_call_target="tpu_custom_call" | custom-call | flops 1000000 | bytes 100000 | tf_op jit(solution)/shard_map/finish/pallas_call | solution.py:550
  63.0 11.6 %all-to-all-done.1.returned = bf16[64,112,128]{2,1,0:T(8,128)(2,1)S(1)} async-done(((bf16[64,112,128]{2,1,0:T(8,128)(2,1)}), bf16[64,112,128]{2,1,0:T(8,128)(2,1)S(1)}, u32[]{:S(2)}, u32[]{:S(2)}) %all-to-all-start.1) | async-done | bytes 1835040 | tf_op jit(solution)/shard_map/all_to_all | solution.py:521
  74.6 0.0 copy-done.2
  74.6 0.0 copy-start
  74.6 1.0 %copy-done = bf16[8,64,512]{2,1,0:T(8,128)(2,1)S(1)} copy-done((bf16[8,64,512]{2,1,0:T(8,128)(2,1)S(1)}, bf16[8,64,512]{2,1,0:T(8,128)(2,1)}, u32[]{:S(2)}) %copy-start) | copy-done | bytes 524312
  75.7 0.8 %copy-done.1 = bf16[64,512]{1,0:T(8,128)(2,1)S(1)} copy-done((bf16[64,512]{1,0:T(8,128)(2,1)S(1)}, bf16[64,512]{1,0:T(8,128)(2,1)}, u32[]{:S(2)}) %copy-start.1) | copy-done | bytes 65560
  76.5 2.7 %lower.1 = bf16[64,32,64]{2,1,0:T(8,128)(2,1)} custom-call(s32[3,1,128]{2,1,0:T(1,128)S(1)} %bitcast.7, bf16[64,112,128]{2,1,0:T(8,128)(2,1)S(1)} %all-to-all-done.1.returned, bf16[8,64,512]{2,1,0:T(8,128)(2,1)S(1)} %copy-done, bf16[64,512]{1,0:T(8,128)(2,1)S(1)} %copy-done.1), custom_call_target="tpu_custom_call" | custom-call | tf_op jit(solution)/shard_map/lower/pallas_call | solution.py:564
  (1 shorter events, 0.0 us)
Async XLA Ops:
  4.4 38.3 %all-to-all-start = ((bf16[128,56,128]{2,1,0:T(8,128)(2,1)}), bf16[128,56,128]{2,1,0:T(8,128)(2,1)}, u32[]{:S(2)}, u32[]{:S(2)}) async-start(bf16[128,56,128]{2,1,0:T(8,128)(2,1)} %lift.1.outgoing), calls=%async_computation | async-start | bytes 3670016 | tf_op jit(solution)/shard_map/all_to_all | solution.py:414
  19.2 13.6 %copy-start.6 = (bf16[64,16,128]{2,1,0:T(8,128)(2,1)S(1)}, bf16[64,16,128]{2,1,0:T(8,128)(2,1)}, u32[]{:S(2)}) copy-start(bf16[64,16,128]{2,1,0:T(8,128)(2,1)} %get-tuple-element.23) | copy-start | bytes 786436
  32.7 3.8 %copy-start.4 = (f32[64,16,128]{2,1,0:T(8,128)S(1)}, f32[64,16,128]{2,1,0:T(8,128)}, u32[]{:S(2)}) copy-start(f32[64,16,128]{2,1,0:T(8,128)} %get-tuple-element.22) | copy-start | bytes 1572868
  32.8 2.7 %collective-permute-start.1 = (bf16[64,48,128]{2,1,0:T(8,128)(2,1)}, bf16[64,48,128]{2,1,0:T(8,128)(2,1)S(1)}, u32[]{:S(2)}, u32[]{:S(2)}) collective-permute-start(bf16[64,48,128]{2,1,0:T(8,128)(2,1)} %get-tuple-element.21), channel_id=1, source_target_pairs={{0,16},{16,0},{32,48},{48,32},{64,80},{80,64},{96,112},{112,96},{1... | collective-permute-start | bytes 2359304 | tf_op jit(solution)/shard_map/ppermute | solution.py:418
  32.9 3.7 %collective-permute-start.2 = (bf16[64,16,128]{2,1,0:T(8,128)(2,1)S(1)}, bf16[64,16,128]{2,1,0:T(8,128)(2,1)S(1)}, u32[]{:S(2)}, u32[]{:S(2)}) collective-permute-start(bf16[64,16,128]{2,1,0:T(8,128)(2,1)S(1)} %copy-done.6), channel_id=1, source_target_pairs={{0,16},{16,0},{32,48},{48,32},{64,80},{80,64},{96,112},{112,96},{1... | collective-permute-start | bytes 786440 | tf_op jit(solution)/shard_map/ppermute | solution.py:418
  42.8 31.9 %all-to-all-start.1 = ((bf16[64,112,128]{2,1,0:T(8,128)(2,1)}), bf16[64,112,128]{2,1,0:T(8,128)(2,1)S(1)}, u32[]{:S(2)}, u32[]{:S(2)}) async-start(bf16[64,112,128]{2,1,0:T(8,128)(2,1)} %fusion), calls=%async_computation.1 | async-start | bytes 3670016 | tf_op jit(solution)/shard_map/all_to_all | solution.py:521
  48.5 9.2 %copy-start.3 = (bf16[128,8,128]{2,1,0:T(8,128)(2,1)}, bf16[128,8,128]{2,1,0:T(8,128)(2,1)S(1)}, u32[]{:S(2)}) copy-start(bf16[128,8,128]{2,1,0:T(8,128)(2,1)S(1)} %slice.4.own_half) | copy-start | bytes 786436
  48.5 9.2 %collective-permute-start = (bf16[128,8,128]{2,1,0:T(8,128)(2,1)S(1)}, bf16[128,8,128]{2,1,0:T(8,128)(2,1)S(1)}, u32[]{:S(2)}, u32[]{:S(2)}) collective-permute-start(bf16[128,8,128]{2,1,0:T(8,128)(2,1)S(1)} %slice.4.own_half), channel_id=1, source_target_pairs={{0,16},{16,0},{32,48},{48,32},{64,80},{80,64},{96,112},{112,96},{1... | collective-permute-start | bytes 786440 | tf_op jit(solution)/shard_map/ppermute | solution.py:418
  57.7 16.9 %copy-start.2 = (s32[1,128,3]{1,0,2:T(1,128)S(1)}, s32[1,128,3]{1,0,2:T(1,128)}, u32[]{:S(2)}) copy-start(s32[1,128,3]{1,0,2:T(1,128)} %param.18) | copy-start | bytes 4612
  57.7 0.7 copy-start.5
  74.6 1.0 %copy-start = (bf16[8,64,512]{2,1,0:T(8,128)(2,1)S(1)}, bf16[8,64,512]{2,1,0:T(8,128)(2,1)}, u32[]{:S(2)}) copy-start(bf16[8,64,512]{2,1,0:T(8,128)(2,1)} %get-tuple-element.24.down_leaf) | copy-start | bytes 1572868
  75.7 0.8 %copy-start.1 = (bf16[64,512]{1,0:T(8,128)(2,1)S(1)}, bf16[64,512]{1,0:T(8,128)(2,1)}, u32[]{:S(2)}) copy-start(bf16[64,512]{1,0:T(8,128)(2,1)} %get-tuple-element.25.down_mid) | copy-start | bytes 196612

commit v5 on v4

--- a/solution.py
+++ b/solution.py
@@ -347,7 +347,7 @@
 
 
 def finish_kernel(
-    top_list, own_half, other_half, leaf_near, mid_near, up_leaf, up_mid, couple_top, forward, down_leaf, down_mid
+    top_list, own_half, other_half, leaf_near, mid_near, up_leaf, up_mid, couple_top, forward, down_all
 ):
     nf, rank = forward.shape[1:]
     shape = (rank, rank)
@@ -360,19 +360,24 @@
     near = gather(lambda k: side(couple_top[0, 2 * k], couple_top[0, 2 * k + 1]), partner)
     swapped = jnp.concatenate([near[nf // 2 :], near[: nf // 2]], axis=0)
     core = lax.axis_index("grp") % 2
-    down_mid[...] = turn(up_mid, 0, eye)
-    below_top = lower(jnp.where(core == 0, near, swapped).astype(BF16), down_mid[...])
-    for c in range(mid_near.shape[0]):
+    mids = mid_near.shape[0]
+    down_all[mids] = turn(up_mid, 0, eye)
+    below_top = lower(jnp.where(core == 0, near, swapped).astype(BF16), down_all[mids])
+    for c in range(mids):
         down = turn(up_leaf, c, eye)
-        down_leaf[c] = down
+        down_all[c] = down
         below = lower((mid_near[c] + below_top[c]).astype(BF16), down)
         for i in range(8):
             forward[8 * c + i] = (leaf_near[8 * c + i] + below[i]).astype(BF16)
 
 
-def lower_kernel(slots, returned, down_leaf, down_mid, out, adjoint, even, odd, even_mid, odd_mid, sems):
+def lower_kernel(
+    slots, returned, down_all_in, out, down_all, adjoint, even, odd, even_mid, odd_mid, sems
+):
     leaves, nf, rank = adjoint.shape
-    mids = down_leaf.shape[0]
+    mids = even_mid.shape[0]
+    fetch = pltpu.make_async_copy(down_all_in, down_all, sems.at[mids])
+    fetch.start()
     for far in (even, odd, even_mid, odd_mid):
         far[...] = jnp.zeros(far.shape, F32)
     half = nf // 2
@@ -392,10 +397,11 @@
 
     top = lax.fori_loop(0, returned.shape[0], collect, jnp.zeros((half, 2 * rank), F32), unroll=8)
     fars = [unfold(even_mid[c] + odd_mid[c]) for c in range(mids)]
-    below_top = lower(unfold(top).astype(BF16), down_mid[...])
+    fetch.wait()
+    below_top = lower(unfold(top).astype(BF16), down_all[mids])
     sends = []
     for c in range(mids):
-        below = lower((fars[c] + below_top[c]).astype(BF16), down_leaf[c])
+        below = lower((fars[c] + below_top[c]).astype(BF16), down_all[c])
         for i in range(8):
             a = c * 8 + i
             adjoint[a] = (unfold(even[a] + odd[a]) + below[i]).astype(BF16)
@@ -547,16 +553,16 @@
         cost_estimate=small,
         name="forward",
     )(leaf_slots, mid_list, arrived, leaf_pairs, mid_pairs)
-    forward, down_leaf, down_mid = pl.pallas_call(
+    down_shape = (mids + 1, rank, 8 * rank)
+    forward, down_all = pl.pallas_call(
         finish_kernel,
         out_shape=(
             shape((leaves, nf, rank), BF16),
-            shape((mids, rank, 8 * rank), BF16),
-            shape((rank, 8 * rank), BF16),
+            shape(down_shape, BF16),
         ),
         in_specs=[SMEM] + [VMEM] * 7,
-        out_specs=(VMEM, VMEM, VMEM),
-        compiler_params=roomy,
+        out_specs=(VMEM, VMEM),
+        compiler_params=pltpu.CompilerParams(vmem_limit_bytes=40000000),
         cost_estimate=small,
         name="finish",
     )(top_list, own_half, other_half, leaf_near, mid_near, up_leaf, up_mid, couple_top)
@@ -564,19 +570,20 @@
     adjoint = pl.pallas_call(
         lower_kernel,
         out_shape=shape((leaves, nf, rank), BF16),
-        in_specs=[SMEM, VMEM, VMEM, VMEM],
+        in_specs=[SMEM, VMEM, HBM],
         out_specs=HBM,
         scratch_shapes=[
+            pltpu.VMEM(down_shape, BF16),
             pltpu.VMEM((leaves, nf, rank), BF16),
             pltpu.VMEM((leaves, nf // 2, 2 * rank), F32),
             pltpu.VMEM((leaves, nf // 2, 2 * rank), F32),
             pltpu.VMEM((mids, nf // 2, 2 * rank), F32),
             pltpu.VMEM((mids, nf // 2, 2 * rank), F32),
-            pltpu.SemaphoreType.DMA((mids,)),
+            pltpu.SemaphoreType.DMA((mids + 1,)),
         ],
         compiler_params=pltpu.CompilerParams(vmem_limit_bytes=40000000),
         name="lower",
-    )(slots, returned, down_leaf, down_mid)
+    )(slots, returned, down_all)
     return jnp.swapaxes(forward, 1, 2), jnp.swapaxes(adjoint, 1, 2)
 
 

time: 79.7 us -> 79.1 us (level)
  waiting for transfers between devices: 19.1 us -> 16 us
  local copies, waits for them, and re-layouts: 4.71 us -> 7.75 us
    all_to_all x1, waiting for transfers between devices: 11.6 us -> 8.51 us  [on_device(): lax.all_to_all(per_slot, ('grp', 'dev'), split_axis=0, concat_axis=0, axi...]
    unnamed x14 -> x22, local copies, waits for them, and re-layouts: 2.59 us -> 4.99 us
    pallas_call x1, Pallas kernels: 4.62 us -> 3.79 us  [on_device(): pl.pallas_call(finish_kernel, out_shape=(shape((leaves, nf, rank), BF16),...]
  transfers between devices with their start and end apart: 5 -> 5, of which waited for: 3 -> 3; matrix products, arithmetic and copies ran while one was open for 4% -> 5% of each run, Pallas kernels for 38% -> 38%
where the time goes in v5:
time: 79.1 us; the launch traced here: 78.6 us
  Pallas kernels  36.3 us (46%)
  starting transfers between devices  16.9 us (21%)
  waiting for transfers between devices  16 us (20%)
  local copies, waits for them, and re-layouts  7.75 us (10%)
  other arithmetic  0.82 us (1%)
    pallas_call x1, Pallas kernels, on_device(): pl.pallas_call(adjoint_kernel, out_shape=(shape(second_message, BF16), sh...  13.5 us
    all_to_all x1, starting transfers between devices, exchange(): lax.all_to_all(x, ('grp', 'dev'), split_axis=0, concat_axis=0, tiled=True)  11.6 us
    pallas_call x1, Pallas kernels, on_device(): pl.pallas_call(forward_kernel, out_shape=(shape((leaves, nf, rank), F32),...  9.17 us
    all_to_all x1, waiting for transfers between devices, on_device(): lax.all_to_all(per_slot, ('grp', 'dev'), split_axis=0, concat_axis=0, axi...  8.51 us
    all_to_all x1, waiting for transfers between devices, exchange(): lax.all_to_all(x, ('grp', 'dev'), split_axis=0, concat_axis=0, tiled=True)  5.42 us
    unnamed x22, local copies, waits for them, and re-layouts  4.99 us
    all_to_all x1, starting transfers between devices, on_device(): lax.all_to_all(per_slot, ('grp', 'dev'), split_axis=0, concat_axis=0, axi...  4.73 us
    pallas_call x1, Pallas kernels, on_device(): pl.pallas_call(lift_kernel, out_shape=shape(message, BF16), in_specs=[HBM...  3.79 us
  transfers between devices with their start and end apart: 5, of which 3 were waited for; matrix products, arithmetic and copies ran while one was open for 5% of the time, Pallas kernels for 38%

profile of v5, /device:TPU:0, one launch (start us, length us, event | category | flops | bytes accessed | tf_op | source)
XLA Modules:
  0.0 78.6 jit_solution(5461046770330257826)
XLA Ops:
  0.6 3.8 %lift.1.outgoing = bf16[128,56,128]{2,1,0:T(8,128)(2,1)} custom-call(s32[3,1,128]{2,1,0:T(1,128)} %bitcast.6, bf16[64,32,64]{2,1,0:T(8,128)(2,1)} %bitcast.10, bf16[64,64,64]{2,1,0:T(8,128)(2,1)} %up_leaf.3, bf16[8,64,64]{2,1,0:T(8,128)(2,1)} %up_mid.3), custom_call_target="tpu_custom_call" | custom-call | tf_op jit(solution)/shard_map/lift/pallas_call | solution.py:459
  4.4 11.6 %all-to-all-start = ((bf16[128,56,128]{2,1,0:T(8,128)(2,1)}), bf16[128,56,128]{2,1,0:T(8,128)(2,1)}, u32[]{:S(2)}, u32[]{:S(2)}) async-start(bf16[128,56,128]{2,1,0:T(8,128)(2,1)} %lift.1.outgoing), calls=%async_computation | async-start | bytes 3670016 | tf_op jit(solution)/shard_map/all_to_all | solution.py:420
  16.1 3.2 %top.1 = (bf16[8,32,64]{2,1,0:T(8,128)(2,1)}, f32[64,16,128]{2,1,0:T(8,128)}, bf16[64,16,128]{2,1,0:T(8,128)(2,1)}) custom-call(s32[1,16]{1,0:T(1,128)} %top_list.3, bf16[64,32,64]{2,1,0:T(8,128)(2,1)} %bitcast.8, bf16[64,64,64]{2,1,0:T(8,128)(2,1)} %up_leaf.3, bf16[8,64,64]{2,1,0:T(8,128)(2,1)} %up_mid.3, bf16[1,16,64,64]{3,2,1,0:T(8,128)(2,1)} %couple_top.3, ...), custom_call_target="tpu_custom_call" | custom-call | flops 1000000 | bytes 100000 | tf_op jit(solution)/shard_map/top/pallas_call | solution.py:479
  19.2 13.5 %adjoint.1 = (bf16[64,112,128]{2,1,0:T(8,128)(2,1)}, bf16[64,48,128]{2,1,0:T(8,128)(2,1)}, bf16[64,8,64,128]{3,2,1,0:T(8,128)(2,1)}, bf16[8,8,64,128]{3,2,1,0:T(8,128)(2,1)}) custom-call(s32[16,64]{1,0:T(8,128)} %bitcast.12, s32[8,16]{1,0:T(8,128)} %mid_list_in.3, bf16[64,32,64]{2,1,0:T(8,128)(2,1)} %bitcast.9, ...), custom_call_target="tpu_custom_call" | custom-call | flops 1000000 | bytes 100000 | tf_op jit(solution)/shard_map/adjoint/pallas_call | solution.py:492
  32.7 0.0 copy-start.9
  32.8 0.1 collective-permute-start.1
  32.8 0.0 copy-done.10
  32.9 0.5 collective-permute-start.2
  33.3 2.1 %collective-permute-done.1 = bf16[64,48,128]{2,1,0:T(8,128)(2,1)S(1)} collective-permute-done((bf16[64,48,128]{2,1,0:T(8,128)(2,1)}, bf16[64,48,128]{2,1,0:T(8,128)(2,1)S(1)}, u32[]{:S(2)}, u32[]{:S(2)}) %collective-permute-start.1) | collective-permute-done | bytes 786464 | tf_op jit(solution)/shard_map/ppermute | solution.py:424
  35.4 1.1 %constant_dynamic-update-slice_fusion = bf16[64,112,128]{2,1,0:T(8,128)(2,1)} fusion(bf16[64,112,128]{2,1,0:T(8,128)(2,1)} %get-tuple-element.19, bf16[64,48,128]{2,1,0:T(8,128)(2,1)S(1)} %collective-permute-done.1), kind=kLoop, calls=%fused_computation.2 | loop fusion | bytes 1572864 | tf_op jit(solution)/shard_map/dynamic_update_slice | solution.py:524
  36.5 0.0 collective-permute-done.2
  36.5 0.0 copy-done.9
  36.5 0.8 %fusion = bf16[64,112,128]{2,1,0:T(8,128)(2,1)} fusion(bf16[64,112,128]{2,1,0:T(8,128)(2,1)} %constant_dynamic-update-slice_fusion, f32[64,16,128]{2,1,0:T(8,128)S(1)} %copy-done.9, bf16[64,16,128]{2,1,0:T(8,128)(2,1)S(1)} %collective-permute-done.2), kind=kLoop, calls=%fused_computation.1 | loop fusion | flops 393216 | bytes 1048576 | tf_op jit(solution)/shard_map/dynamic_update_slice | solution.py:525
  37.3 5.4 %all-to-all-done.arrived_in = bf16[128,56,128]{2,1,0:T(8,128)(2,1)} async-done(((bf16[128,56,128]{2,1,0:T(8,128)(2,1)}), bf16[128,56,128]{2,1,0:T(8,128)(2,1)}, u32[]{:S(2)}, u32[]{:S(2)}) %all-to-all-start) | async-done | bytes 1835040 | tf_op jit(solution)/shard_map/all_to_all | solution.py:420
  42.8 4.7 %all-to-all-start.1 = ((bf16[64,112,128]{2,1,0:T(8,128)(2,1)}), bf16[64,112,128]{2,1,0:T(8,128)(2,1)S(1)}, u32[]{:S(2)}, u32[]{:S(2)}) async-start(bf16[64,112,128]{2,1,0:T(8,128)(2,1)} %fusion), calls=%async_computation.1 | async-start | bytes 3670016 | tf_op jit(solution)/shard_map/all_to_all | solution.py:527
  47.5 1.7 %slice.4.own_half = bf16[128,8,128]{2,1,0:T(8,128)(2,1)} slice(bf16[128,56,128]{2,1,0:T(8,128)(2,1)} %all-to-all-done.arrived_in), slice={[0:128], [48:56], [0:128]} | slice | bytes 524288 | tf_op jit(solution)/shard_map/slice | solution.py:531
  49.2 0.0 collective-permute-start
  49.2 9.2 %forward.1 = (f32[64,32,64]{2,1,0:T(8,128)}, f32[8,32,64]{2,1,0:T(8,128)}) custom-call(s32[16,64]{1,0:T(8,128)} %bitcast.13, s32[8,16]{1,0:T(8,128)} %mid_list_in.3, bf16[128,56,128]{2,1,0:T(8,128)(2,1)} %all-to-all-done.arrived_in, bf16[64,8,64,128]{3,2,1,0:T(8,128)(2,1)} %get-tuple-element.14.leaf_pairs_in, ...), custom_call_target="tpu_custom_call" | custom-call | flops 1000000 | bytes 100000 | tf_op jit(solution)/shard_map/forward/pallas_call | solution.py:533
  58.4 0.0 copy-start.7
  58.4 0.0 collective-permute-done.other_half
  58.4 0.0 copy-done
  58.4 0.0 copy-done.1
  58.4 0.0 copy-done.8
  58.4 0.0 copy-start.2
  58.4 1.2 %copy-done.2 = f32[64,32,64]{2,1,0:T(8,128)S(1)} copy-done((f32[64,32,64]{2,1,0:T(8,128)S(1)}, f32[64,32,64]{2,1,0:T(8,128)}, u32[]{:S(2)}) %copy-start.2) | copy-done | bytes 524312
  59.6 0.9 %copy-done.3 = bf16[1,16,64,64]{3,2,1,0:T(8,128)(2,1)S(1)} copy-done((bf16[1,16,64,64]{3,2,1,0:T(8,128)(2,1)S(1)}, bf16[1,16,64,64]{3,2,1,0:T(8,128)(2,1)}, u32[]{:S(2)}) %copy-start.3) | copy-done | bytes 131096
  60.6 0.9 %copy-done.6 = f32[8,32,64]{2,1,0:T(8,128)S(1)} copy-done((f32[8,32,64]{2,1,0:T(8,128)S(1)}, f32[8,32,64]{2,1,0:T(8,128)}, u32[]{:S(2)}) %copy-start.6) | copy-done | bytes 65560
  61.5 3.8 %finish.1 = (bf16[64,32,64]{2,1,0:T(8,128)(2,1)}, bf16[9,64,512]{2,1,0:T(8,128)(2,1)S(1)}) custom-call(s32[1,16]{1,0:T(1,128)S(1)} %copy-done.8, bf16[128,8,128]{2,1,0:T(8,128)(2,1)} %slice.4.own_half, bf16[128,8,128]{2,1,0:T(8,128)(2,1)} %collective-permute-done.other_half, f32[64,32,64]{2,1,0:T(8,128)S(1)} %copy-done.2, f32[8,32,64]{2,1,0:T(8,128)S(1)} %copy-done.6, ...), custom_call_target="tpu_custom_call" | custom-call | flops 1000000 | bytes 100000 | tf_op jit(solution)/shard_map/finish/pallas_call | solution.py:557
  65.3 0.8 %copy-done.4 = bf16[9,64,512]{2,1,0:T(8,128)(2,1)} copy-done((bf16[9,64,512]{2,1,0:T(8,128)(2,1)}, bf16[9,64,512]{2,1,0:T(8,128)(2,1)S(1)}, u32[]{:S(2)}) %copy-start.4) | copy-done | bytes 589848
  66.1 8.5 %all-to-all-done.1.returned = bf16[64,112,128]{2,1,0:T(8,128)(2,1)S(1)} async-done(((bf16[64,112,128]{2,1,0:T(8,128)(2,1)}), bf16[64,112,128]{2,1,0:T(8,128)(2,1)S(1)}, u32[]{:S(2)}, u32[]{:S(2)}) %all-to-all-start.1) | async-done | bytes 1835040 | tf_op jit(solution)/shard_map/all_to_all | solution.py:527
  74.6 1.1 %copy-done.5 = bf16[9,64,512]{2,1,0:T(8,128)(2,1)S(1)} copy-done((bf16[9,64,512]{2,1,0:T(8,128)(2,1)S(1)}, bf16[9,64,512]{2,1,0:T(8,128)(2,1)}, u32[]{:S(2)}) %copy-start.5) | copy-done | bytes 589848
  75.7 2.9 %lower.1 = bf16[64,32,64]{2,1,0:T(8,128)(2,1)} custom-call(s32[3,1,128]{2,1,0:T(1,128)S(1)} %bitcast.7, bf16[64,112,128]{2,1,0:T(8,128)(2,1)S(1)} %all-to-all-done.1.returned, bf16[9,64,512]{2,1,0:T(8,128)(2,1)S(1)} %copy-done.5), custom_call_target="tpu_custom_call" | custom-call | tf_op jit(solution)/shard_map/lower/pallas_call | solution.py:570
  (9 shorter events, 0.0 us)
Async XLA Ops:
  4.4 38.3 %all-to-all-start = ((bf16[128,56,128]{2,1,0:T(8,128)(2,1)}), bf16[128,56,128]{2,1,0:T(8,128)(2,1)}, u32[]{:S(2)}, u32[]{:S(2)}) async-start(bf16[128,56,128]{2,1,0:T(8,128)(2,1)} %lift.1.outgoing), calls=%async_computation | async-start | bytes 3670016 | tf_op jit(solution)/shard_map/all_to_all | solution.py:420
  19.2 13.6 %copy-start.10 = (bf16[64,16,128]{2,1,0:T(8,128)(2,1)S(1)}, bf16[64,16,128]{2,1,0:T(8,128)(2,1)}, u32[]{:S(2)}) copy-start(bf16[64,16,128]{2,1,0:T(8,128)(2,1)} %get-tuple-element.22) | copy-start | bytes 786436
  32.7 3.8 %copy-start.9 = (f32[64,16,128]{2,1,0:T(8,128)S(1)}, f32[64,16,128]{2,1,0:T(8,128)}, u32[]{:S(2)}) copy-start(f32[64,16,128]{2,1,0:T(8,128)} %get-tuple-element.21) | copy-start | bytes 1572868
  32.8 2.7 %collective-permute-start.1 = (bf16[64,48,128]{2,1,0:T(8,128)(2,1)}, bf16[64,48,128]{2,1,0:T(8,128)(2,1)S(1)}, u32[]{:S(2)}, u32[]{:S(2)}) collective-permute-start(bf16[64,48,128]{2,1,0:T(8,128)(2,1)} %get-tuple-element.20), channel_id=1, source_target_pairs={{0,16},{16,0},{32,48},{48,32},{64,80},{80,64},{96,112},{112,96},{1... | collective-permute-start | bytes 2359304 | tf_op jit(solution)/shard_map/ppermute | solution.py:424
  32.9 3.7 %collective-permute-start.2 = (bf16[64,16,128]{2,1,0:T(8,128)(2,1)S(1)}, bf16[64,16,128]{2,1,0:T(8,128)(2,1)S(1)}, u32[]{:S(2)}, u32[]{:S(2)}) collective-permute-start(bf16[64,16,128]{2,1,0:T(8,128)(2,1)S(1)} %copy-done.10), channel_id=1, source_target_pairs={{0,16},{16,0},{32,48},{48,32},{64,80},{80,64},{96,112},{112,96},{1... | collective-permute-start | bytes 786440 | tf_op jit(solution)/shard_map/ppermute | solution.py:424
  42.8 31.9 %all-to-all-start.1 = ((bf16[64,112,128]{2,1,0:T(8,128)(2,1)}), bf16[64,112,128]{2,1,0:T(8,128)(2,1)S(1)}, u32[]{:S(2)}, u32[]{:S(2)}) async-start(bf16[64,112,128]{2,1,0:T(8,128)(2,1)} %fusion), calls=%async_computation.1 | async-start | bytes 3670016 | tf_op jit(solution)/shard_map/all_to_all | solution.py:527
  49.2 9.2 %collective-permute-start = (bf16[128,8,128]{2,1,0:T(8,128)(2,1)}, bf16[128,8,128]{2,1,0:T(8,128)(2,1)}, u32[]{:S(2)}, u32[]{:S(2)}) collective-permute-start(bf16[128,8,128]{2,1,0:T(8,128)(2,1)} %slice.4.own_half), channel_id=1, source_target_pairs={{0,16},{16,0},{32,48},{48,32},{64,80},{80,64},{96,112},{112,96},{1... | collective-permute-start | bytes 786440 | tf_op jit(solution)/shard_map/ppermute | solution.py:424
  49.2 9.2 %copy-start = (bf16[64,64,64]{2,1,0:T(8,128)(2,1)S(1)}, bf16[64,64,64]{2,1,0:T(8,128)(2,1)}, u32[]{:S(2)}) copy-start(bf16[64,64,64]{2,1,0:T(8,128)(2,1)} %up_leaf.3) | copy-start | bytes 1572868
  49.2 9.2 %copy-start.1 = (bf16[8,64,64]{2,1,0:T(8,128)(2,1)S(1)}, bf16[8,64,64]{2,1,0:T(8,128)(2,1)}, u32[]{:S(2)}) copy-start(bf16[8,64,64]{2,1,0:T(8,128)(2,1)} %up_mid.3) | copy-start | bytes 196612
  49.2 9.2 %copy-start.8 = (s32[1,16]{1,0:T(1,128)S(1)}, s32[1,16]{1,0:T(1,128)}, u32[]{:S(2)}) copy-start(s32[1,16]{1,0:T(1,128)} %top_list.3) | copy-start | bytes 196
  58.4 16.3 %copy-start.7 = (s32[1,128,3]{1,0,2:T(1,128)S(1)}, s32[1,128,3]{1,0,2:T(1,128)}, u32[]{:S(2)}) copy-start(s32[1,128,3]{1,0,2:T(1,128)} %param.18) | copy-start | bytes 4612
  58.4 1.2 %copy-start.2 = (f32[64,32,64]{2,1,0:T(8,128)S(1)}, f32[64,32,64]{2,1,0:T(8,128)}, u32[]{:S(2)}) copy-start(f32[64,32,64]{2,1,0:T(8,128)} %get-tuple-element.16.leaf_near) | copy-start | bytes 1572868
  59.6 0.9 %copy-start.3 = (bf16[1,16,64,64]{3,2,1,0:T(8,128)(2,1)S(1)}, bf16[1,16,64,64]{3,2,1,0:T(8,128)(2,1)}, u32[]{:S(2)}) copy-start(bf16[1,16,64,64]{3,2,1,0:T(8,128)(2,1)} %couple_top.3) | copy-start | bytes 393220
  60.6 0.9 %copy-start.6 = (f32[8,32,64]{2,1,0:T(8,128)S(1)}, f32[8,32,64]{2,1,0:T(8,128)}, u32[]{:S(2)}) copy-start(f32[8,32,64]{2,1,0:T(8,128)} %get-tuple-element.17.mid_near) | copy-start | bytes 196612
  65.3 0.8 %copy-start.4 = (bf16[9,64,512]{2,1,0:T(8,128)(2,1)}, bf16[9,64,512]{2,1,0:T(8,128)(2,1)S(1)}, u32[]{:S(2)}) copy-start(bf16[9,64,512]{2,1,0:T(8,128)(2,1)S(1)} %get-tuple-element.23.down_all_in) | copy-start | bytes 1769476
  74.6 1.1 %copy-start.5 = (bf16[9,64,512]{2,1,0:T(8,128)(2,1)S(1)}, bf16[9,64,512]{2,1,0:T(8,128)(2,1)}, u32[]{:S(2)}) copy-start(bf16[9,64,512]{2,1,0:T(8,128)(2,1)} %copy-done.4) | copy-start | bytes 1769476

commit v6 on v5

--- a/solution.py
+++ b/solution.py
@@ -347,7 +347,7 @@
 
 
 def finish_kernel(
-    top_list, own_half, other_half, leaf_near, mid_near, up_leaf, up_mid, couple_top, forward, down_all
+    top_list, own_half, other_half, leaf_near, mid_near, up_leaf, up_mid, couple_top, forward, down_out, down_all, sem
 ):
     nf, rank = forward.shape[1:]
     shape = (rank, rank)
@@ -369,6 +369,9 @@
         below = lower((mid_near[c] + below_top[c]).astype(BF16), down)
         for i in range(8):
             forward[8 * c + i] = (leaf_near[8 * c + i] + below[i]).astype(BF16)
+    keep = pltpu.make_async_copy(down_all, down_out.at[pl.ds(0, mids + 1)], sem)
+    keep.start()
+    keep.wait()
 
 
 def lower_kernel(
@@ -376,7 +379,7 @@
 ):
     leaves, nf, rank = adjoint.shape
     mids = even_mid.shape[0]
-    fetch = pltpu.make_async_copy(down_all_in, down_all, sems.at[mids])
+    fetch = pltpu.make_async_copy(down_all_in.at[pl.ds(0, mids + 1)], down_all, sems.at[mids])
     fetch.start()
     for far in (even, odd, even_mid, odd_mid):
         far[...] = jnp.zeros(far.shape, F32)
@@ -558,11 +561,12 @@
         finish_kernel,
         out_shape=(
             shape((leaves, nf, rank), BF16),
-            shape(down_shape, BF16),
+            shape((50 * mids,) + down_shape[1:], BF16),
         ),
         in_specs=[SMEM] + [VMEM] * 7,
-        out_specs=(VMEM, VMEM),
-        compiler_params=pltpu.CompilerParams(vmem_limit_bytes=40000000),
+        out_specs=(VMEM, HBM),
+        scratch_shapes=[pltpu.VMEM(down_shape, BF16), pltpu.SemaphoreType.DMA],
+        compiler_params=roomy,
         cost_estimate=small,
         name="finish",
     )(top_list, own_half, other_half, leaf_near, mid_near, up_leaf, up_mid, couple_top)
@@ -581,7 +585,7 @@
             pltpu.VMEM((mids, nf // 2, 2 * rank), F32),
             pltpu.SemaphoreType.DMA((mids + 1,)),
         ],
-        compiler_params=pltpu.CompilerParams(vmem_limit_bytes=40000000),
+        compiler_params=pltpu.CompilerParams(vmem_limit_bytes=42000000),
         name="lower",
     )(slots, returned, down_all)
     return jnp.swapaxes(forward, 1, 2), jnp.swapaxes(adjoint, 1, 2)

time: 79.1 us -> 78 us (0.986)
  local copies, waits for them, and re-layouts: 7.75 us -> 2.78 us
  waiting for transfers between devices: 16 us -> 18.5 us
  Pallas kernels: 36.3 us -> 37.7 us
    unnamed x22 -> x10, local copies, waits for them, and re-layouts: 4.99 us -> 0.72 us
    all_to_all x1, waiting for transfers between devices: 8.51 us -> 11 us  [on_device(): lax.all_to_all(per_slot, ('grp', 'dev'), split_axis=0, concat_axis=0, axi...]
    pallas_call x1, Pallas kernels: 3.79 us -> 5.25 us  [on_device(): pl.pallas_call(finish_kernel, out_shape=(shape((leaves, nf, rank), BF16),...]
  transfers between devices with their start and end apart: 5 -> 5, of which waited for: 3 -> 3; matrix products, arithmetic and copies ran while one was open for 5% -> 4% of each run, Pallas kernels for 38% -> 40%
where the time goes in v6:
time: 78 us; the launch traced here: 77.6 us
  Pallas kernels  37.7 us (48%)
  waiting for transfers between devices  18.5 us (24%)
  starting transfers between devices  17 us (22%)
  local copies, waits for them, and re-layouts  2.78 us (4%)
  other arithmetic  0.8 us (1%)
    pallas_call x1, Pallas kernels, on_device(): pl.pallas_call(adjoint_kernel, out_shape=(shape(second_message, BF16), sh...  13.5 us
    all_to_all x1, starting transfers between devices, exchange(): lax.all_to_all(x, ('grp', 'dev'), split_axis=0, concat_axis=0, tiled=True)  11.6 us
    all_to_all x1, waiting for transfers between devices, on_device(): lax.all_to_all(per_slot, ('grp', 'dev'), split_axis=0, concat_axis=0, axi...  11 us
    pallas_call x1, Pallas kernels, on_device(): pl.pallas_call(forward_kernel, out_shape=(shape((leaves, nf, rank), F32),...  9.07 us
    all_to_all x1, waiting for transfers between devices, exchange(): lax.all_to_all(x, ('grp', 'dev'), split_axis=0, concat_axis=0, tiled=True)  5.42 us
    pallas_call x1, Pallas kernels, on_device(): pl.pallas_call(finish_kernel, out_shape=(shape((leaves, nf, rank), BF16),...  5.25 us
    all_to_all x1, starting transfers between devices, on_device(): lax.all_to_all(per_slot, ('grp', 'dev'), split_axis=0, concat_axis=0, axi...  4.73 us
    pallas_call x1, Pallas kernels, on_device(): pl.pallas_call(lift_kernel, out_shape=shape(message, BF16), in_specs=[HBM...  3.81 us
  transfers between devices with their start and end apart: 5, of which 3 were waited for; matrix products, arithmetic and copies ran while one was open for 4% of the time, Pallas kernels for 40%

profile of v6, /device:TPU:0, one launch (start us, length us, event | category | flops | bytes accessed | tf_op | source)
XLA Modules:
  0.0 77.6 jit_solution(7533535716118663544)
XLA Ops:
  0.6 3.8 %lift.1.outgoing = bf16[128,56,128]{2,1,0:T(8,128)(2,1)} custom-call(s32[3,1,128]{2,1,0:T(1,128)} %bitcast.6, bf16[64,32,64]{2,1,0:T(8,128)(2,1)} %bitcast.11, bf16[64,64,64]{2,1,0:T(8,128)(2,1)} %up_leaf.3, bf16[8,64,64]{2,1,0:T(8,128)(2,1)} %up_mid.3), custom_call_target="tpu_custom_call" | custom-call | tf_op jit(solution)/shard_map/lift/pallas_call | solution.py:462
  4.4 11.6 %all-to-all-start = ((bf16[128,56,128]{2,1,0:T(8,128)(2,1)}), bf16[128,56,128]{2,1,0:T(8,128)(2,1)}, u32[]{:S(2)}, u32[]{:S(2)}) async-start(bf16[128,56,128]{2,1,0:T(8,128)(2,1)} %lift.1.outgoing), calls=%async_computation | async-start | bytes 3670016 | tf_op jit(solution)/shard_map/all_to_all | solution.py:423
  16.1 3.2 %top.1 = (bf16[8,32,64]{2,1,0:T(8,128)(2,1)}, f32[64,16,128]{2,1,0:T(8,128)}, bf16[64,16,128]{2,1,0:T(8,128)(2,1)}) custom-call(s32[1,16]{1,0:T(1,128)} %top_list.3, bf16[64,32,64]{2,1,0:T(8,128)(2,1)} %bitcast.8, bf16[64,64,64]{2,1,0:T(8,128)(2,1)} %up_leaf.3, bf16[8,64,64]{2,1,0:T(8,128)(2,1)} %up_mid.3, bf16[1,16,64,64]{3,2,1,0:T(8,128)(2,1)} %couple_top.3, ...), custom_call_target="tpu_custom_call" | custom-call | flops 1000000 | bytes 100000 | tf_op jit(solution)/shard_map/top/pallas_call | solution.py:482
  19.2 0.0 copy-start.4
  19.2 13.5 %adjoint.1 = (bf16[64,112,128]{2,1,0:T(8,128)(2,1)}, bf16[64,48,128]{2,1,0:T(8,128)(2,1)}, bf16[64,8,64,128]{3,2,1,0:T(8,128)(2,1)}, bf16[8,8,64,128]{3,2,1,0:T(8,128)(2,1)}) custom-call(s32[16,64]{1,0:T(8,128)} %bitcast.12, s32[8,16]{1,0:T(8,128)} %mid_list_in.3, bf16[64,32,64]{2,1,0:T(8,128)(2,1)} %bitcast.9, ...), custom_call_target="tpu_custom_call" | custom-call | flops 1000000 | bytes 100000 | tf_op jit(solution)/shard_map/adjoint/pallas_call | solution.py:495
  32.8 0.0 copy-start.2
  32.8 0.1 collective-permute-start.1
  32.9 0.0 copy-done.4
  32.9 0.5 collective-permute-start.2
  33.4 2.1 %collective-permute-done.1 = bf16[64,48,128]{2,1,0:T(8,128)(2,1)S(1)} collective-permute-done((bf16[64,48,128]{2,1,0:T(8,128)(2,1)}, bf16[64,48,128]{2,1,0:T(8,128)(2,1)S(1)}, u32[]{:S(2)}, u32[]{:S(2)}) %collective-permute-start.1) | collective-permute-done | bytes 786464 | tf_op jit(solution)/shard_map/ppermute | solution.py:427
  35.5 1.1 %constant_dynamic-update-slice_fusion = bf16[64,112,128]{2,1,0:T(8,128)(2,1)} fusion(bf16[64,112,128]{2,1,0:T(8,128)(2,1)} %get-tuple-element.19, bf16[64,48,128]{2,1,0:T(8,128)(2,1)S(1)} %collective-permute-done.1), kind=kLoop, calls=%fused_computation.2 | loop fusion | bytes 1572864 | tf_op jit(solution)/shard_map/dynamic_update_slice | solution.py:527
  36.5 0.0 collective-permute-done.2
  36.6 0.0 copy-done.2
  36.6 0.8 %fusion = bf16[64,112,128]{2,1,0:T(8,128)(2,1)} fusion(bf16[64,112,128]{2,1,0:T(8,128)(2,1)} %constant_dynamic-update-slice_fusion, f32[64,16,128]{2,1,0:T(8,128)S(1)} %copy-done.2, bf16[64,16,128]{2,1,0:T(8,128)(2,1)S(1)} %collective-permute-done.2), kind=kLoop, calls=%fused_computation.1 | loop fusion | flops 393216 | bytes 1048576 | tf_op jit(solution)/shard_map/dynamic_update_slice | solution.py:528
  37.4 5.4 %all-to-all-done.arrived_in = bf16[128,56,128]{2,1,0:T(8,128)(2,1)} async-done(((bf16[128,56,128]{2,1,0:T(8,128)(2,1)}), bf16[128,56,128]{2,1,0:T(8,128)(2,1)}, u32[]{:S(2)}, u32[]{:S(2)}) %all-to-all-start) | async-done | bytes 1835040 | tf_op jit(solution)/shard_map/all_to_all | solution.py:423
  42.8 4.7 %all-to-all-start.1 = ((bf16[64,112,128]{2,1,0:T(8,128)(2,1)}), bf16[64,112,128]{2,1,0:T(8,128)(2,1)S(1)}, u32[]{:S(2)}, u32[]{:S(2)}) async-start(bf16[64,112,128]{2,1,0:T(8,128)(2,1)} %fusion), calls=%async_computation.1 | async-start | bytes 3670016 | tf_op jit(solution)/shard_map/all_to_all | solution.py:530
  47.5 1.0 %slice.4.own_half = bf16[128,8,128]{2,1,0:T(8,128)(2,1)S(1)} slice(bf16[128,56,128]{2,1,0:T(8,128)(2,1)} %all-to-all-done.arrived_in), slice={[0:128], [48:56], [0:128]} | slice | bytes 524288 | tf_op jit(solution)/shard_map/slice | solution.py:534
  48.5 0.0 copy-start.1
  48.5 0.1 collective-permute-start
  48.6 9.1 %forward.1 = (f32[64,32,64]{2,1,0:T(8,128)}, f32[8,32,64]{2,1,0:T(8,128)}) custom-call(s32[16,64]{1,0:T(8,128)} %bitcast.13, s32[8,16]{1,0:T(8,128)} %mid_list_in.3, bf16[128,56,128]{2,1,0:T(8,128)(2,1)} %all-to-all-done.arrived_in, bf16[64,8,64,128]{3,2,1,0:T(8,128)(2,1)} %get-tuple-element.14.leaf_pairs_in, ...), custom_call_target="tpu_custom_call" | custom-call | flops 1000000 | bytes 100000 | tf_op jit(solution)/shard_map/forward/pallas_call | solution.py:536
  57.7 0.0 copy-done.1
  57.7 0.0 copy-start
  57.7 0.0 collective-permute-done.other_half
  57.7 0.0 copy-start.3
  57.7 0.7 copy-done.3
  58.4 5.3 %finish.1 = (bf16[64,32,64]{2,1,0:T(8,128)(2,1)}, bf16[400,64,512]{2,1,0:T(8,128)(2,1)}) custom-call(s32[1,16]{1,0:T(1,128)} %top_list.3, bf16[128,8,128]{2,1,0:T(8,128)(2,1)} %copy-done.1, bf16[128,8,128]{2,1,0:T(8,128)(2,1)} %copy-done.3, f32[64,32,64]{2,1,0:T(8,128)} %get-tuple-element.16.leaf_near, f32[8,32,64]{2,1,0:T(8,128)} %get-tuple-element.17.mid_near, ...), custom_call_target="tpu_custom_call" | custom-call | flops 1000000 | bytes 100000 | tf_op jit(solution)/shard_map/finish/pallas_call | solution.py:560
  63.7 11.0 %all-to-all-done.1.returned = bf16[64,112,128]{2,1,0:T(8,128)(2,1)S(1)} async-done(((bf16[64,112,128]{2,1,0:T(8,128)(2,1)}), bf16[64,112,128]{2,1,0:T(8,128)(2,1)S(1)}, u32[]{:S(2)}, u32[]{:S(2)}) %all-to-all-start.1) | async-done | bytes 1835040 | tf_op jit(solution)/shard_map/all_to_all | solution.py:530
  74.6 0.0 copy-done
  74.6 2.9 %lower.1 = bf16[64,32,64]{2,1,0:T(8,128)(2,1)} custom-call(s32[3,1,128]{2,1,0:T(1,128)S(1)} %bitcast.7, bf16[64,112,128]{2,1,0:T(8,128)(2,1)S(1)} %all-to-all-done.1.returned, bf16[400,64,512]{2,1,0:T(8,128)(2,1)} %get-tuple-element.23.down_all_in), custom_call_target="tpu_custom_call" | custom-call | tf_op jit(solution)/shard_map/lower/pallas_call | solution.py:574
Async XLA Ops:
  4.4 38.3 %all-to-all-start = ((bf16[128,56,128]{2,1,0:T(8,128)(2,1)}), bf16[128,56,128]{2,1,0:T(8,128)(2,1)}, u32[]{:S(2)}, u32[]{:S(2)}) async-start(bf16[128,56,128]{2,1,0:T(8,128)(2,1)} %lift.1.outgoing), calls=%async_computation | async-start | bytes 3670016 | tf_op jit(solution)/shard_map/all_to_all | solution.py:423
  19.2 13.7 %copy-start.4 = (bf16[64,16,128]{2,1,0:T(8,128)(2,1)S(1)}, bf16[64,16,128]{2,1,0:T(8,128)(2,1)}, u32[]{:S(2)}) copy-start(bf16[64,16,128]{2,1,0:T(8,128)(2,1)} %get-tuple-element.22) | copy-start | bytes 786436
  32.8 3.8 %copy-start.2 = (f32[64,16,128]{2,1,0:T(8,128)S(1)}, f32[64,16,128]{2,1,0:T(8,128)}, u32[]{:S(2)}) copy-start(f32[64,16,128]{2,1,0:T(8,128)} %get-tuple-element.21) | copy-start | bytes 1572868
  32.8 2.7 %collective-permute-start.1 = (bf16[64,48,128]{2,1,0:T(8,128)(2,1)}, bf16[64,48,128]{2,1,0:T(8,128)(2,1)S(1)}, u32[]{:S(2)}, u32[]{:S(2)}) collective-permute-start(bf16[64,48,128]{2,1,0:T(8,128)(2,1)} %get-tuple-element.20), channel_id=1, source_target_pairs={{0,16},{16,0},{32,48},{48,32},{64,80},{80,64},{96,112},{112,96},{1... | collective-permute-start | bytes 2359304 | tf_op jit(solution)/shard_map/ppermute | solution.py:427
  32.9 3.7 %collective-permute-start.2 = (bf16[64,16,128]{2,1,0:T(8,128)(2,1)S(1)}, bf16[64,16,128]{2,1,0:T(8,128)(2,1)S(1)}, u32[]{:S(2)}, u32[]{:S(2)}) collective-permute-start(bf16[64,16,128]{2,1,0:T(8,128)(2,1)S(1)} %copy-done.4), channel_id=1, source_target_pairs={{0,16},{16,0},{32,48},{48,32},{64,80},{80,64},{96,112},{112,96},{1... | collective-permute-start | bytes 786440 | tf_op jit(solution)/shard_map/ppermute | solution.py:427
  42.8 31.9 %all-to-all-start.1 = ((bf16[64,112,128]{2,1,0:T(8,128)(2,1)}), bf16[64,112,128]{2,1,0:T(8,128)(2,1)S(1)}, u32[]{:S(2)}, u32[]{:S(2)}) async-start(bf16[64,112,128]{2,1,0:T(8,128)(2,1)} %fusion), calls=%async_computation.1 | async-start | bytes 3670016 | tf_op jit(solution)/shard_map/all_to_all | solution.py:530
  48.5 9.2 %copy-start.1 = (bf16[128,8,128]{2,1,0:T(8,128)(2,1)}, bf16[128,8,128]{2,1,0:T(8,128)(2,1)S(1)}, u32[]{:S(2)}) copy-start(bf16[128,8,128]{2,1,0:T(8,128)(2,1)S(1)} %slice.4.own_half) | copy-start | bytes 786436
  48.5 9.2 %collective-permute-start = (bf16[128,8,128]{2,1,0:T(8,128)(2,1)S(1)}, bf16[128,8,128]{2,1,0:T(8,128)(2,1)S(1)}, u32[]{:S(2)}, u32[]{:S(2)}) collective-permute-start(bf16[128,8,128]{2,1,0:T(8,128)(2,1)S(1)} %slice.4.own_half), channel_id=1, source_target_pairs={{0,16},{16,0},{32,48},{48,32},{64,80},{80,64},{96,112},{112,96},{1... | collective-permute-start | bytes 786440 | tf_op jit(solution)/shard_map/ppermute | solution.py:427
  57.7 17.0 %copy-start = (s32[1,128,3]{1,0,2:T(1,128)S(1)}, s32[1,128,3]{1,0,2:T(1,128)}, u32[]{:S(2)}) copy-start(s32[1,128,3]{1,0,2:T(1,128)} %param.18) | copy-start | bytes 4612
  57.7 0.7 copy-start.3

commit v7 on v6

--- a/solution.py
+++ b/solution.py
@@ -52,12 +52,12 @@
 ):
     leaves, nf, rank = src.shape
     mids = up_mid.shape[0]
-    parts = 4
+    parts = 8
     part = out.shape[0] // parts
-    fetch_src = pltpu.make_async_copy(src_in, src, sems.at[4])
-    fetch_leaf = pltpu.make_async_copy(up_leaf_in, up_leaf, sems.at[5])
-    fetch_mid = pltpu.make_async_copy(up_mid_in, up_mid, sems.at[6])
-    fetch_slots = pltpu.make_async_copy(slots_in, slots, sems.at[7])
+    fetch_src = pltpu.make_async_copy(src_in, src, sems.at[8])
+    fetch_leaf = pltpu.make_async_copy(up_leaf_in, up_leaf, sems.at[9])
+    fetch_mid = pltpu.make_async_copy(up_mid_in, up_mid, sems.at[10])
+    fetch_slots = pltpu.make_async_copy(slots_in, slots, sems.at[11])
     fetch_slots.start()
     fetch_src.start()
     fetch_leaf.start()
@@ -82,14 +82,13 @@
 
     sends = []
     for n in range(parts):
-        for core in range(2):
-
-            def pack_rest(i, carry):
-                p = n * part + core * (part // 2) + i
-                message[p, nf:] = tile[core, slots[2, 0, p] - leaves]
-                return carry
-
-            lax.fori_loop(0, part // 2, pack_rest, 0, unroll=16)
+        core = n & 1
+
+        def pack_rest(p, carry):
+            message[p, nf:] = tile[core, slots[2, 0, p] - leaves]
+            return carry
+
+        lax.fori_loop(n * part, (n + 1) * part, pack_rest, 0, unroll=16)
         place = pl.ds(n * part, part)
         sends.append(pltpu.make_async_copy(message.at[place], out.at[place], sems.at[n]))
         sends[n].start()
@@ -398,7 +397,7 @@
             held[u] = value
         return top + returned[i, 6 * half :].astype(F32)
 
-    top = lax.fori_loop(0, returned.shape[0], collect, jnp.zeros((half, 2 * rank), F32), unroll=8)
+    top = lax.fori_loop(0, returned.shape[0], collect, jnp.zeros((half, 2 * rank), F32), unroll=16)
     fars = [unfold(even_mid[c] + odd_mid[c]) for c in range(mids)]
     fetch.wait()
     below_top = lower(unfold(top).astype(BF16), down_all[mids])
@@ -472,7 +471,7 @@
             pltpu.VMEM(message, BF16),
             pltpu.VMEM((mids, nf, rank), BF16),
             pltpu.VMEM((2, mids, 3 * nf // 4, 2 * rank), BF16),
-            pltpu.SemaphoreType.DMA((8,)),
+            pltpu.SemaphoreType.DMA((12,)),
         ],
         compiler_params=params,
         name="lift",

time: 78 us -> 78 us (level)
  no operation moved by 1% of the time
where the time goes in v7:
time: 78 us; the launch traced here: 77.6 us
  Pallas kernels  37.8 us (48%)
  waiting for transfers between devices  18.5 us (24%)
  starting transfers between devices  17 us (22%)
  local copies, waits for them, and re-layouts  2.78 us (4%)
  other arithmetic  0.8 us (1%)
    pallas_call x1, Pallas kernels, on_device(): pl.pallas_call(adjoint_kernel, out_shape=(shape(second_message, BF16), sh...  13.5 us
    all_to_all x1, starting transfers between devices, exchange(): lax.all_to_all(x, ('grp', 'dev'), split_axis=0, concat_axis=0, tiled=True)  11.6 us
    all_to_all x1, waiting for transfers between devices, on_device(): lax.all_to_all(per_slot, ('grp', 'dev'), split_axis=0, concat_axis=0, axi...  11 us
    pallas_call x1, Pallas kernels, on_device(): pl.pallas_call(forward_kernel, out_shape=(shape((leaves, nf, rank), F32),...  9.07 us
    all_to_all x1, waiting for transfers between devices, exchange(): lax.all_to_all(x, ('grp', 'dev'), split_axis=0, concat_axis=0, tiled=True)  5.42 us
    pallas_call x1, Pallas kernels, on_device(): pl.pallas_call(finish_kernel, out_shape=(shape((leaves, nf, rank), BF16),...  5.25 us
    all_to_all x1, starting transfers between devices, on_device(): lax.all_to_all(per_slot, ('grp', 'dev'), split_axis=0, concat_axis=0, axi...  4.73 us
    pallas_call x1, Pallas kernels, on_device(): pl.pallas_call(lift_kernel, out_shape=shape(message, BF16), in_specs=[HBM...  3.83 us
  transfers between devices with their start and end apart: 5, of which 3 were waited for; matrix products, arithmetic and copies ran while one was open for 4% of the time, Pallas kernels for 40%

profile of v7, /device:TPU:0, one launch (start us, length us, event | category | flops | bytes accessed | tf_op | source)
XLA Modules:
  0.0 77.6 jit_solution(12690285574936889258)
XLA Ops:
  0.6 3.8 %lift.1.outgoing = bf16[128,56,128]{2,1,0:T(8,128)(2,1)} custom-call(s32[3,1,128]{2,1,0:T(1,128)} %bitcast.6, bf16[64,32,64]{2,1,0:T(8,128)(2,1)} %bitcast.11, bf16[64,64,64]{2,1,0:T(8,128)(2,1)} %up_leaf.3, bf16[8,64,64]{2,1,0:T(8,128)(2,1)} %up_mid.3), custom_call_target="tpu_custom_call" | custom-call | tf_op jit(solution)/shard_map/lift/pallas_call | solution.py:461
  4.5 11.6 %all-to-all-start = ((bf16[128,56,128]{2,1,0:T(8,128)(2,1)}), bf16[128,56,128]{2,1,0:T(8,128)(2,1)}, u32[]{:S(2)}, u32[]{:S(2)}) async-start(bf16[128,56,128]{2,1,0:T(8,128)(2,1)} %lift.1.outgoing), calls=%async_computation | async-start | bytes 3670016 | tf_op jit(solution)/shard_map/all_to_all | solution.py:422
  16.1 3.2 %top.1 = (bf16[8,32,64]{2,1,0:T(8,128)(2,1)}, f32[64,16,128]{2,1,0:T(8,128)}, bf16[64,16,128]{2,1,0:T(8,128)(2,1)}) custom-call(s32[1,16]{1,0:T(1,128)} %top_list.3, bf16[64,32,64]{2,1,0:T(8,128)(2,1)} %bitcast.8, bf16[64,64,64]{2,1,0:T(8,128)(2,1)} %up_leaf.3, bf16[8,64,64]{2,1,0:T(8,128)(2,1)} %up_mid.3, bf16[1,16,64,64]{3,2,1,0:T(8,128)(2,1)} %couple_top.3, ...), custom_call_target="tpu_custom_call" | custom-call | flops 1000000 | bytes 100000 | tf_op jit(solution)/shard_map/top/pallas_call | solution.py:481
  19.2 0.0 copy-start.4
  19.2 13.5 %adjoint.1 = (bf16[64,112,128]{2,1,0:T(8,128)(2,1)}, bf16[64,48,128]{2,1,0:T(8,128)(2,1)}, bf16[64,8,64,128]{3,2,1,0:T(8,128)(2,1)}, bf16[8,8,64,128]{3,2,1,0:T(8,128)(2,1)}) custom-call(s32[16,64]{1,0:T(8,128)} %bitcast.12, s32[8,16]{1,0:T(8,128)} %mid_list_in.3, bf16[64,32,64]{2,1,0:T(8,128)(2,1)} %bitcast.9, ...), custom_call_target="tpu_custom_call" | custom-call | flops 1000000 | bytes 100000 | tf_op jit(solution)/shard_map/adjoint/pallas_call | solution.py:494
  32.8 0.0 copy-start.2
  32.8 0.1 collective-permute-start.1
  32.9 0.0 copy-done.4
  32.9 0.5 collective-permute-start.2
  33.4 2.1 %collective-permute-done.1 = bf16[64,48,128]{2,1,0:T(8,128)(2,1)S(1)} collective-permute-done((bf16[64,48,128]{2,1,0:T(8,128)(2,1)}, bf16[64,48,128]{2,1,0:T(8,128)(2,1)S(1)}, u32[]{:S(2)}, u32[]{:S(2)}) %collective-permute-start.1) | collective-permute-done | bytes 786464 | tf_op jit(solution)/shard_map/ppermute | solution.py:426
  35.5 1.1 %constant_dynamic-update-slice_fusion = bf16[64,112,128]{2,1,0:T(8,128)(2,1)} fusion(bf16[64,112,128]{2,1,0:T(8,128)(2,1)} %get-tuple-element.19, bf16[64,48,128]{2,1,0:T(8,128)(2,1)S(1)} %collective-permute-done.1), kind=kLoop, calls=%fused_computation.2 | loop fusion | bytes 1572864 | tf_op jit(solution)/shard_map/dynamic_update_slice | solution.py:526
  36.6 0.0 collective-permute-done.2
  36.6 0.0 copy-done.2
  36.6 0.8 %fusion = bf16[64,112,128]{2,1,0:T(8,128)(2,1)} fusion(bf16[64,112,128]{2,1,0:T(8,128)(2,1)} %constant_dynamic-update-slice_fusion, f32[64,16,128]{2,1,0:T(8,128)S(1)} %copy-done.2, bf16[64,16,128]{2,1,0:T(8,128)(2,1)S(1)} %collective-permute-done.2), kind=kLoop, calls=%fused_computation.1 | loop fusion | flops 393216 | bytes 1048576 | tf_op jit(solution)/shard_map/dynamic_update_slice | solution.py:527
  37.4 5.4 %all-to-all-done.arrived_in = bf16[128,56,128]{2,1,0:T(8,128)(2,1)} async-done(((bf16[128,56,128]{2,1,0:T(8,128)(2,1)}), bf16[128,56,128]{2,1,0:T(8,128)(2,1)}, u32[]{:S(2)}, u32[]{:S(2)}) %all-to-all-start) | async-done | bytes 1835040 | tf_op jit(solution)/shard_map/all_to_all | solution.py:422
  42.8 4.7 %all-to-all-start.1 = ((bf16[64,112,128]{2,1,0:T(8,128)(2,1)}), bf16[64,112,128]{2,1,0:T(8,128)(2,1)S(1)}, u32[]{:S(2)}, u32[]{:S(2)}) async-start(bf16[64,112,128]{2,1,0:T(8,128)(2,1)} %fusion), calls=%async_computation.1 | async-start | bytes 3670016 | tf_op jit(solution)/shard_map/all_to_all | solution.py:529
  47.5 1.0 %slice.4.own_half = bf16[128,8,128]{2,1,0:T(8,128)(2,1)S(1)} slice(bf16[128,56,128]{2,1,0:T(8,128)(2,1)} %all-to-all-done.arrived_in), slice={[0:128], [48:56], [0:128]} | slice | bytes 524288 | tf_op jit(solution)/shard_map/slice | solution.py:533
  48.5 0.0 copy-start.1
  48.5 0.1 collective-permute-start
  48.6 9.1 %forward.1 = (f32[64,32,64]{2,1,0:T(8,128)}, f32[8,32,64]{2,1,0:T(8,128)}) custom-call(s32[16,64]{1,0:T(8,128)} %bitcast.13, s32[8,16]{1,0:T(8,128)} %mid_list_in.3, bf16[128,56,128]{2,1,0:T(8,128)(2,1)} %all-to-all-done.arrived_in, bf16[64,8,64,128]{3,2,1,0:T(8,128)(2,1)} %get-tuple-element.14.leaf_pairs_in, ...), custom_call_target="tpu_custom_call" | custom-call | flops 1000000 | bytes 100000 | tf_op jit(solution)/shard_map/forward/pallas_call | solution.py:535
  57.7 0.0 copy-done.1
  57.7 0.0 copy-start
  57.7 0.0 collective-permute-done.other_half
  57.7 0.0 copy-start.3
  57.7 0.7 copy-done.3
  58.4 5.3 %finish.1 = (bf16[64,32,64]{2,1,0:T(8,128)(2,1)}, bf16[400,64,512]{2,1,0:T(8,128)(2,1)}) custom-call(s32[1,16]{1,0:T(1,128)} %top_list.3, bf16[128,8,128]{2,1,0:T(8,128)(2,1)} %copy-done.1, bf16[128,8,128]{2,1,0:T(8,128)(2,1)} %copy-done.3, f32[64,32,64]{2,1,0:T(8,128)} %get-tuple-element.16.leaf_near, f32[8,32,64]{2,1,0:T(8,128)} %get-tuple-element.17.mid_near, ...), custom_call_target="tpu_custom_call" | custom-call | flops 1000000 | bytes 100000 | tf_op jit(solution)/shard_map/finish/pallas_call | solution.py:559
  63.7 11.0 %all-to-all-done.1.returned = bf16[64,112,128]{2,1,0:T(8,128)(2,1)S(1)} async-done(((bf16[64,112,128]{2,1,0:T(8,128)(2,1)}), bf16[64,112,128]{2,1,0:T(8,128)(2,1)S(1)}, u32[]{:S(2)}, u32[]{:S(2)}) %all-to-all-start.1) | async-done | bytes 1835040 | tf_op jit(solution)/shard_map/all_to_all | solution.py:529
  74.7 0.0 copy-done
  74.7 2.9 %lower.1 = bf16[64,32,64]{2,1,0:T(8,128)(2,1)} custom-call(s32[3,1,128]{2,1,0:T(1,128)S(1)} %bitcast.7, bf16[64,112,128]{2,1,0:T(8,128)(2,1)S(1)} %all-to-all-done.1.returned, bf16[400,64,512]{2,1,0:T(8,128)(2,1)} %get-tuple-element.23.down_all_in), custom_call_target="tpu_custom_call" | custom-call | tf_op jit(solution)/shard_map/lower/pallas_call | solution.py:573
Async XLA Ops:
  4.5 38.3 %all-to-all-start = ((bf16[128,56,128]{2,1,0:T(8,128)(2,1)}), bf16[128,56,128]{2,1,0:T(8,128)(2,1)}, u32[]{:S(2)}, u32[]{:S(2)}) async-start(bf16[128,56,128]{2,1,0:T(8,128)(2,1)} %lift.1.outgoing), calls=%async_computation | async-start | bytes 3670016 | tf_op jit(solution)/shard_map/all_to_all | solution.py:422
  19.2 13.7 %copy-start.4 = (bf16[64,16,128]{2,1,0:T(8,128)(2,1)S(1)}, bf16[64,16,128]{2,1,0:T(8,128)(2,1)}, u32[]{:S(2)}) copy-start(bf16[64,16,128]{2,1,0:T(8,128)(2,1)} %get-tuple-element.22) | copy-start | bytes 786436
  32.8 3.8 %copy-start.2 = (f32[64,16,128]{2,1,0:T(8,128)S(1)}, f32[64,16,128]{2,1,0:T(8,128)}, u32[]{:S(2)}) copy-start(f32[64,16,128]{2,1,0:T(8,128)} %get-tuple-element.21) | copy-start | bytes 1572868
  32.8 2.7 %collective-permute-start.1 = (bf16[64,48,128]{2,1,0:T(8,128)(2,1)}, bf16[64,48,128]{2,1,0:T(8,128)(2,1)S(1)}, u32[]{:S(2)}, u32[]{:S(2)}) collective-permute-start(bf16[64,48,128]{2,1,0:T(8,128)(2,1)} %get-tuple-element.20), channel_id=1, source_target_pairs={{0,16},{16,0},{32,48},{48,32},{64,80},{80,64},{96,112},{112,96},{1... | collective-permute-start | bytes 2359304 | tf_op jit(solution)/shard_map/ppermute | solution.py:426
  32.9 3.7 %collective-permute-start.2 = (bf16[64,16,128]{2,1,0:T(8,128)(2,1)S(1)}, bf16[64,16,128]{2,1,0:T(8,128)(2,1)S(1)}, u32[]{:S(2)}, u32[]{:S(2)}) collective-permute-start(bf16[64,16,128]{2,1,0:T(8,128)(2,1)S(1)} %copy-done.4), channel_id=1, source_target_pairs={{0,16},{16,0},{32,48},{48,32},{64,80},{80,64},{96,112},{112,96},{1... | collective-permute-start | bytes 786440 | tf_op jit(solution)/shard_map/ppermute | solution.py:426
  42.8 31.9 %all-to-all-start.1 = ((bf16[64,112,128]{2,1,0:T(8,128)(2,1)}), bf16[64,112,128]{2,1,0:T(8,128)(2,1)S(1)}, u32[]{:S(2)}, u32[]{:S(2)}) async-start(bf16[64,112,128]{2,1,0:T(8,128)(2,1)} %fusion), calls=%async_computation.1 | async-start | bytes 3670016 | tf_op jit(solution)/shard_map/all_to_all | solution.py:529
  48.5 9.2 %copy-start.1 = (bf16[128,8,128]{2,1,0:T(8,128)(2,1)}, bf16[128,8,128]{2,1,0:T(8,128)(2,1)S(1)}, u32[]{:S(2)}) copy-start(bf16[128,8,128]{2,1,0:T(8,128)(2,1)S(1)} %slice.4.own_half) | copy-start | bytes 786436
  48.5 9.2 %collective-permute-start = (bf16[128,8,128]{2,1,0:T(8,128)(2,1)S(1)}, bf16[128,8,128]{2,1,0:T(8,128)(2,1)S(1)}, u32[]{:S(2)}, u32[]{:S(2)}) collective-permute-start(bf16[128,8,128]{2,1,0:T(8,128)(2,1)S(1)} %slice.4.own_half), channel_id=1, source_target_pairs={{0,16},{16,0},{32,48},{48,32},{64,80},{80,64},{96,112},{112,96},{1... | collective-permute-start | bytes 786440 | tf_op jit(solution)/shard_map/ppermute | solution.py:426
  57.7 17.0 %copy-start = (s32[1,128,3]{1,0,2:T(1,128)S(1)}, s32[1,128,3]{1,0,2:T(1,128)}, u32[]{:S(2)}) copy-start(s32[1,128,3]{1,0,2:T(1,128)} %param.18) | copy-start | bytes 4612
  57.7 0.7 copy-start.3
